TPU v7x, 256 devices: a whole 4x4x8 slice. The times are simulated.
256 devices in a mesh: ctx: 64 (over z, x, core), head: 4 (over y).
Axes of the slice: x: 4, y: 4, z: 8, core: 2. Of those that a mesh axis runs over, the one named last changes fastest.
Arguments:
- query_states: bfloat16 [32768, 2048], P('ctx', 'head'), may hold values from -6 to 6
- key_states: bfloat16 [32768, 256], P('ctx'), may hold values from -6 to 6
- value_states: bfloat16 [32768, 256], P('ctx'), may hold values from -6 to 6
- out_grad: bfloat16 [32768, 2048], P('ctx', 'head'), may hold values from -6 to 6
- lengths: int32 [64], replicated, may hold values from 1 to 2048, as said below
Outputs:
- attended: bfloat16 [32768, 2048], P('ctx', 'head')
- query_grad: bfloat16 [32768, 2048], P('ctx', 'head')
- key_grad: bfloat16 [32768, 256], P('ctx', 'head')
- value_grad: bfloat16 [32768, 256], P('ctx', 'head')
Inputs may be any that keep to these rules, and one draw needn't show every extreme that they name: The lengths sum to 32768; the first document has 256 tokens and the second exactly 2048.
All inputs are finite; a program needn't handle non-finite values.
Results may differ from a plain program's by a relative error of at most 0.028.
Values may be sent and summed in bfloat16 or wider, within the bound.
No kernel may reach another device: no remote copies, remote signals or barrier semaphores. Data moves between devices by JAX's collectives and lax.ppermute only.
A program may use at most 128 MiB of HBM per device.

v0:
```python
import math

import jax
import jax.numpy as jnp
from jax import lax
from jax.experimental import pallas as pl
from jax.experimental.pallas import tpu as pltpu
from jax.sharding import PartitionSpec as P

HEAD_DIM = 128
HEADS = 16
KV_HEADS = 2
WINDOW = 4
TOK_DEV = 512
NDOCS = 64
LOCAL = 4
TILE = 256
SPAN = (WINDOW + 1) * TOK_DEV
N_TILES = SPAN // TILE
LANES = LOCAL * TILE
SCALE = HEAD_DIM ** (-0.5)
SCALE_LOG2 = SCALE * math.log2(math.e)
NEG = -1e30


def contract_last(first_matrix, second_matrix):
    return lax.dot_general(
        first_matrix, second_matrix, (((1,), (1,)), ((), ())), preferred_element_type=jnp.float32
    )


def matmul(first_matrix, second_matrix):
    return jnp.dot(first_matrix, second_matrix, preferred_element_type=jnp.float32)


def attention_kernel(
    lengths_ref, block_ref, q_ref, grad_ref, kv0, kv1, kv2, kv3, kv4,
    out_ref, dq_ref, t0, t1, t2, t3, t4,
    kv_buf, scores, kv_acc, q_cat, g_cat, o_acc, dq_acc, sems,
):
    copies = []
    for distance, kv in enumerate((kv0, kv1, kv2, kv3, kv4)):
        row = (WINDOW - distance) * TOK_DEV
        copy = pltpu.make_async_copy(kv, kv_buf.at[pl.ds(row, TOK_DEV)], sems.at[distance])
        copy.start()
        copies.append(copy)
    kv_acc[...] = jnp.zeros_like(kv_acc)
    first_query = block_ref[0] * TOK_DEV
    origin = first_query - WINDOW * TOK_DEV
    lane_pos = first_query + lax.broadcasted_iota(jnp.int32, (1, TOK_DEV), 1)

    def next_doc(doc, carry):
        end, lane_start, edges = carry
        end = end + lengths_ref[doc]
        lane_start = jnp.where(lane_pos >= end, end, lane_start)
        edges = tuple(
            jnp.where(first_query + place >= end, end, edge)
            for place, edge in zip((0, TILE - 1, TILE, TOK_DEV - 1), edges)
        )
        return end, lane_start, edges

    zero = jnp.int32(0)
    _, lane_start, edges = lax.fori_loop(
        0, NDOCS, next_doc, (zero, jnp.zeros((1, TOK_DEV), jnp.int32), (zero,) * 4), unroll=8
    )
    for copy in copies:
        copy.wait()

    for half in range(TOK_DEV // TILE):
        rows = slice(half * TILE, (half + 1) * TILE)
        for head in range(LOCAL):
            cols = slice(head * HEAD_DIM, (head + 1) * HEAD_DIM)
            place = slice(head * TILE, (head + 1) * TILE)
            q_cat[place, :] = q_ref[rows, cols]
            g_cat[place, :] = grad_ref[rows, cols]
        diagonal = WINDOW * TOK_DEV // TILE + half
        start_rel = jnp.concatenate([lane_start[:, rows] - origin] * LOCAL, axis=1)
        query_rel = jnp.concatenate([lane_pos[:, rows] - origin] * LOCAL, axis=1)
        lowest = lax.div(edges[2 * half] - origin, TILE)
        first_full = jnp.minimum(
            lax.div(edges[2 * half + 1] - origin + TILE - 1, TILE), diagonal
        )
        o_acc[...] = jnp.zeros_like(o_acc)

        def forward_tile(masked, tile, carry):
            row_max, total = carry
            kv_rows = pl.ds(pl.multiple_of(tile * TILE, TILE), TILE)
            keys = kv_buf[kv_rows, :HEAD_DIM]
            values = kv_buf[kv_rows, HEAD_DIM:]
            raw = contract_last(keys, q_cat[...])
            if masked:
                key_rel = tile * TILE + lax.broadcasted_iota(jnp.int32, (TILE, LANES), 0)
                raw = jnp.where((key_rel >= start_rel) & (key_rel <= query_rel), raw, NEG)
            scores[tile] = raw
            new_max = jnp.maximum(row_max, jnp.max(raw, axis=0, keepdims=True))
            weights = jnp.exp2((raw - new_max) * SCALE_LOG2)
            fade = jnp.exp2((row_max - new_max) * SCALE_LOG2)
            total = total * fade + jnp.sum(weights, axis=0, keepdims=True)
            o_acc[...] = o_acc[...] * fade + matmul(values.T, weights.astype(jnp.bfloat16))
            return new_max, total

        def forward_masked(tile, carry):
            return forward_tile(True, tile, carry)

        def forward_full(tile, carry):
            return forward_tile(False, tile, carry)

        carry = (jnp.full((1, LANES), NEG, jnp.float32), jnp.zeros((1, LANES), jnp.float32))
        carry = forward_masked(diagonal, carry)
        carry = lax.fori_loop(first_full, diagonal, forward_full, carry)
        carry = lax.fori_loop(lowest, first_full, forward_masked, carry)
        row_max, total = carry
        attended = (o_acc[...] * (1.0 / total)).astype(jnp.bfloat16).astype(jnp.float32)
        grad_dots = []
        for head in range(LOCAL):
            cols = slice(head * HEAD_DIM, (head + 1) * HEAD_DIM)
            place = slice(head * TILE, (head + 1) * TILE)
            att_head = attended[:, place].T
            out_ref[rows, cols] = att_head.astype(jnp.bfloat16)
            grad_t = grad_ref[rows, cols].astype(jnp.float32).T
            grad_dots.append(jnp.sum(grad_t * attended[:, place], axis=0, keepdims=True))
        grad_dot = jnp.concatenate(grad_dots, axis=1)
        log_total = row_max * SCALE_LOG2 + jnp.log2(total)
        dq_acc[...] = jnp.zeros_like(dq_acc)

        def backward_tile(tile, carry):
            kv_rows = pl.ds(pl.multiple_of(tile * TILE, TILE), TILE)
            keys = kv_buf[kv_rows, :HEAD_DIM]
            values = kv_buf[kv_rows, HEAD_DIM:]
            weights = jnp.exp2(scores[tile] * SCALE_LOG2 - log_total)
            prob_grad = contract_last(values, g_cat[...])
            score_grad = (weights * (prob_grad - grad_dot)).astype(jnp.bfloat16)
            prob = weights.astype(jnp.bfloat16)
            kv_acc[kv_rows, HEAD_DIM:] += matmul(prob, g_cat[...])
            kv_acc[kv_rows, :HEAD_DIM] += matmul(score_grad, q_cat[...])
            dq_acc[...] += matmul(keys.T, score_grad)
            return carry

        lax.fori_loop(lowest, diagonal + 1, backward_tile, 0)
        for head in range(LOCAL):
            cols = slice(head * HEAD_DIM, (head + 1) * HEAD_DIM)
            place = slice(head * TILE, (head + 1) * TILE)
            dq_ref[rows, cols] = (dq_acc[:, place].T * SCALE).astype(jnp.bfloat16)
    for distance, term in enumerate((t0, t1, t2, t3, t4)):
        row = (WINDOW - distance) * TOK_DEV
        term[:, :HEAD_DIM] = (kv_acc[row : row + TOK_DEV, :HEAD_DIM] * SCALE).astype(term.dtype)
        term[:, HEAD_DIM:] = kv_acc[row : row + TOK_DEV, HEAD_DIM:].astype(term.dtype)


def attention_block(lengths, block, queries, grads, kv_blocks):
    vmem = pl.BlockSpec(memory_space=pltpu.VMEM)
    smem = pl.BlockSpec(memory_space=pltpu.SMEM)
    anywhere = pl.BlockSpec(memory_space=pl.ANY)
    wide = jax.ShapeDtypeStruct((TOK_DEV, LOCAL * HEAD_DIM), jnp.bfloat16)
    term = jax.ShapeDtypeStruct((TOK_DEV, 2 * HEAD_DIM), jnp.bfloat16)
    own = jax.ShapeDtypeStruct((TOK_DEV, 2 * HEAD_DIM), jnp.float32)
    return pl.pallas_call(
        attention_kernel,
        out_shape=[wide, wide, own, term, term, term, term],
        in_specs=[smem, smem, vmem, vmem] + [anywhere] * 5,
        out_specs=[vmem] * 7,
        scratch_shapes=[
            pltpu.VMEM((SPAN, 2 * HEAD_DIM), jnp.bfloat16),
            pltpu.VMEM((N_TILES, TILE, LANES), jnp.float32),
            pltpu.VMEM((SPAN, 2 * HEAD_DIM), jnp.float32),
            pltpu.VMEM((LANES, HEAD_DIM), jnp.bfloat16),
            pltpu.VMEM((LANES, HEAD_DIM), jnp.bfloat16),
            pltpu.VMEM((HEAD_DIM, LANES), jnp.float32),
            pltpu.VMEM((HEAD_DIM, LANES), jnp.float32),
            pltpu.SemaphoreType.DMA((WINDOW + 1,)),
        ],
        compiler_params=pltpu.CompilerParams(vmem_limit_bytes=40 * 1024 * 1024),
        cost_estimate=pl.CostEstimate(
            flops=5 * 10**9, bytes_accessed=4 * 10**6, transcendentals=6 * 10**6
        ),
        name="attention",
    )(lengths, block, queries, grads, *kv_blocks)


def passed_along(value, axis, steps):
    count = lax.axis_size(axis)
    initial, last = (max(0, -steps), min(count, count - steps))
    return lax.ppermute(value, axis, [(source, source + steps) for source in range(initial, last)])


def from_partner(value, axis, apart):
    mask = 2**apart
    pairs = [(source, source ^ mask) for source in range(lax.axis_size(axis))]
    return lax.ppermute(value, axis, pairs)


def column_half(matrix, which, half_width):
    return lax.dynamic_slice_in_dim(matrix, which * half_width, half_width, 1)


def shards(query_states, key_states, value_states, out_grad, lengths):
    half_width = HEAD_DIM // 2
    block_index = lax.axis_index("ctx")
    head_index = lax.axis_index("head")
    kv_start = head_index * LOCAL // (HEADS // KV_HEADS) * HEAD_DIM
    own_half = head_index % 2
    other_half = 1 - own_half
    own_keys = lax.dynamic_slice_in_dim(key_states, kv_start, HEAD_DIM, 1)
    own_values = lax.dynamic_slice_in_dim(value_states, kv_start, HEAD_DIM, 1)
    own_pair = jnp.concatenate([own_keys, own_values], axis=1)
    blocks = [own_pair]
    for distance in range(1, WINDOW + 1):
        blocks.append(passed_along(own_pair, "ctx", distance))
    attended, query_grad, *terms = attention_block(
        lengths, block_index.astype(jnp.int32).reshape(1), query_states, out_grad, blocks
    )
    gathered = terms[0]
    for distance in range(1, WINDOW + 1):
        gathered = gathered + passed_along(terms[distance], "ctx", -distance).astype(jnp.float32)
    key_sum = gathered[:, :HEAD_DIM]
    value_sum = gathered[:, HEAD_DIM:]
    outgoing = jnp.concatenate(
        [
            column_half(key_sum, other_half, half_width),
            column_half(value_sum, other_half, half_width),
        ],
        axis=1,
    )
    received = from_partner(outgoing.astype(jnp.bfloat16), "head", 0).astype(jnp.float32)
    key_part = column_half(key_sum, own_half, half_width) + received[:, :half_width]
    value_part = column_half(value_sum, own_half, half_width) + received[:, half_width:]
    return attended, query_grad, key_part.astype(jnp.bfloat16), value_part.astype(jnp.bfloat16)


def solution(mesh):
    return jax.shard_map(
        shards,
        mesh=mesh,
        in_specs=(P("ctx", "head"), P("ctx", None), P("ctx", None), P("ctx", "head"), P()),
        out_specs=(P("ctx", "head"), P("ctx", "head"), P("ctx", "head"), P("ctx", "head")),
        check_vma=False,
    )
```

profile of v0, /device:TPU:28, one launch (start us, length us, event | category | flops | bytes accessed | tf_op | source)
XLA Modules:
  0.0 82.3 jit_solution(16417939160986943070)
XLA Ops:
  0.7 0.0 copy-start
  0.7 0.0 copy-start.1
  0.7 1.1 %constant_dynamic-slice_fusion = (bf16[512,128]{1,0:T(8,128)(2,1)S(1)}, bf16[512,128]{1,0:T(8,128)(2,1)S(1)}) fusion(bf16[512,256]{1,0:T(8,128)(2,1)} %param.7, s32[]{:T(128)S(6)} %select_n.24, bf16[512,256]{1,0:T(8,128)(2,1)} %param.6), kind=kLoop, calls=%fused_computation.9 | loop fusion | bytes 524292 | tf_op jit(solution)/shard_map/dynamic_slice | solution.py:204
  1.8 1.9 %collective-permute-start = (bf16[512,256]{1,0:T(8,128)(2,1)S(1)}, bf16[512,256]{1,0:T(8,128)(2,1)S(1)}, u32[]{:S(2)}, u32[]{:S(2)}) collective-permute-start(bf16[512,256]{1,0:T(8,128)(2,1)S(1)} %pad_maximum_fusion.kv0), channel_id=1, source_target_pairs={{0,4},{4,8},{8,12},{12,16},{16,20},{20,24},{24,28},{28,32},{32,36}... | collective-permute-start | bytes 786440 | tf_op jit(solution)/shard_map/ppermute | solution.py:183
  3.7 3.1 %collective-permute-start.1 = (bf16[512,256]{1,0:T(8,128)(2,1)S(1)}, bf16[512,256]{1,0:T(8,128)(2,1)S(1)}, u32[]{:S(2)}, u32[]{:S(2)}) collective-permute-start(bf16[512,256]{1,0:T(8,128)(2,1)S(1)} %pad_maximum_fusion.kv0), channel_id=1, source_target_pairs={{0,8},{4,12},{8,16},{12,20},{16,24},{20,28},{24,32},{28,36},{32,40... | collective-permute-start | bytes 786440 | tf_op jit(solution)/shard_map/ppermute | solution.py:183
  6.8 4.7 %collective-permute-start.2 = (bf16[512,256]{1,0:T(8,128)(2,1)S(1)}, bf16[512,256]{1,0:T(8,128)(2,1)S(1)}, u32[]{:S(2)}, u32[]{:S(2)}) collective-permute-start(bf16[512,256]{1,0:T(8,128)(2,1)S(1)} %pad_maximum_fusion.kv0), channel_id=1, source_target_pairs={{0,12},{4,16},{8,20},{12,24},{16,28},{20,32},{24,36},{28,40},{32,4... | collective-permute-start | bytes 786440 | tf_op jit(solution)/shard_map/ppermute | solution.py:183
  11.5 3.4 %collective-permute-start.3 = (bf16[512,256]{1,0:T(8,128)(2,1)S(1)}, bf16[512,256]{1,0:T(8,128)(2,1)S(1)}, u32[]{:S(2)}, u32[]{:S(2)}) collective-permute-start(bf16[512,256]{1,0:T(8,128)(2,1)S(1)} %pad_maximum_fusion.kv0), channel_id=1, source_target_pairs={{0,16},{4,20},{8,24},{12,28},{16,32},{20,36},{24,40},{28,44},{32,4... | collective-permute-start | bytes 786440 | tf_op jit(solution)/shard_map/ppermute | solution.py:183
  14.9 0.0 copy-start.6
  15.0 0.0 collective-permute-done.kv1
  15.0 0.0 collective-permute-done.1.kv2
  15.0 6.1 %collective-permute-done.2.kv3 = bf16[512,256]{1,0:T(8,128)(2,1)S(1)} collective-permute-done((bf16[512,256]{1,0:T(8,128)(2,1)S(1)}, bf16[512,256]{1,0:T(8,128)(2,1)S(1)}, u32[]{:S(2)}, u32[]{:S(2)}) %collective-permute-start.2) | collective-permute-done | bytes 262176 | tf_op jit(solution)/shard_map/ppermute | solution.py:183
  21.0 0.0 copy-start.2
  21.0 0.7 copy-done.2
  21.7 4.3 %collective-permute-done.3.kv4 = bf16[512,256]{1,0:T(8,128)(2,1)S(1)} collective-permute-done((bf16[512,256]{1,0:T(8,128)(2,1)S(1)}, bf16[512,256]{1,0:T(8,128)(2,1)S(1)}, u32[]{:S(2)}, u32[]{:S(2)}) %collective-permute-start.3) | collective-permute-done | bytes 262176 | tf_op jit(solution)/shard_map/ppermute | solution.py:183
  26.0 0.0 copy-start.4
  26.0 0.7 copy-done.4
  26.7 0.0 copy-done
  26.7 0.0 copy-done.1
  26.7 0.0 copy-done.6
  26.7 0.0 copy-start.3
  26.7 0.9 %copy-done.3 = bf16[512,256]{1,0:T(8,128)(2,1)S(1)} copy-done((bf16[512,256]{1,0:T(8,128)(2,1)S(1)}, bf16[512,256]{1,0:T(8,128)(2,1)}, u32[]{:S(2)}) %copy-start.3) | copy-done | bytes 262168
  27.7 0.0 copy-start.5
  27.7 0.9 %copy-done.5 = bf16[512,256]{1,0:T(8,128)(2,1)S(1)} copy-done((bf16[512,256]{1,0:T(8,128)(2,1)S(1)}, bf16[512,256]{1,0:T(8,128)(2,1)}, u32[]{:S(2)}) %copy-start.5) | copy-done | bytes 262168
  28.6 14.9 %attention.1 = (bf16[512,512]{1,0:T(8,128)(2,1)}, bf16[512,512]{1,0:T(8,128)(2,1)}, f32[512,256]{1,0:T(8,128)S(1)}, bf16[512,256]{1,0:T(8,128)(2,1)S(1)}, bf16[5...) custom-call(s32[64]{0:T(128)S(1)} %copy-done.6, s32[1]{0:T(128)} %bitcast.block_ref, ...), custom_call_target="tpu_custom_call" | custom-call | flops 5000000000 | bytes 4000000 | tf_op jit(solution)/shard_map/attention/pallas_call | solution.py:157
  43.5 2.3 %collective-permute-start.4 = (bf16[512,256]{1,0:T(8,128)(2,1)S(1)}, bf16[512,256]{1,0:T(8,128)(2,1)S(1)}, u32[]{:S(2)}, u32[]{:S(2)}) collective-permute-start(bf16[512,256]{1,0:T(8,128)(2,1)S(1)} %get-tuple-element.14), channel_id=1, source_target_pairs={{4,0},{8,4},{12,8},{16,12},{20,16},{24,20},{28,24},{32,28},{36,32}... | collective-permute-start | bytes 786440 | tf_op jit(solution)/shard_map/ppermute | solution.py:183
  45.9 1.9 %collective-permute-start.5 = (bf16[512,256]{1,0:T(8,128)(2,1)S(1)}, bf16[512,256]{1,0:T(8,128)(2,1)S(1)}, u32[]{:S(2)}, u32[]{:S(2)}) collective-permute-start(bf16[512,256]{1,0:T(8,128)(2,1)S(1)} %get-tuple-element.15), channel_id=1, source_target_pairs={{8,0},{12,4},{16,8},{20,12},{24,16},{28,20},{32,24},{36,28},{40,32... | collective-permute-start | bytes 786440 | tf_op jit(solution)/shard_map/ppermute | solution.py:183
  47.8 1.9 %collective-permute-start.6 = (bf16[512,256]{1,0:T(8,128)(2,1)S(1)}, bf16[512,256]{1,0:T(8,128)(2,1)S(1)}, u32[]{:S(2)}, u32[]{:S(2)}) collective-permute-start(bf16[512,256]{1,0:T(8,128)(2,1)S(1)} %get-tuple-element.16), channel_id=1, source_target_pairs={{12,0},{16,4},{20,8},{24,12},{28,16},{32,20},{36,24},{40,28},{44,3... | collective-permute-start | bytes 786440 | tf_op jit(solution)/shard_map/ppermute | solution.py:183
  49.7 1.9 %collective-permute-start.7 = (bf16[512,256]{1,0:T(8,128)(2,1)S(1)}, bf16[512,256]{1,0:T(8,128)(2,1)S(1)}, u32[]{:S(2)}, u32[]{:S(2)}) collective-permute-start(bf16[512,256]{1,0:T(8,128)(2,1)S(1)} %get-tuple-element.17), channel_id=1, source_target_pairs={{16,0},{20,4},{24,8},{28,12},{32,16},{36,20},{40,24},{44,28},{48,3... | collective-permute-start | bytes 786440 | tf_op jit(solution)/shard_map/ppermute | solution.py:183
  51.7 0.0 collective-permute-done.4
  51.7 5.4 %collective-permute-done.5 = bf16[512,256]{1,0:T(8,128)(2,1)S(1)} collective-permute-done((bf16[512,256]{1,0:T(8,128)(2,1)S(1)}, bf16[512,256]{1,0:T(8,128)(2,1)S(1)}, u32[]{:S(2)}, u32[]{:S(2)}) %collective-permute-start.5) | collective-permute-done | bytes 262176 | tf_op jit(solution)/shard_map/ppermute | solution.py:183
  57.1 3.7 %collective-permute-done.6 = bf16[512,256]{1,0:T(8,128)(2,1)S(1)} collective-permute-done((bf16[512,256]{1,0:T(8,128)(2,1)S(1)}, bf16[512,256]{1,0:T(8,128)(2,1)S(1)}, u32[]{:S(2)}, u32[]{:S(2)}) %collective-permute-start.6) | collective-permute-done | bytes 262176 | tf_op jit(solution)/shard_map/ppermute | solution.py:183
  60.8 14.1 %collective-permute-done.7 = bf16[512,256]{1,0:T(8,128)(2,1)S(1)} collective-permute-done((bf16[512,256]{1,0:T(8,128)(2,1)S(1)}, bf16[512,256]{1,0:T(8,128)(2,1)S(1)}, u32[]{:S(2)}, u32[]{:S(2)}) %collective-permute-start.7) | collective-permute-done | bytes 262176 | tf_op jit(solution)/shard_map/ppermute | solution.py:183
  75.0 0.1 convert_add_fusion
  75.2 0.1 dynamic-slice_convert_fusion.1
  75.3 0.1 dynamic-slice_convert_fusion
  75.4 0.1 pad_maximum_fusion.1
  75.5 0.8 %collective-permute-start.8 = (bf16[512,128]{1,0:T(8,128)(2,1)S(1)}, bf16[512,128]{1,0:T(8,128)(2,1)S(1)}, u32[]{:S(2)}, u32[]{:S(2)}) collective-permute-start(bf16[512,128]{1,0:T(8,128)(2,1)S(1)} %pad_maximum_fusion.1), channel_id=1, source_target_pairs={{0,1},{1,0},{2,3},{3,2},{4,5},{5,4},{6,7},{7,6},{8,9},{9,8},{10,11... | collective-permute-start | bytes 393224 | tf_op jit(solution)/shard_map/ppermute | solution.py:189
  76.3 4.2 %collective-permute-done.8 = bf16[512,128]{1,0:T(8,128)(2,1)S(1)} collective-permute-done((bf16[512,128]{1,0:T(8,128)(2,1)S(1)}, bf16[512,128]{1,0:T(8,128)(2,1)S(1)}, u32[]{:S(2)}, u32[]{:S(2)}) %collective-permute-start.8) | collective-permute-done | bytes 131104 | tf_op jit(solution)/shard_map/ppermute | solution.py:189
  80.6 0.3 fusion
  80.9 0.7 copy.10
  81.6 0.7 copy.9
  (3 shorter events, 0.1 us)
Async XLA Ops:
  0.7 26.1 %copy-start = (bf16[512,512]{1,0:T(8,128)(2,1)S(1)}, bf16[512,512]{1,0:T(8,128)(2,1)}, u32[]{:S(2)}) copy-start(bf16[512,512]{1,0:T(8,128)(2,1)} %q_ref.1) | copy-start | bytes 1572868
  0.7 26.1 %copy-start.1 = (bf16[512,512]{1,0:T(8,128)(2,1)S(1)}, bf16[512,512]{1,0:T(8,128)(2,1)}, u32[]{:S(2)}) copy-start(bf16[512,512]{1,0:T(8,128)(2,1)} %grad_ref.1) | copy-start | bytes 1572868
  1.8 13.2 %collective-permute-start = (bf16[512,256]{1,0:T(8,128)(2,1)S(1)}, bf16[512,256]{1,0:T(8,128)(2,1)S(1)}, u32[]{:S(2)}, u32[]{:S(2)}) collective-permute-start(bf16[512,256]{1,0:T(8,128)(2,1)S(1)} %pad_maximum_fusion.kv0), channel_id=1, source_target_pairs={{0,4},{4,8},{8,12},{12,16},{16,20},{20,24},{24,28},{28,32},{32,36}... | collective-permute-start | bytes 786440 | tf_op jit(solution)/shard_map/ppermute | solution.py:183
  3.7 11.2 %collective-permute-start.1 = (bf16[512,256]{1,0:T(8,128)(2,1)S(1)}, bf16[512,256]{1,0:T(8,128)(2,1)S(1)}, u32[]{:S(2)}, u32[]{:S(2)}) collective-permute-start(bf16[512,256]{1,0:T(8,128)(2,1)S(1)} %pad_maximum_fusion.kv0), channel_id=1, source_target_pairs={{0,8},{4,12},{8,16},{12,20},{16,24},{20,28},{24,32},{28,36},{32,40... | collective-permute-start | bytes 786440 | tf_op jit(solution)/shard_map/ppermute | solution.py:183
  6.8 14.2 %collective-permute-start.2 = (bf16[512,256]{1,0:T(8,128)(2,1)S(1)}, bf16[512,256]{1,0:T(8,128)(2,1)S(1)}, u32[]{:S(2)}, u32[]{:S(2)}) collective-permute-start(bf16[512,256]{1,0:T(8,128)(2,1)S(1)} %pad_maximum_fusion.kv0), channel_id=1, source_target_pairs={{0,12},{4,16},{8,20},{12,24},{16,28},{20,32},{24,36},{28,40},{32,4... | collective-permute-start | bytes 786440 | tf_op jit(solution)/shard_map/ppermute | solution.py:183
  11.5 14.5 %collective-permute-start.3 = (bf16[512,256]{1,0:T(8,128)(2,1)S(1)}, bf16[512,256]{1,0:T(8,128)(2,1)S(1)}, u32[]{:S(2)}, u32[]{:S(2)}) collective-permute-start(bf16[512,256]{1,0:T(8,128)(2,1)S(1)} %pad_maximum_fusion.kv0), channel_id=1, source_target_pairs={{0,16},{4,20},{8,24},{12,28},{16,32},{20,36},{24,40},{28,44},{32,4... | collective-permute-start | bytes 786440 | tf_op jit(solution)/shard_map/ppermute | solution.py:183
  14.9 11.8 %copy-start.6 = (s32[64]{0:T(128)S(1)}, s32[64]{0:T(128)}, u32[]{:S(2)}) copy-start(s32[64]{0:T(128)} %lengths_ref.1) | copy-start | bytes 772
  21.0 0.7 copy-start.2
  26.0 0.7 copy-start.4
  26.7 1.0 %copy-start.3 = (bf16[512,256]{1,0:T(8,128)(2,1)S(1)}, bf16[512,256]{1,0:T(8,128)(2,1)}, u32[]{:S(2)}) copy-start(bf16[512,256]{1,0:T(8,128)(2,1)} %copy-done.2) | copy-start | bytes 786436
  27.7 0.9 %copy-start.5 = (bf16[512,256]{1,0:T(8,128)(2,1)S(1)}, bf16[512,256]{1,0:T(8,128)(2,1)}, u32[]{:S(2)}) copy-start(bf16[512,256]{1,0:T(8,128)(2,1)} %copy-done.4) | copy-start | bytes 786436
  43.5 8.1 %collective-permute-start.4 = (bf16[512,256]{1,0:T(8,128)(2,1)S(1)}, bf16[512,256]{1,0:T(8,128)(2,1)S(1)}, u32[]{:S(2)}, u32[]{:S(2)}) collective-permute-start(bf16[512,256]{1,0:T(8,128)(2,1)S(1)} %get-tuple-element.14), channel_id=1, source_target_pairs={{4,0},{8,4},{12,8},{16,12},{20,16},{24,20},{28,24},{32,28},{36,32}... | collective-permute-start | bytes 786440 | tf_op jit(solution)/shard_map/ppermute | solution.py:183
  45.9 11.2 %collective-permute-start.5 = (bf16[512,256]{1,0:T(8,128)(2,1)S(1)}, bf16[512,256]{1,0:T(8,128)(2,1)S(1)}, u32[]{:S(2)}, u32[]{:S(2)}) collective-permute-start(bf16[512,256]{1,0:T(8,128)(2,1)S(1)} %get-tuple-element.15), channel_id=1, source_target_pairs={{8,0},{12,4},{16,8},{20,12},{24,16},{28,20},{32,24},{36,28},{40,32... | collective-permute-start | bytes 786440 | tf_op jit(solution)/shard_map/ppermute | solution.py:183
  47.8 13.0 %collective-permute-start.6 = (bf16[512,256]{1,0:T(8,128)(2,1)S(1)}, bf16[512,256]{1,0:T(8,128)(2,1)S(1)}, u32[]{:S(2)}, u32[]{:S(2)}) collective-permute-start(bf16[512,256]{1,0:T(8,128)(2,1)S(1)} %get-tuple-element.16), channel_id=1, source_target_pairs={{12,0},{16,4},{20,8},{24,12},{28,16},{32,20},{36,24},{40,28},{44,3... | collective-permute-start | bytes 786440 | tf_op jit(solution)/shard_map/ppermute | solution.py:183
  49.7 25.3 %collective-permute-start.7 = (bf16[512,256]{1,0:T(8,128)(2,1)S(1)}, bf16[512,256]{1,0:T(8,128)(2,1)S(1)}, u32[]{:S(2)}, u32[]{:S(2)}) collective-permute-start(bf16[512,256]{1,0:T(8,128)(2,1)S(1)} %get-tuple-element.17), channel_id=1, source_target_pairs={{16,0},{20,4},{24,8},{28,12},{32,16},{36,20},{40,24},{44,28},{48,3... | collective-permute-start | bytes 786440 | tf_op jit(solution)/shard_map/ppermute | solution.py:183
  75.5 5.1 %collective-permute-start.8 = (bf16[512,128]{1,0:T(8,128)(2,1)S(1)}, bf16[512,128]{1,0:T(8,128)(2,1)S(1)}, u32[]{:S(2)}, u32[]{:S(2)}) collective-permute-start(bf16[512,128]{1,0:T(8,128)(2,1)S(1)} %pad_maximum_fusion.1), channel_id=1, source_target_pairs={{0,1},{1,0},{2,3},{3,2},{4,5},{5,4},{6,7},{7,6},{8,9},{9,8},{10,11... | collective-permute-start | bytes 393224 | tf_op jit(solution)/shard_map/ppermute | solution.py:189
where the time goes:
time: 82.7 us; the launch traced here: 82.3 us
  waiting for transfers between devices  37.9 us (46%)
  starting transfers between devices  22 us (27%)
  Pallas kernels  14.9 us (18%)
  local copies, waits for them, and re-layouts  6.09 us (7%)
  between operations  0.85 us (1%)
    ppermute x8, waiting for transfers between devices, passed_along(): lax.ppermute(value, axis, [(source, source + steps) for source in range(i...  33.6 us
    ppermute x8, starting transfers between devices, passed_along(): lax.ppermute(value, axis, [(source, source + steps) for source in range(i...  21.2 us
    pallas_call x1, Pallas kernels, attention_block(): pl.pallas_call(attention_kernel, out_shape=[wide, wide, own, term, term,...  14.9 us
    unnamed x16, local copies, waits for them, and re-layouts  4.77 us
    ppermute x1, waiting for transfers between devices, from_partner(): return lax.ppermute(value, axis, pairs)  4.22 us
  transfers between devices with their start and end apart: 9, of which 6 were waited for; matrix products, arithmetic and copies ran while one was open for 0% of the time, Pallas kernels for 0%

commit v1 on v0

v1 whole, which is shorter than its diff:
```python
import math

import jax
import jax.numpy as jnp
from jax import lax
from jax.experimental import pallas as pl
from jax.experimental.pallas import tpu as pltpu
from jax.sharding import PartitionSpec as P

HEAD_DIM = 128
HEADS = 16
KV_HEADS = 2
WINDOW = 4
TOK_DEV = 512
NDOCS = 64
LOCAL = 4
HALF = HEAD_DIM // 2
TILE = 256
SPAN = (WINDOW + 1) * TOK_DEV
N_TILES = SPAN // TILE
LANES = LOCAL * TILE
SCALE = HEAD_DIM ** (-0.5)
SCALE_LOG2 = SCALE * math.log2(math.e)
NEG = -1e30


def contract_last(first_matrix, second_matrix):
    return lax.dot_general(
        first_matrix, second_matrix, (((1,), (1,)), ((), ())), preferred_element_type=jnp.float32
    )


def matmul(first_matrix, second_matrix):
    return jnp.dot(first_matrix, second_matrix, preferred_element_type=jnp.float32)


def attention_kernel(
    lengths_ref, block_ref, q_ref, grad_ref, kv0, kv1, kv2, kv3, kv4, far,
    out_ref, dq_ref, t0, t1, t2, t3, t4a, t4b,
    kv_buf, scores, grads, kv_acc, kv_t, q_cat, g_cat, q_t, g_t, o_acc, dq_acc, sems,
):
    is_far = block_ref[1] == 1

    def copy_in(source, row, rows, place):
        return pltpu.make_async_copy(source, kv_buf.at[pl.ds(row, rows)], sems.at[place])

    always = [
        copy_in(kv, (WINDOW - distance) * TOK_DEV, TOK_DEV, distance)
        for distance, kv in enumerate((kv0, kv1, kv2))
    ]
    near_only = [copy_in(kv3, TOK_DEV, TOK_DEV, 3), copy_in(kv4, TILE, TILE, 4)]
    far_only = [copy_in(far.at[0], TOK_DEV, TOK_DEV, 3), copy_in(far.at[1], 0, TOK_DEV, 4)]
    for copy in always:
        copy.start()

    @pl.when(is_far)
    def _():
        for copy in far_only:
            copy.start()

    @pl.when(jnp.logical_not(is_far))
    def _():
        for copy in near_only:
            copy.start()

    kv_acc[...] = jnp.zeros_like(kv_acc)
    first_query = block_ref[0] * TOK_DEV
    origin = first_query - WINDOW * TOK_DEV
    lane_pos = first_query + lax.broadcasted_iota(jnp.int32, (1, TOK_DEV), 1)

    def next_doc(doc, carry):
        end, lane_start, edges = carry
        end = end + lengths_ref[doc]
        lane_start = jnp.where(lane_pos >= end, end, lane_start)
        edges = tuple(
            jnp.where(first_query + place >= end, end, edge)
            for place, edge in zip((0, TILE - 1, TILE, TOK_DEV - 1), edges)
        )
        return end, lane_start, edges

    zero = jnp.int32(0)
    _, lane_start, edges = lax.fori_loop(
        0, NDOCS, next_doc, (zero, jnp.zeros((1, TOK_DEV), jnp.int32), (zero,) * 4), unroll=8
    )
    for copy in always:
        copy.wait()

    @pl.when(is_far)
    def _():
        for copy in far_only:
            copy.wait()

    @pl.when(jnp.logical_not(is_far))
    def _():
        for copy in near_only:
            copy.wait()

    for half in range(TOK_DEV // TILE):
        rows = slice(half * TILE, (half + 1) * TILE)
        for head in range(LOCAL):
            cols = slice(head * HEAD_DIM, (head + 1) * HEAD_DIM)
            place = slice(head * TILE, (head + 1) * TILE)
            q_cat[place, :] = q_ref[rows, cols]
            g_cat[place, :] = grad_ref[rows, cols]
            q_t[:, place] = q_ref[rows, cols].T
            g_t[:, place] = grad_ref[rows, cols].T
        diagonal = WINDOW * TOK_DEV // TILE + half
        start_rel = jnp.concatenate([lane_start[:, rows] - origin] * LOCAL, axis=1)
        query_rel = jnp.concatenate([lane_pos[:, rows] - origin] * LOCAL, axis=1)
        lowest = lax.div(edges[2 * half] - origin, TILE)
        first_full = jnp.minimum(
            lax.div(edges[2 * half + 1] - origin + TILE - 1, TILE), diagonal
        )
        def score_tile(masked, tile, row_max):
            kv_rows = pl.ds(pl.multiple_of(tile * TILE, TILE), TILE)
            raw = matmul(kv_buf[kv_rows, :HEAD_DIM], q_t[...])
            if masked:
                key_rel = tile * TILE + lax.broadcasted_iota(jnp.int32, (TILE, LANES), 0)
                raw = jnp.where((key_rel >= start_rel) & (key_rel <= query_rel), raw, NEG)
            scores[tile] = raw
            if half == 0 or masked:
                kv_t[tile] = kv_buf[kv_rows, :].T
            return jnp.maximum(row_max, jnp.max(raw.reshape(TILE // 8, 8, LANES), axis=0))

        def score_masked(tile, row_max):
            return score_tile(True, tile, row_max)

        def score_full(tile, row_max):
            return score_tile(False, tile, row_max)

        row_max = score_masked(diagonal, jnp.full((8, LANES), NEG, jnp.float32))
        row_max = lax.fori_loop(first_full, diagonal, score_full, row_max)
        row_max = lax.fori_loop(lowest, first_full, score_masked, row_max)
        shift = jnp.max(row_max, axis=0, keepdims=True) * SCALE_LOG2

        def total_tile(tile, carry):
            total, dots = carry
            kv_rows = pl.ds(pl.multiple_of(tile * TILE, TILE), TILE)
            prob_grad = matmul(kv_buf[kv_rows, HEAD_DIM:], g_t[...])
            weights = jnp.exp2(scores[tile] * SCALE_LOG2 - shift)
            scores[tile] = weights
            grads[tile] = prob_grad
            total = total + jnp.sum(weights.reshape(TILE // 8, 8, LANES), axis=0)
            dots = dots + jnp.sum((weights * prob_grad).reshape(TILE // 8, 8, LANES), axis=0)
            return total, dots

        nothing = jnp.zeros((8, LANES), jnp.float32)
        total, dots = lax.fori_loop(lowest, diagonal + 1, total_tile, (nothing, nothing))
        inverse = 1.0 / jnp.sum(total, axis=0, keepdims=True)
        grad_dot = jnp.sum(dots, axis=0, keepdims=True) * inverse
        o_acc[...] = jnp.zeros_like(o_acc)
        dq_acc[...] = jnp.zeros_like(dq_acc)

        def backward_tile(tile, carry):
            kv_rows = pl.ds(pl.multiple_of(tile * TILE, TILE), TILE)
            keys = kv_buf[kv_rows, :HEAD_DIM]
            values = kv_buf[kv_rows, HEAD_DIM:]
            weights = scores[tile] * inverse
            score_grad = (weights * (grads[tile] - grad_dot)).astype(jnp.bfloat16)
            prob = weights.astype(jnp.bfloat16)
            kv_acc[kv_rows, HEAD_DIM:] += matmul(prob, g_cat[...])
            kv_acc[kv_rows, :HEAD_DIM] += matmul(score_grad, q_cat[...])
            o_acc[...] += matmul(kv_t[tile, HEAD_DIM:], prob)
            dq_acc[...] += matmul(kv_t[tile, :HEAD_DIM], score_grad)
            return carry

        lax.fori_loop(lowest, diagonal + 1, backward_tile, 0)
        for head in range(LOCAL):
            cols = slice(head * HEAD_DIM, (head + 1) * HEAD_DIM)
            place = slice(head * TILE, (head + 1) * TILE)
            out_ref[rows, cols] = o_acc[:, place].T.astype(jnp.bfloat16)
        for head in range(LOCAL):
            cols = slice(head * HEAD_DIM, (head + 1) * HEAD_DIM)
            place = slice(head * TILE, (head + 1) * TILE)
            dq_ref[rows, cols] = (dq_acc[:, place].T * SCALE).astype(jnp.bfloat16)
    def write_term(term, row, rows):
        keys = (kv_acc[row : row + rows, :HEAD_DIM] * SCALE).T.astype(term.dtype)
        values = kv_acc[row : row + rows, HEAD_DIM:].T.astype(term.dtype)
        for half in range(2):
            part = slice(half * HALF, (half + 1) * HALF)
            term[2 * half * HALF : (2 * half + 1) * HALF, :] = keys[part]
            term[(2 * half + 1) * HALF : (2 * half + 2) * HALF, :] = values[part]

    for distance, term in enumerate((t0, t1, t2, t3)):
        write_term(term, (WINDOW - distance) * TOK_DEV, TOK_DEV)
    write_term(t4a, 0, TILE)
    write_term(t4b, TILE, TILE)


def attention_block(lengths, block, queries, grads, kv_blocks, far_blocks):
    vmem = pl.BlockSpec(memory_space=pltpu.VMEM)
    smem = pl.BlockSpec(memory_space=pltpu.SMEM)
    anywhere = pl.BlockSpec(memory_space=pl.ANY)
    wide = jax.ShapeDtypeStruct((TOK_DEV, LOCAL * HEAD_DIM), jnp.bfloat16)
    own = jax.ShapeDtypeStruct((2 * HEAD_DIM, TOK_DEV), jnp.float32)
    term = jax.ShapeDtypeStruct((2 * HEAD_DIM, TOK_DEV), jnp.bfloat16)
    short = jax.ShapeDtypeStruct((2 * HEAD_DIM, TILE), jnp.bfloat16)
    return pl.pallas_call(
        attention_kernel,
        out_shape=[wide, wide, own, term, term, term, short, short],
        in_specs=[smem, smem, vmem, vmem] + [anywhere] * 6,
        out_specs=[vmem] * 8,
        scratch_shapes=[
            pltpu.VMEM((SPAN, 2 * HEAD_DIM), jnp.bfloat16),
            pltpu.VMEM((N_TILES, TILE, LANES), jnp.float32),
            pltpu.VMEM((N_TILES, TILE, LANES), jnp.float32),
            pltpu.VMEM((SPAN, 2 * HEAD_DIM), jnp.float32),
            pltpu.VMEM((N_TILES, 2 * HEAD_DIM, TILE), jnp.bfloat16),
            pltpu.VMEM((LANES, HEAD_DIM), jnp.bfloat16),
            pltpu.VMEM((LANES, HEAD_DIM), jnp.bfloat16),
            pltpu.VMEM((HEAD_DIM, LANES), jnp.bfloat16),
            pltpu.VMEM((HEAD_DIM, LANES), jnp.bfloat16),
            pltpu.VMEM((HEAD_DIM, LANES), jnp.float32),
            pltpu.VMEM((HEAD_DIM, LANES), jnp.float32),
            pltpu.SemaphoreType.DMA((WINDOW + 1,)),
        ],
        compiler_params=pltpu.CompilerParams(vmem_limit_bytes=44 * 1024 * 1024),
        cost_estimate=pl.CostEstimate(
            flops=5 * 10**9, bytes_accessed=4 * 10**6, transcendentals=6 * 10**6
        ),
        name="attention",
    )(lengths, block, queries, grads, *kv_blocks, far_blocks)


def moved(value, pairs):
    return lax.ppermute(value, "ctx", pairs)


def from_partner(value, axis, apart):
    mask = 2**apart
    pairs = [(source, source ^ mask) for source in range(lax.axis_size(axis))]
    return lax.ppermute(value, axis, pairs)


def pairs_at(distance, count):
    return [(source, source + distance) for source in range(count - distance)]


def needed(source, target):
    return target < 5 or source >= 4


def reversed_pairs(pairs):
    return [(target, source) for source, target in pairs]


def any_far(lengths):
    ends = jnp.cumsum(lengths)
    starts = ends - lengths
    blocks_back = (ends - 1) // TOK_DEV - starts // TOK_DEV
    return jnp.any((blocks_back >= 3) & (jnp.arange(NDOCS) != 1))


def shards(query_states, key_states, value_states, out_grad, lengths):
    count = lax.axis_size("ctx")
    block_index = lax.axis_index("ctx")
    head_index = lax.axis_index("head")
    kv_start = head_index * LOCAL // (HEADS // KV_HEADS) * HEAD_DIM
    own_half = head_index % 2
    own_keys = lax.dynamic_slice_in_dim(key_states, kv_start, HEAD_DIM, 1)
    own_values = lax.dynamic_slice_in_dim(value_states, kv_start, HEAD_DIM, 1)
    own_pair = jnp.concatenate([own_keys, own_values], axis=1)
    near = {
        distance: [pair for pair in pairs_at(distance, count) if needed(*pair)]
        for distance in (1, 2)
    }
    near[3] = [(0, 3), (1, 4)]
    near[4] = [(0, 4)]
    wide = {
        distance: [pair for pair in pairs_at(distance, count) if needed(*pair)]
        for distance in (3, 4)
    }
    second = moved(own_pair, near[2])
    first = moved(own_pair, near[1])
    third = moved(own_pair, near[3])
    fourth = moved(own_pair[TILE:], near[4])
    is_far = any_far(lengths)
    far_blocks = lax.cond(
        is_far,
        lambda pair: jnp.stack([moved(pair, wide[3]), moved(pair, wide[4])]),
        lambda pair: jnp.zeros((2,) + pair.shape, pair.dtype),
        own_pair,
    )
    place = jnp.stack([block_index.astype(jnp.int32), is_far.astype(jnp.int32)])
    attended, query_grad, t0, t1, t2, t3, t4a, t4b = attention_block(
        lengths, place, query_states, out_grad, [own_pair, first, second, third, fourth], far_blocks
    )
    back4 = moved(t4b, reversed_pairs(near[4]))
    back3 = moved(t3, reversed_pairs(near[3]))
    back2 = moved(t2, reversed_pairs(near[2]))
    back1 = moved(t1, reversed_pairs(near[1]))

    def far_terms(third_term, fourth_term):
        from3 = moved(third_term, [p for p in reversed_pairs(wide[3]) if p[1] > 1])
        from4 = moved(fourth_term, [p for p in reversed_pairs(wide[4]) if p[1] > 0])
        return from3.astype(jnp.float32) + from4.astype(jnp.float32)

    far_sum = lax.cond(
        is_far,
        lambda args: far_terms(args[0], jnp.concatenate([args[1], args[2]], axis=1)),
        lambda args: jnp.zeros(t0.shape, jnp.float32),
        (t3, t4a, t4b),
    )
    sums = [back1, back2, back3, jnp.pad(back4, ((0, 0), (TILE, 0)))]
    gathered = t0 + far_sum
    for term in sums:
        gathered = gathered + term.astype(jnp.float32)
    outgoing = lax.dynamic_slice_in_dim(gathered, (1 - own_half) * HEAD_DIM, HEAD_DIM, 0)
    received = from_partner(outgoing.astype(jnp.bfloat16), "head", 0).astype(jnp.float32)
    kept = lax.dynamic_slice_in_dim(gathered, own_half * HEAD_DIM, HEAD_DIM, 0)
    both = (kept + received).astype(jnp.bfloat16)
    return attended, query_grad, both[:HALF].T, both[HALF:].T


def solution(mesh):
    return jax.shard_map(
        shards,
        mesh=mesh,
        in_specs=(P("ctx", "head"), P("ctx", None), P("ctx", None), P("ctx", "head"), P()),
        out_specs=(P("ctx", "head"), P("ctx", "head"), P("ctx", "head"), P("ctx", "head")),
        check_vma=False,
    )
```

time: 82.7 us -> 59.2 us (0.72)
  the two profiles are of different devices: /device:TPU:28 before, /device:TPU:16 now
where the time goes in v1:
time: 59.2 us; the launch traced here: 58.8 us
  waiting for transfers between devices  29.4 us (50%)
  starting transfers between devices  18 us (30%)
  Pallas kernels  6.06 us (10%)
  other arithmetic  1.9 us (3%)
  local copies, waits for them, and re-layouts  1.88 us (3%)
  between operations  1.5 us (3%)
    ppermute x8, waiting for transfers between devices, moved(): return lax.ppermute(value, 'ctx', pairs)  25.7 us
    ppermute x8, starting transfers between devices, moved(): return lax.ppermute(value, 'ctx', pairs)  16.7 us
    pallas_call x1, Pallas kernels, attention_block(): pl.pallas_call(attention_kernel, out_shape=[wide, wide, own, term, term,...  6.06 us
    ppermute x1, waiting for transfers between devices, from_partner(): return lax.ppermute(value, axis, pairs)  3.68 us
    ppermute x1, starting transfers between devices, from_partner(): return lax.ppermute(value, axis, pairs)  1.37 us
  transfers between devices with their start and end apart: 9, of which 3 were waited for; matrix products, arithmetic and copies ran while one was open for 2% of the time, Pallas kernels for 0%

profile of v1, /device:TPU:16, one launch (start us, length us, event | category | flops | bytes accessed | tf_op | source)
XLA Modules:
  0.0 58.8 jit_solution(15242083185993334800)
XLA Ops:
  0.7 1.0 %constant_dynamic-slice_fusion = (bf16[512,128]{1,0:T(8,128)(2,1)S(1)}, bf16[512,128]{1,0:T(8,128)(2,1)S(1)}) fusion(bf16[512,256]{1,0:T(8,128)(2,1)} %param.11, s32[]{:T(128)S(6)} %select_n.32, bf16[512,256]{1,0:T(8,128)(2,1)} %param.10), kind=kLoop, calls=%fused_computation.21 | loop fusion | bytes 524292 | tf_op jit(solution)/shard_map/dynamic_slice | solution.py:261
  1.6 0.7 %pad_maximum_fusion.2.kv0 = bf16[512,256]{1,0:T(8,128)(2,1)} fusion(bf16[512,128]{1,0:T(8,128)(2,1)S(1)} %get-tuple-element.38, bf16[512,128]{1,0:T(8,128)(2,1)S(1)} %get-tuple-element.39), kind=kLoop, calls=%fused_computation.5 | loop fusion | flops 524288 | bytes 524288 | tf_op jit(solution)/shard_map/concatenate | solution.py:262
  2.4 0.0 copy-start
  2.4 1.9 %collective-permute-start.4 = (bf16[512,256]{1,0:T(8,128)(2,1)}, bf16[512,256]{1,0:T(8,128)(2,1)S(1)}, u32[]{:S(2)}, u32[]{:S(2)}) collective-permute-start(bf16[512,256]{1,0:T(8,128)(2,1)} %pad_maximum_fusion.2.kv0), channel_id=1, source_target_pairs={{0,4},{4,8},{8,12},{12,16},{16,20},{20,24},{24,28},{28,32},{32,36}... | collective-permute-start | bytes 786440 | tf_op jit(solution)/shard_map/ppermute | solution.py:226
  4.3 3.6 %collective-permute-start.5 = (bf16[512,256]{1,0:T(8,128)(2,1)}, bf16[512,256]{1,0:T(8,128)(2,1)S(1)}, u32[]{:S(2)}, u32[]{:S(2)}) collective-permute-start(bf16[512,256]{1,0:T(8,128)(2,1)} %pad_maximum_fusion.2.kv0), channel_id=1, source_target_pairs={{0,8},{4,12},{8,16},{16,24},{20,28},{24,32},{28,36},{32,40},{36,44... | collective-permute-start | bytes 786440 | tf_op jit(solution)/shard_map/ppermute | solution.py:226
  7.8 2.5 %collective-permute-start.6 = (bf16[512,256]{1,0:T(8,128)(2,1)}, bf16[512,256]{1,0:T(8,128)(2,1)S(1)}, u32[]{:S(2)}, u32[]{:S(2)}) collective-permute-start(bf16[512,256]{1,0:T(8,128)(2,1)} %pad_maximum_fusion.2.kv0), channel_id=1, source_target_pairs={{0,12},{4,16},{1,13},{5,17},{2,14},{6,18},{3,15},{7,19}} | collective-permute-start | bytes 786440 | tf_op jit(solution)/shard_map/ppermute | solution.py:226
  10.3 0.0 copy-done
  10.3 0.1 copy.10
  10.4 0.1 reduce-window.9
  10.5 0.1 reduce
  10.7 0.7 %and_reduce_fusion = pred[]{:T(512)} fusion(s32[64]{0:T(128)S(1)} %reduce, s32[64]{0:T(128)S(1)} %copy-done), kind=kLoop, calls=%fused_computation.12 | loop fusion | flops 2367 | bytes 513 | tf_op jit(solution)/shard_map/reduce_or | solution.py:251
  12.0 0.0 copy-start.1
  12.0 0.0 copy-start.2
  12.0 0.1 conditional.2
  12.1 3.6 %collective-permute-start.7 = (bf16[256,256]{1,0:T(8,128)(2,1)S(1)}, bf16[256,256]{1,0:T(8,128)(2,1)S(1)}, u32[]{:S(2)}, u32[]{:S(2)}) collective-permute-start(bf16[256,256]{1,0:T(8,128)(2,1)S(1)} %fusion), channel_id=1, source_target_pairs={{0,16},{1,17},{2,18},{3,19}} | collective-permute-start | bytes 393224 | tf_op jit(solution)/shard_map/ppermute | solution.py:226
  15.7 0.1 pad_add_fusion.block_ref
  15.7 6.3 %collective-permute-done.7.kv4 = bf16[256,256]{1,0:T(8,128)(2,1)S(1)} collective-permute-done((bf16[256,256]{1,0:T(8,128)(2,1)S(1)}, bf16[256,256]{1,0:T(8,128)(2,1)S(1)}, u32[]{:S(2)}, u32[]{:S(2)}) %collective-permute-start.7) | collective-permute-done | bytes 131104 | tf_op jit(solution)/shard_map/ppermute | solution.py:226
  22.0 0.0 collective-permute-done.4.kv1
  22.0 0.0 collective-permute-done.5.kv2
  22.1 0.0 collective-permute-done.6.kv3
  22.1 0.0 copy-done.1
  22.1 0.0 copy-done.2
  22.1 6.1 %attention.1 = (bf16[512,512]{1,0:T(8,128)(2,1)}, bf16[512,512]{1,0:T(8,128)(2,1)}, f32[256,512]{1,0:T(8,128)S(1)}, bf16[256,512]{1,0:T(8,128)(2,1)S(1)}, bf16[2...) custom-call(s32[64]{0:T(128)S(1)} %copy-done, ...), custom_call_target="tpu_custom_call" | custom-call | flops 5000000000 | bytes 4000000 | tf_op jit(solution)/shard_map/attention/pallas_call | solution.py:198
  28.1 1.3 %collective-permute-start.10 = (bf16[256,512]{1,0:T(8,128)(2,1)}, bf16[256,512]{1,0:T(8,128)(2,1)S(1)}, u32[]{:S(2)}, u32[]{:S(2)}) collective-permute-start(bf16[256,512]{1,0:T(8,128)(2,1)} %get-tuple-element.31), channel_id=1, source_target_pairs={{12,0},{16,4},{13,1},{17,5},{14,2},{18,6},{15,3},{19,7}} | collective-permute-start | bytes 786440 | tf_op jit(solution)/shard_map/ppermute | solution.py:226
  29.4 1.3 %collective-permute-start.8 = (bf16[256,512]{1,0:T(8,128)(2,1)S(1)}, bf16[256,512]{1,0:T(8,128)(2,1)S(1)}, u32[]{:S(2)}, u32[]{:S(2)}) collective-permute-start(bf16[256,512]{1,0:T(8,128)(2,1)S(1)} %get-tuple-element.34), channel_id=1, source_target_pairs={{4,0},{8,4},{12,8},{16,12},{20,16},{24,20},{28,24},{32,28},{36,32}... | collective-permute-start | bytes 786440 | tf_op jit(solution)/shard_map/ppermute | solution.py:226
  30.7 1.3 %collective-permute-start.9 = (bf16[256,512]{1,0:T(8,128)(2,1)S(1)}, bf16[256,512]{1,0:T(8,128)(2,1)S(1)}, u32[]{:S(2)}, u32[]{:S(2)}) collective-permute-start(bf16[256,512]{1,0:T(8,128)(2,1)S(1)} %get-tuple-element.35), channel_id=1, source_target_pairs={{8,0},{12,4},{16,8},{24,16},{28,20},{32,24},{36,28},{40,32},{44,36... | collective-permute-start | bytes 786440 | tf_op jit(solution)/shard_map/ppermute | solution.py:226
  32.0 0.1 conditional.3
  32.1 0.1 broadcast.21
  32.1 1.3 %collective-permute-start.11 = (bf16[256,256]{1,0:T(8,128)(2,1)}, bf16[256,256]{1,0:T(8,128)(2,1)S(1)}, u32[]{:S(2)}, u32[]{:S(2)}) collective-permute-start(bf16[256,256]{1,0:T(8,128)(2,1)} %get-tuple-element.33), channel_id=1, source_target_pairs={{16,0},{17,1},{18,2},{19,3}} | collective-permute-start | bytes 393224 | tf_op jit(solution)/shard_map/ppermute | solution.py:226
  33.4 19.4 %collective-permute-done.11 = bf16[256,256]{1,0:T(8,128)(2,1)S(1)} collective-permute-done((bf16[256,256]{1,0:T(8,128)(2,1)}, bf16[256,256]{1,0:T(8,128)(2,1)S(1)}, u32[]{:S(2)}, u32[]{:S(2)}) %collective-permute-start.11) | collective-permute-done | bytes 131104 | tf_op jit(solution)/shard_map/ppermute | solution.py:226
  52.8 0.0 collective-permute-done.10
  52.8 0.0 collective-permute-done.8
  52.8 0.0 collective-permute-done.9
  52.8 0.2 convert_add_fusion.1
  53.1 1.4 %collective-permute-start.12 = (bf16[128,512]{1,0:T(8,128)(2,1)S(1)}, bf16[128,512]{1,0:T(8,128)(2,1)S(1)}, u32[]{:S(2)}, u32[]{:S(2)}) collective-permute-start(bf16[128,512]{1,0:T(8,128)(2,1)S(1)} %dynamic-slice_convert_fusion), channel_id=1, source_target_pairs={{0,1},{1,0},{2,3},{3,2},{4,5},{5,4},{6,7},{7,6},{8,9},{9,8},{10,11... | collective-permute-start | bytes 393224 | tf_op jit(solution)/shard_map/ppermute | solution.py:232
  54.5 3.7 %collective-permute-done.12 = bf16[128,512]{1,0:T(8,128)(2,1)S(1)} collective-permute-done((bf16[128,512]{1,0:T(8,128)(2,1)S(1)}, bf16[128,512]{1,0:T(8,128)(2,1)S(1)}, u32[]{:S(2)}, u32[]{:S(2)}) %collective-permute-start.12) | collective-permute-done | bytes 131104 | tf_op jit(solution)/shard_map/ppermute | solution.py:232
  58.2 0.7 %slice_bitcast_fusion = (bf16[512,64]{0,1:T(8,128)(2,1)}, bf16[512,64]{0,1:T(8,128)(2,1)}) fusion(bf16[128,512]{1,0:T(8,128)(2,1)S(1)} %add_convert_fusion), kind=kLoop, calls=%fused_computation.10 | loop fusion | bytes 262144 | tf_op jit(solution)/shard_map/transpose | solution.py:312
  (4 shorter events, 0.1 us)
Async XLA Ops:
  2.4 8.0 %copy-start = (s32[64]{0:T(128)S(1)}, s32[64]{0:T(128)}, u32[]{:S(2)}) copy-start(s32[64]{0:T(128)} %lengths_ref.1) | copy-start | bytes 772
  2.4 19.7 %collective-permute-start.4 = (bf16[512,256]{1,0:T(8,128)(2,1)}, bf16[512,256]{1,0:T(8,128)(2,1)S(1)}, u32[]{:S(2)}, u32[]{:S(2)}) collective-permute-start(bf16[512,256]{1,0:T(8,128)(2,1)} %pad_maximum_fusion.2.kv0), channel_id=1, source_target_pairs={{0,4},{4,8},{8,12},{12,16},{16,20},{20,24},{24,28},{28,32},{32,36}... | collective-permute-start | bytes 786440 | tf_op jit(solution)/shard_map/ppermute | solution.py:226
  4.3 17.8 %collective-permute-start.5 = (bf16[512,256]{1,0:T(8,128)(2,1)}, bf16[512,256]{1,0:T(8,128)(2,1)S(1)}, u32[]{:S(2)}, u32[]{:S(2)}) collective-permute-start(bf16[512,256]{1,0:T(8,128)(2,1)} %pad_maximum_fusion.2.kv0), channel_id=1, source_target_pairs={{0,8},{4,12},{8,16},{16,24},{20,28},{24,32},{28,36},{32,40},{36,44... | collective-permute-start | bytes 786440 | tf_op jit(solution)/shard_map/ppermute | solution.py:226
  7.8 14.2 %collective-permute-start.6 = (bf16[512,256]{1,0:T(8,128)(2,1)}, bf16[512,256]{1,0:T(8,128)(2,1)S(1)}, u32[]{:S(2)}, u32[]{:S(2)}) collective-permute-start(bf16[512,256]{1,0:T(8,128)(2,1)} %pad_maximum_fusion.2.kv0), channel_id=1, source_target_pairs={{0,12},{4,16},{1,13},{5,17},{2,14},{6,18},{3,15},{7,19}} | collective-permute-start | bytes 786440 | tf_op jit(solution)/shard_map/ppermute | solution.py:226
  12.0 10.1 %copy-start.1 = (bf16[512,512]{1,0:T(8,128)(2,1)S(1)}, bf16[512,512]{1,0:T(8,128)(2,1)}, u32[]{:S(2)}) copy-start(bf16[512,512]{1,0:T(8,128)(2,1)} %q_ref.1) | copy-start | bytes 1572868
  12.0 10.1 %copy-start.2 = (bf16[512,512]{1,0:T(8,128)(2,1)S(1)}, bf16[512,512]{1,0:T(8,128)(2,1)}, u32[]{:S(2)}) copy-start(bf16[512,512]{1,0:T(8,128)(2,1)} %grad_ref.1) | copy-start | bytes 1572868
  12.1 10.0 %collective-permute-start.7 = (bf16[256,256]{1,0:T(8,128)(2,1)S(1)}, bf16[256,256]{1,0:T(8,128)(2,1)S(1)}, u32[]{:S(2)}, u32[]{:S(2)}) collective-permute-start(bf16[256,256]{1,0:T(8,128)(2,1)S(1)} %fusion), channel_id=1, source_target_pairs={{0,16},{1,17},{2,18},{3,19}} | collective-permute-start | bytes 393224 | tf_op jit(solution)/shard_map/ppermute | solution.py:226
  28.1 24.7 %collective-permute-start.10 = (bf16[256,512]{1,0:T(8,128)(2,1)}, bf16[256,512]{1,0:T(8,128)(2,1)S(1)}, u32[]{:S(2)}, u32[]{:S(2)}) collective-permute-start(bf16[256,512]{1,0:T(8,128)(2,1)} %get-tuple-element.31), channel_id=1, source_target_pairs={{12,0},{16,4},{13,1},{17,5},{14,2},{18,6},{15,3},{19,7}} | collective-permute-start | bytes 786440 | tf_op jit(solution)/shard_map/ppermute | solution.py:226
  29.4 23.4 %collective-permute-start.8 = (bf16[256,512]{1,0:T(8,128)(2,1)S(1)}, bf16[256,512]{1,0:T(8,128)(2,1)S(1)}, u32[]{:S(2)}, u32[]{:S(2)}) collective-permute-start(bf16[256,512]{1,0:T(8,128)(2,1)S(1)} %get-tuple-element.34), channel_id=1, source_target_pairs={{4,0},{8,4},{12,8},{16,12},{20,16},{24,20},{28,24},{32,28},{36,32}... | collective-permute-start | bytes 786440 | tf_op jit(solution)/shard_map/ppermute | solution.py:226
  30.7 22.1 %collective-permute-start.9 = (bf16[256,512]{1,0:T(8,128)(2,1)S(1)}, bf16[256,512]{1,0:T(8,128)(2,1)S(1)}, u32[]{:S(2)}, u32[]{:S(2)}) collective-permute-start(bf16[256,512]{1,0:T(8,128)(2,1)S(1)} %get-tuple-element.35), channel_id=1, source_target_pairs={{8,0},{12,4},{16,8},{24,16},{28,20},{32,24},{36,28},{40,32},{44,36... | collective-permute-start | bytes 786440 | tf_op jit(solution)/shard_map/ppermute | solution.py:226
  32.1 20.7 %collective-permute-start.11 = (bf16[256,256]{1,0:T(8,128)(2,1)}, bf16[256,256]{1,0:T(8,128)(2,1)S(1)}, u32[]{:S(2)}, u32[]{:S(2)}) collective-permute-start(bf16[256,256]{1,0:T(8,128)(2,1)} %get-tuple-element.33), channel_id=1, source_target_pairs={{16,0},{17,1},{18,2},{19,3}} | collective-permute-start | bytes 393224 | tf_op jit(solution)/shard_map/ppermute | solution.py:226
  53.1 5.1 %collective-permute-start.12 = (bf16[128,512]{1,0:T(8,128)(2,1)S(1)}, bf16[128,512]{1,0:T(8,128)(2,1)S(1)}, u32[]{:S(2)}, u32[]{:S(2)}) collective-permute-start(bf16[128,512]{1,0:T(8,128)(2,1)S(1)} %dynamic-slice_convert_fusion), channel_id=1, source_target_pairs={{0,1},{1,0},{2,3},{3,2},{4,5},{5,4},{6,7},{7,6},{8,9},{9,8},{10,11... | collective-permute-start | bytes 393224 | tf_op jit(solution)/shard_map/ppermute | solution.py:232

commit v2 on v1

--- a/solution.py
+++ b/solution.py
@@ -35,36 +35,41 @@
 
 
 def attention_kernel(
-    lengths_ref, block_ref, q_ref, grad_ref, kv0, kv1, kv2, kv3, kv4, far,
+    lengths_ref, block_ref, q_ref, grad_ref, kv0, kv1, kv2, swapped, kv3, kv4, far,
     out_ref, dq_ref, t0, t1, t2, t3, t4a, t4b,
     kv_buf, scores, grads, kv_acc, kv_t, q_cat, g_cat, q_t, g_t, o_acc, dq_acc, sems,
 ):
+    block = block_ref[0]
     is_far = block_ref[1] == 1
 
     def copy_in(source, row, rows, place):
         return pltpu.make_async_copy(source, kv_buf.at[pl.ds(row, rows)], sems.at[place])
 
+    by_case = (
+        (block != 2, [copy_in(kv1, 3 * TOK_DEV, TOK_DEV, 1)]),
+        (block == 2, [copy_in(swapped, 3 * TOK_DEV, TOK_DEV, 1)]),
+        (block == 3, [copy_in(swapped, TOK_DEV, TOK_DEV, 3)]),
+        (block == 4, [copy_in(kv3, TOK_DEV, TOK_DEV, 3), copy_in(kv4, TILE, TILE, 4)]),
+        (
+            is_far & (block > 4),
+            [copy_in(far.at[0], TOK_DEV, TOK_DEV, 3), copy_in(far.at[1], 0, TOK_DEV, 4)],
+        ),
+    )
     always = [
-        copy_in(kv, (WINDOW - distance) * TOK_DEV, TOK_DEV, distance)
-        for distance, kv in enumerate((kv0, kv1, kv2))
+        copy_in(kv0, WINDOW * TOK_DEV, TOK_DEV, 0),
+        copy_in(kv2, 2 * TOK_DEV, TOK_DEV, 2),
     ]
-    near_only = [copy_in(kv3, TOK_DEV, TOK_DEV, 3), copy_in(kv4, TILE, TILE, 4)]
-    far_only = [copy_in(far.at[0], TOK_DEV, TOK_DEV, 3), copy_in(far.at[1], 0, TOK_DEV, 4)]
     for copy in always:
         copy.start()
-
-    @pl.when(is_far)
-    def _():
-        for copy in far_only:
-            copy.start()
-
-    @pl.when(jnp.logical_not(is_far))
-    def _():
-        for copy in near_only:
-            copy.start()
+    for case, copies in by_case:
+
+        @pl.when(case)
+        def _(copies=copies):
+            for copy in copies:
+                copy.start()
 
     kv_acc[...] = jnp.zeros_like(kv_acc)
-    first_query = block_ref[0] * TOK_DEV
+    first_query = block * TOK_DEV
     origin = first_query - WINDOW * TOK_DEV
     lane_pos = first_query + lax.broadcasted_iota(jnp.int32, (1, TOK_DEV), 1)
 
@@ -84,16 +89,12 @@
     )
     for copy in always:
         copy.wait()
-
-    @pl.when(is_far)
-    def _():
-        for copy in far_only:
-            copy.wait()
-
-    @pl.when(jnp.logical_not(is_far))
-    def _():
-        for copy in near_only:
-            copy.wait()
+    for case, copies in by_case:
+
+        @pl.when(case)
+        def _(copies=copies):
+            for copy in copies:
+                copy.wait()
 
     for half in range(TOK_DEV // TILE):
         rows = slice(half * TILE, (half + 1) * TILE)
@@ -187,6 +188,48 @@
     write_term(t4b, TILE, TILE)
 
 
+def pick_kernel(column_ref, keys_ref, values_ref, pair_ref, high_ref, sems):
+    column = pl.multiple_of(column_ref[0], HEAD_DIM)
+    copies = []
+    for place, source in enumerate((keys_ref, values_ref)):
+        cols = pl.ds(place * HEAD_DIM, HEAD_DIM)
+        copies.append(
+            pltpu.make_async_copy(
+                source.at[:, pl.ds(column, HEAD_DIM)], pair_ref.at[:, cols], sems.at[place]
+            )
+        )
+        copies.append(
+            pltpu.make_async_copy(
+                source.at[pl.ds(TILE, TILE), pl.ds(column, HEAD_DIM)],
+                high_ref.at[:, cols],
+                sems.at[2 + place],
+            )
+        )
+    for copy in copies:
+        copy.start()
+    for copy in copies:
+        copy.wait()
+
+
+def pick_block(column, keys, values):
+    smem = pl.BlockSpec(memory_space=pltpu.SMEM)
+    vmem = pl.BlockSpec(memory_space=pltpu.VMEM)
+    anywhere = pl.BlockSpec(memory_space=pltpu.HBM)
+    return pl.pallas_call(
+        pick_kernel,
+        out_shape=[
+            jax.ShapeDtypeStruct((TOK_DEV, 2 * HEAD_DIM), jnp.bfloat16),
+            jax.ShapeDtypeStruct((TILE, 2 * HEAD_DIM), jnp.bfloat16),
+        ],
+        in_specs=[smem, anywhere, anywhere],
+        out_specs=[vmem, vmem],
+        scratch_shapes=[pltpu.SemaphoreType.DMA((4,))],
+        compiler_params=pltpu.CompilerParams(vmem_limit_bytes=60 * 1024 * 1024),
+        cost_estimate=pl.CostEstimate(flops=0, bytes_accessed=10**6, transcendentals=0),
+        name="pick",
+    )(column, keys, values)
+
+
 def attention_block(lengths, block, queries, grads, kv_blocks, far_blocks):
     vmem = pl.BlockSpec(memory_space=pltpu.VMEM)
     smem = pl.BlockSpec(memory_space=pltpu.SMEM)
@@ -198,7 +241,7 @@
     return pl.pallas_call(
         attention_kernel,
         out_shape=[wide, wide, own, term, term, term, short, short],
-        in_specs=[smem, smem, vmem, vmem] + [anywhere] * 6,
+        in_specs=[smem, smem, vmem, vmem] + [anywhere] * 7,
         out_specs=[vmem] * 8,
         scratch_shapes=[
             pltpu.VMEM((SPAN, 2 * HEAD_DIM), jnp.bfloat16),
@@ -257,54 +300,52 @@
     head_index = lax.axis_index("head")
     kv_start = head_index * LOCAL // (HEADS // KV_HEADS) * HEAD_DIM
     own_half = head_index % 2
-    own_keys = lax.dynamic_slice_in_dim(key_states, kv_start, HEAD_DIM, 1)
-    own_values = lax.dynamic_slice_in_dim(value_states, kv_start, HEAD_DIM, 1)
-    own_pair = jnp.concatenate([own_keys, own_values], axis=1)
+    own_pair, own_high = pick_block(
+        kv_start.astype(jnp.int32).reshape(1), key_states, value_states
+    )
     near = {
         distance: [pair for pair in pairs_at(distance, count) if needed(*pair)]
         for distance in (1, 2)
     }
     near[3] = [(0, 3), (1, 4)]
     near[4] = [(0, 4)]
-    wide = {
-        distance: [pair for pair in pairs_at(distance, count) if needed(*pair)]
-        for distance in (3, 4)
-    }
+    wide = {distance: pairs_at(distance, count)[WINDOW:] for distance in (3, 4)}
     second = moved(own_pair, near[2])
-    first = moved(own_pair, near[1])
-    third = moved(own_pair, near[3])
-    fourth = moved(own_pair[TILE:], near[4])
+    first = moved(own_pair, [pair for pair in near[1] if pair != (1, 2)])
+    third = moved(own_pair, near[3][1:])
+    fourth = moved(own_high, near[4])
+    second, fourth, kept_pair = lax.optimization_barrier((second, fourth, own_pair))
+    swapped = moved(second, [(2, 3), (3, 2)])
     is_far = any_far(lengths)
     far_blocks = lax.cond(
         is_far,
         lambda pair: jnp.stack([moved(pair, wide[3]), moved(pair, wide[4])]),
         lambda pair: jnp.zeros((2,) + pair.shape, pair.dtype),
-        own_pair,
+        kept_pair,
     )
     place = jnp.stack([block_index.astype(jnp.int32), is_far.astype(jnp.int32)])
     attended, query_grad, t0, t1, t2, t3, t4a, t4b = attention_block(
-        lengths, place, query_states, out_grad, [own_pair, first, second, third, fourth], far_blocks
+        lengths, place, query_states, out_grad,
+        [own_pair, first, second, swapped, third, fourth], far_blocks,
     )
     back4 = moved(t4b, reversed_pairs(near[4]))
     back3 = moved(t3, reversed_pairs(near[3]))
     back2 = moved(t2, reversed_pairs(near[2]))
     back1 = moved(t1, reversed_pairs(near[1]))
-
-    def far_terms(third_term, fourth_term):
-        from3 = moved(third_term, [p for p in reversed_pairs(wide[3]) if p[1] > 1])
-        from4 = moved(fourth_term, [p for p in reversed_pairs(wide[4]) if p[1] > 0])
-        return from3.astype(jnp.float32) + from4.astype(jnp.float32)
-
-    far_sum = lax.cond(
-        is_far,
-        lambda args: far_terms(args[0], jnp.concatenate([args[1], args[2]], axis=1)),
-        lambda args: jnp.zeros(t0.shape, jnp.float32),
-        (t3, t4a, t4b),
-    )
-    sums = [back1, back2, back3, jnp.pad(back4, ((0, 0), (TILE, 0)))]
-    gathered = t0 + far_sum
-    for term in sums:
-        gathered = gathered + term.astype(jnp.float32)
+    gathered = t0 + back3.astype(jnp.float32)
+    gathered = gathered + jnp.pad(back4, ((0, 0), (TILE, 0))).astype(jnp.float32)
+    gathered = lax.optimization_barrier(gathered)
+    gathered = gathered + back2.astype(jnp.float32) + back1.astype(jnp.float32)
+
+    def with_far(total, third_term, low_term, high_term):
+        fourth_term = jnp.concatenate([low_term, high_term], axis=1)
+        from3 = moved(third_term, reversed_pairs(wide[3]))
+        from4 = moved(fourth_term, reversed_pairs(wide[4]))
+        return total + from3.astype(jnp.float32) + from4.astype(jnp.float32)
+
+    gathered = lax.cond(
+        is_far, with_far, lambda total, *others: total, gathered, t3, t4a, t4b
+    )
     outgoing = lax.dynamic_slice_in_dim(gathered, (1 - own_half) * HEAD_DIM, HEAD_DIM, 0)
     received = from_partner(outgoing.astype(jnp.bfloat16), "head", 0).astype(jnp.float32)
     kept = lax.dynamic_slice_in_dim(gathered, own_half * HEAD_DIM, HEAD_DIM, 0)

time: 59.2 us -> 55.9 us (0.944)
  the two profiles are of different devices: /device:TPU:16 before, /device:TPU:1 now
where the time goes in v2:
time: 55.9 us; the launch traced here: 55.6 us
  waiting for transfers between devices  19.7 us (35%)
  starting transfers between devices  19.6 us (35%)
  Pallas kernels  11.2 us (20%)
  local copies, waits for them, and re-layouts  2.27 us (4%)
  between operations  1.5 us (3%)
  other arithmetic  1.29 us (2%)
    ppermute x9, starting transfers between devices, moved(): return lax.ppermute(value, 'ctx', pairs)  18.2 us
    ppermute x9, waiting for transfers between devices, moved(): return lax.ppermute(value, 'ctx', pairs)  17.2 us
    pallas_call x1, Pallas kernels, attention_block(): pl.pallas_call(attention_kernel, out_shape=[wide, wide, own, term, term,...  9.46 us
    ppermute x1, waiting for transfers between devices, from_partner(): return lax.ppermute(value, axis, pairs)  2.52 us
    pallas_call x1, Pallas kernels, pick_block(): pl.pallas_call(pick_kernel, out_shape=[jax.ShapeDtypeStruct((TOK_DEV, 2 *...  1.78 us
    unnamed x8, local copies, waits for them, and re-layouts  1.45 us
    ppermute x1, starting transfers between devices, from_partner(): return lax.ppermute(value, axis, pairs)  1.38 us
  transfers between devices with their start and end apart: 10, of which 4 were waited for; matrix products, arithmetic and copies ran while one was open for 2% of the time, Pallas kernels for 0%

profile of v2, /device:TPU:1, one launch (start us, length us, event | category | flops | bytes accessed | tf_op | source)
XLA Modules:
  0.0 55.6 jit_solution(6229793889582448438)
XLA Ops:
  0.6 1.8 %pick.1 = (bf16[512,256]{1,0:T(8,128)(2,1)}, bf16[256,256]{1,0:T(8,128)(2,1)}) custom-call(s32[1]{0:T(128)} %bitcast.5.column_ref, bf16[512,256]{1,0:T(8,128)(2,1)} %keys_ref.1, bf16[512,256]{1,0:T(8,128)(2,1)} %values_ref.1), custom_call_target="tpu_custom_call" | custom-call | bytes 1000000 | tf_op jit(solution)/shard_map/pick/pallas_call | solution.py:218
  2.4 4.0 %collective-permute-start.5 = (bf16[512,256]{1,0:T(8,128)(2,1)}, bf16[512,256]{1,0:T(8,128)(2,1)S(1)}, u32[]{:S(2)}, u32[]{:S(2)}) collective-permute-start(bf16[512,256]{1,0:T(8,128)(2,1)} %get-tuple-element.41.kv0), channel_id=1, source_target_pairs={{0,8},{4,12},{8,16},{16,24},{20,28},{24,32},{28,36},{32,40},{36,44... | collective-permute-start | bytes 786440 | tf_op jit(solution)/shard_map/ppermute | solution.py:269
  6.4 0.7 %collective-permute-start.6 = (bf16[256,256]{1,0:T(8,128)(2,1)}, bf16[256,256]{1,0:T(8,128)(2,1)S(1)}, u32[]{:S(2)}, u32[]{:S(2)}) collective-permute-start(bf16[256,256]{1,0:T(8,128)(2,1)} %get-tuple-element.38), channel_id=1, source_target_pairs={{0,16},{1,17},{2,18},{3,19}} | collective-permute-start | bytes 393224 | tf_op jit(solution)/shard_map/ppermute | solution.py:269
  7.1 1.3 %collective-permute-start.4 = (bf16[512,256]{1,0:T(8,128)(2,1)}, bf16[512,256]{1,0:T(8,128)(2,1)S(1)}, u32[]{:S(2)}, u32[]{:S(2)}) collective-permute-start(bf16[512,256]{1,0:T(8,128)(2,1)} %get-tuple-element.41.kv0), channel_id=1, source_target_pairs={{0,4},{8,12},{12,16},{16,20},{20,24},{24,28},{28,32},{32,36},{36,4... | collective-permute-start | bytes 786440 | tf_op jit(solution)/shard_map/ppermute | solution.py:269
  8.4 6.4 %collective-permute-start.8 = (bf16[512,256]{1,0:T(8,128)(2,1)}, bf16[512,256]{1,0:T(8,128)(2,1)S(1)}, u32[]{:S(2)}, u32[]{:S(2)}) collective-permute-start(bf16[512,256]{1,0:T(8,128)(2,1)} %get-tuple-element.41.kv0), channel_id=1, source_target_pairs={{4,16},{5,17},{6,18},{7,19}} | collective-permute-start | bytes 786440 | tf_op jit(solution)/shard_map/ppermute | solution.py:269
  14.8 0.0 collective-permute-done.6.kv4
  14.8 0.0 collective-permute-done.5.kv2
  14.9 0.7 %collective-permute-start.7 = (bf16[512,256]{1,0:T(8,128)(2,1)S(1)}, bf16[512,256]{1,0:T(8,128)(2,1)S(1)}, u32[]{:S(2)}, u32[]{:S(2)}) collective-permute-start(bf16[512,256]{1,0:T(8,128)(2,1)S(1)} %collective-permute-done.5.kv2), channel_id=1, source_target_pairs={{8,12},{12,8},{9,13},{13,9},{10,14},{14,10},{11,15},{15,11}} | collective-permute-start | bytes 786440 | tf_op jit(solution)/shard_map/ppermute | solution.py:269
  15.5 0.0 copy-start
  15.6 0.6 %copy-done = s32[64]{0:T(128)S(1)} copy-done((s32[64]{0:T(128)S(1)}, s32[64]{0:T(128)}, u32[]{:S(2)}) %copy-start) | copy-done | bytes 280
  16.2 0.1 copy.10
  16.3 0.1 reduce-window.9
  16.4 0.1 reduce
  16.5 0.7 %and_reduce_fusion = pred[]{:T(512)} fusion(s32[64]{0:T(128)S(1)} %reduce, s32[64]{0:T(128)S(1)} %copy-done), kind=kLoop, calls=%fused_computation.9 | loop fusion | flops 2367 | bytes 513 | tf_op jit(solution)/shard_map/reduce_or | solution.py:294
  17.8 0.1 pad_add_fusion.block_ref
  17.9 0.0 copy-start.1
  17.9 0.0 copy-start.2
  17.9 0.0 copy-start.3
  18.0 0.0 collective-permute-done.4.kv1
  18.0 0.5 collective-permute-done.8.kv3
  18.5 0.3 copy-done.3
  18.7 0.0 collective-permute-done.7.swapped
  18.7 0.4 copy-done.1
  19.1 0.2 copy-done.2
  19.3 9.5 %attention.1 = (bf16[512,512]{1,0:T(8,128)(2,1)}, bf16[512,512]{1,0:T(8,128)(2,1)}, f32[256,512]{1,0:T(8,128)S(1)}, bf16[256,512]{1,0:T(8,128)(2,1)S(1)}, bf16[2...) custom-call(s32[64]{0:T(128)S(1)} %copy-done, ...), custom_call_target="tpu_custom_call" | custom-call | flops 5000000000 | bytes 4000000 | tf_op jit(solution)/shard_map/attention/pallas_call | solution.py:241
  28.7 1.3 %collective-permute-start.9 = (bf16[256,512]{1,0:T(8,128)(2,1)}, bf16[256,512]{1,0:T(8,128)(2,1)S(1)}, u32[]{:S(2)}, u32[]{:S(2)}) collective-permute-start(bf16[256,512]{1,0:T(8,128)(2,1)} %get-tuple-element.45), channel_id=1, source_target_pairs={{12,0},{16,4},{13,1},{17,5},{14,2},{18,6},{15,3},{19,7}} | collective-permute-start | bytes 786440 | tf_op jit(solution)/shard_map/ppermute | solution.py:269
  30.0 0.7 %collective-permute-start.10 = (bf16[256,256]{1,0:T(8,128)(2,1)S(1)}, bf16[256,256]{1,0:T(8,128)(2,1)S(1)}, u32[]{:S(2)}, u32[]{:S(2)}) collective-permute-start(bf16[256,256]{1,0:T(8,128)(2,1)S(1)} %get-tuple-element.46), channel_id=1, source_target_pairs={{16,0},{17,1},{18,2},{19,3}} | collective-permute-start | bytes 393224 | tf_op jit(solution)/shard_map/ppermute | solution.py:269
  30.7 1.3 %collective-permute-start.11 = (bf16[256,512]{1,0:T(8,128)(2,1)S(1)}, bf16[256,512]{1,0:T(8,128)(2,1)S(1)}, u32[]{:S(2)}, u32[]{:S(2)}) collective-permute-start(bf16[256,512]{1,0:T(8,128)(2,1)S(1)} %get-tuple-element.47), channel_id=1, source_target_pairs={{8,0},{12,4},{16,8},{24,16},{28,20},{32,24},{36,28},{40,32},{44,36... | collective-permute-start | bytes 786440 | tf_op jit(solution)/shard_map/ppermute | solution.py:269
  32.0 1.9 %collective-permute-start.12 = (bf16[256,512]{1,0:T(8,128)(2,1)S(1)}, bf16[256,512]{1,0:T(8,128)(2,1)S(1)}, u32[]{:S(2)}, u32[]{:S(2)}) collective-permute-start(bf16[256,512]{1,0:T(8,128)(2,1)S(1)} %get-tuple-element.48), channel_id=1, source_target_pairs={{4,0},{8,4},{12,8},{16,12},{20,16},{24,20},{28,24},{32,28},{36,32}... | collective-permute-start | bytes 786440 | tf_op jit(solution)/shard_map/ppermute | solution.py:269
  34.0 0.0 collective-permute-done.10
  34.0 8.8 %collective-permute-done.9 = bf16[256,512]{1,0:T(8,128)(2,1)S(1)} collective-permute-done((bf16[256,512]{1,0:T(8,128)(2,1)}, bf16[256,512]{1,0:T(8,128)(2,1)S(1)}, u32[]{:S(2)}, u32[]{:S(2)}) %collective-permute-start.9) | collective-permute-done | bytes 262176 | tf_op jit(solution)/shard_map/ppermute | solution.py:269
  42.8 0.1 convert_add_fusion.2
  42.9 7.8 %collective-permute-done.11 = bf16[256,512]{1,0:T(8,128)(2,1)S(1)} collective-permute-done((bf16[256,512]{1,0:T(8,128)(2,1)S(1)}, bf16[256,512]{1,0:T(8,128)(2,1)S(1)}, u32[]{:S(2)}, u32[]{:S(2)}) %collective-permute-start.11) | collective-permute-done | bytes 262176 | tf_op jit(solution)/shard_map/ppermute | solution.py:269
  50.7 0.0 collective-permute-done.12
  50.7 0.2 convert_add_fusion.1
  51.0 1.4 %collective-permute-start.13 = (bf16[128,512]{1,0:T(8,128)(2,1)S(1)}, bf16[128,512]{1,0:T(8,128)(2,1)S(1)}, u32[]{:S(2)}, u32[]{:S(2)}) collective-permute-start(bf16[128,512]{1,0:T(8,128)(2,1)S(1)} %dynamic-slice_convert_fusion), channel_id=1, source_target_pairs={{0,1},{1,0},{2,3},{3,2},{4,5},{5,4},{6,7},{7,6},{8,9},{9,8},{10,11... | collective-permute-start | bytes 393224 | tf_op jit(solution)/shard_map/ppermute | solution.py:275
  52.4 2.5 %collective-permute-done.13 = bf16[128,512]{1,0:T(8,128)(2,1)S(1)} collective-permute-done((bf16[128,512]{1,0:T(8,128)(2,1)S(1)}, bf16[128,512]{1,0:T(8,128)(2,1)S(1)}, u32[]{:S(2)}, u32[]{:S(2)}) %collective-permute-start.13) | collective-permute-done | bytes 131104 | tf_op jit(solution)/shard_map/ppermute | solution.py:275
  55.0 0.7 %slice_bitcast_fusion = (bf16[512,64]{0,1:T(8,128)(2,1)}, bf16[512,64]{0,1:T(8,128)(2,1)}) fusion(bf16[128,512]{1,0:T(8,128)(2,1)S(1)} %add_convert_fusion), kind=kLoop, calls=%fused_computation.7 | loop fusion | bytes 262144 | tf_op jit(solution)/shard_map/transpose | solution.py:353
  (5 shorter events, 0.1 us)
Async XLA Ops:
  2.4 12.4 %collective-permute-start.5 = (bf16[512,256]{1,0:T(8,128)(2,1)}, bf16[512,256]{1,0:T(8,128)(2,1)S(1)}, u32[]{:S(2)}, u32[]{:S(2)}) collective-permute-start(bf16[512,256]{1,0:T(8,128)(2,1)} %get-tuple-element.41.kv0), channel_id=1, source_target_pairs={{0,8},{4,12},{8,16},{16,24},{20,28},{24,32},{28,36},{32,40},{36,44... | collective-permute-start | bytes 786440 | tf_op jit(solution)/shard_map/ppermute | solution.py:269
  6.4 8.4 %collective-permute-start.6 = (bf16[256,256]{1,0:T(8,128)(2,1)}, bf16[256,256]{1,0:T(8,128)(2,1)S(1)}, u32[]{:S(2)}, u32[]{:S(2)}) collective-permute-start(bf16[256,256]{1,0:T(8,128)(2,1)} %get-tuple-element.38), channel_id=1, source_target_pairs={{0,16},{1,17},{2,18},{3,19}} | collective-permute-start | bytes 393224 | tf_op jit(solution)/shard_map/ppermute | solution.py:269
  7.1 10.9 %collective-permute-start.4 = (bf16[512,256]{1,0:T(8,128)(2,1)}, bf16[512,256]{1,0:T(8,128)(2,1)S(1)}, u32[]{:S(2)}, u32[]{:S(2)}) collective-permute-start(bf16[512,256]{1,0:T(8,128)(2,1)} %get-tuple-element.41.kv0), channel_id=1, source_target_pairs={{0,4},{8,12},{12,16},{16,20},{20,24},{24,28},{28,32},{32,36},{36,4... | collective-permute-start | bytes 786440 | tf_op jit(solution)/shard_map/ppermute | solution.py:269
  8.4 10.1 %collective-permute-start.8 = (bf16[512,256]{1,0:T(8,128)(2,1)}, bf16[512,256]{1,0:T(8,128)(2,1)S(1)}, u32[]{:S(2)}, u32[]{:S(2)}) collective-permute-start(bf16[512,256]{1,0:T(8,128)(2,1)} %get-tuple-element.41.kv0), channel_id=1, source_target_pairs={{4,16},{5,17},{6,18},{7,19}} | collective-permute-start | bytes 786440 | tf_op jit(solution)/shard_map/ppermute | solution.py:269
  14.9 3.9 %collective-permute-start.7 = (bf16[512,256]{1,0:T(8,128)(2,1)S(1)}, bf16[512,256]{1,0:T(8,128)(2,1)S(1)}, u32[]{:S(2)}, u32[]{:S(2)}) collective-permute-start(bf16[512,256]{1,0:T(8,128)(2,1)S(1)} %collective-permute-done.5.kv2), channel_id=1, source_target_pairs={{8,12},{12,8},{9,13},{13,9},{10,14},{14,10},{11,15},{15,11}} | collective-permute-start | bytes 786440 | tf_op jit(solution)/shard_map/ppermute | solution.py:269
  15.5 0.7 %copy-start = (s32[64]{0:T(128)S(1)}, s32[64]{0:T(128)}, u32[]{:S(2)}) copy-start(s32[64]{0:T(128)} %lengths_ref.1) | copy-start | bytes 772
  17.9 1.2 %copy-start.1 = (bf16[512,512]{1,0:T(8,128)(2,1)S(1)}, bf16[512,512]{1,0:T(8,128)(2,1)}, u32[]{:S(2)}) copy-start(bf16[512,512]{1,0:T(8,128)(2,1)} %q_ref.1) | copy-start | bytes 1572868
  17.9 1.4 %copy-start.2 = (bf16[512,512]{1,0:T(8,128)(2,1)S(1)}, bf16[512,512]{1,0:T(8,128)(2,1)}, u32[]{:S(2)}) copy-start(bf16[512,512]{1,0:T(8,128)(2,1)} %grad_ref.1) | copy-start | bytes 1572868
  17.9 0.8 %copy-start.3 = (bf16[2,512,256]{2,1,0:T(8,128)(2,1)}, bf16[2,512,256]{2,1,0:T(8,128)(2,1)S(1)}, u32[]{:S(2)}) copy-start(bf16[2,512,256]{2,1,0:T(8,128)(2,1)S(1)} %get-tuple-element.52.far) | copy-start | bytes 1572868
  28.7 14.1 %collective-permute-start.9 = (bf16[256,512]{1,0:T(8,128)(2,1)}, bf16[256,512]{1,0:T(8,128)(2,1)S(1)}, u32[]{:S(2)}, u32[]{:S(2)}) collective-permute-start(bf16[256,512]{1,0:T(8,128)(2,1)} %get-tuple-element.45), channel_id=1, source_target_pairs={{12,0},{16,4},{13,1},{17,5},{14,2},{18,6},{15,3},{19,7}} | collective-permute-start | bytes 786440 | tf_op jit(solution)/shard_map/ppermute | solution.py:269
  30.0 3.9 %collective-permute-start.10 = (bf16[256,256]{1,0:T(8,128)(2,1)S(1)}, bf16[256,256]{1,0:T(8,128)(2,1)S(1)}, u32[]{:S(2)}, u32[]{:S(2)}) collective-permute-start(bf16[256,256]{1,0:T(8,128)(2,1)S(1)} %get-tuple-element.46), channel_id=1, source_target_pairs={{16,0},{17,1},{18,2},{19,3}} | collective-permute-start | bytes 393224 | tf_op jit(solution)/shard_map/ppermute | solution.py:269
  30.7 20.0 %collective-permute-start.11 = (bf16[256,512]{1,0:T(8,128)(2,1)S(1)}, bf16[256,512]{1,0:T(8,128)(2,1)S(1)}, u32[]{:S(2)}, u32[]{:S(2)}) collective-permute-start(bf16[256,512]{1,0:T(8,128)(2,1)S(1)} %get-tuple-element.47), channel_id=1, source_target_pairs={{8,0},{12,4},{16,8},{24,16},{28,20},{32,24},{36,28},{40,32},{44,36... | collective-permute-start | bytes 786440 | tf_op jit(solution)/shard_map/ppermute | solution.py:269
  32.0 18.7 %collective-permute-start.12 = (bf16[256,512]{1,0:T(8,128)(2,1)S(1)}, bf16[256,512]{1,0:T(8,128)(2,1)S(1)}, u32[]{:S(2)}, u32[]{:S(2)}) collective-permute-start(bf16[256,512]{1,0:T(8,128)(2,1)S(1)} %get-tuple-element.48), channel_id=1, source_target_pairs={{4,0},{8,4},{12,8},{16,12},{20,16},{24,20},{28,24},{32,28},{36,32}... | collective-permute-start | bytes 786440 | tf_op jit(solution)/shard_map/ppermute | solution.py:269
  51.0 3.9 %collective-permute-start.13 = (bf16[128,512]{1,0:T(8,128)(2,1)S(1)}, bf16[128,512]{1,0:T(8,128)(2,1)S(1)}, u32[]{:S(2)}, u32[]{:S(2)}) collective-permute-start(bf16[128,512]{1,0:T(8,128)(2,1)S(1)} %dynamic-slice_convert_fusion), channel_id=1, source_target_pairs={{0,1},{1,0},{2,3},{3,2},{4,5},{5,4},{6,7},{7,6},{8,9},{9,8},{10,11... | collective-permute-start | bytes 393224 | tf_op jit(solution)/shard_map/ppermute | solution.py:275

commit v3 on v2

v3 whole, which is shorter than its diff:
```python
import math

import jax
import jax.numpy as jnp
from jax import lax
from jax.experimental import pallas as pl
from jax.experimental.pallas import tpu as pltpu
from jax.sharding import PartitionSpec as P

HEAD_DIM = 128
HEADS = 16
KV_HEADS = 2
WINDOW = 4
TOK_DEV = 512
NDOCS = 64
LOCAL = 4
HALF = HEAD_DIM // 2
TILE = 256
SPAN = (WINDOW + 1) * TOK_DEV
HALVES = TOK_DEV // TILE
OWN_ROW = WINDOW * TOK_DEV
OWN_TILE = OWN_ROW // TILE
LANES = LOCAL * TILE
SCALE = HEAD_DIM ** (-0.5)
SCALE_LOG2 = SCALE * math.log2(math.e)
NEG = -1e30
STEP = 2


def contract_last(first_matrix, second_matrix):
    return lax.dot_general(
        first_matrix, second_matrix, (((1,), (1,)), ((), ())), preferred_element_type=jnp.float32
    )


def matmul(first_matrix, second_matrix):
    return jnp.dot(first_matrix, second_matrix, preferred_element_type=jnp.float32)


def tile_rows(tile, count):
    return pl.ds(pl.multiple_of(tile * TILE, TILE), count * TILE)


def by_sublane(array):
    return array.reshape(array.shape[0] // 8, 8, LANES)


def prepare_kernel(
    lengths_ref, block_ref, q_ref, grad_ref, pair_ref,
    bounds_ref, far_ref, start_ref, max_ref, q_cat, g_cat, q_t, g_t, own_scores, own_grads, own_t,
):
    first_query = block_ref[0] * TOK_DEV
    origin = first_query - WINDOW * TOK_DEV
    lane_pos = first_query + lax.broadcasted_iota(jnp.int32, (1, TOK_DEV), 1)

    def next_doc(doc, carry):
        start, is_far, lane_start, edges = carry
        end = start + lengths_ref[doc]
        reach = lax.div(end - 1, TOK_DEV) - lax.div(start, TOK_DEV)
        is_far = jnp.where((reach >= 3) & (doc != 1), 1, is_far)
        lane_start = jnp.where(lane_pos >= end, end, lane_start)
        edges = tuple(
            jnp.where(first_query + place >= end, end, edge)
            for place, edge in zip((0, TILE - 1, TILE, TOK_DEV - 1), edges)
        )
        return end, is_far, lane_start, edges

    zero = jnp.int32(0)
    _, is_far, lane_start, edges = lax.fori_loop(
        0, NDOCS, next_doc, (zero, zero, jnp.zeros((1, TOK_DEV), jnp.int32), (zero,) * 4), unroll=8
    )
    far_ref[0] = is_far
    start_ref[...] = lane_start - origin
    for half in range(HALVES):
        lowest = lax.div(edges[2 * half] - origin, TILE)
        full = lax.div(edges[2 * half + 1] - origin + TILE - 1, TILE)
        bounds_ref[2 * half] = jnp.minimum(lowest, OWN_TILE)
        bounds_ref[2 * half + 1] = jnp.minimum(full, OWN_TILE)
    for part in range(HALVES):
        own_t[part] = pair_ref[part * TILE : (part + 1) * TILE, :].T
    for half in range(HALVES):
        rows = slice(half * TILE, (half + 1) * TILE)
        lanes = slice(half * LANES, (half + 1) * LANES)
        for head in range(LOCAL):
            cols = slice(head * HEAD_DIM, (head + 1) * HEAD_DIM)
            place = slice(half * LANES + head * TILE, half * LANES + (head + 1) * TILE)
            q_cat[place, :] = q_ref[rows, cols]
            g_cat[place, :] = grad_ref[rows, cols]
            q_t[:, place] = q_ref[rows, cols].T
            g_t[:, place] = grad_ref[rows, cols].T
        start_rel = jnp.concatenate([lane_start[:, rows] - first_query] * LOCAL, axis=1)
        query_rel = jnp.concatenate([lane_pos[:, rows] - first_query] * LOCAL, axis=1)
        count = 1 + half
        own_rows = slice(half * TILE, (half + count) * TILE)
        keys = pair_ref[: count * TILE, :HEAD_DIM]
        values = pair_ref[: count * TILE, HEAD_DIM:]
        raw = matmul(keys, q_t[:, lanes])
        key_rel = lax.broadcasted_iota(jnp.int32, raw.shape, 0)
        raw = jnp.where((key_rel >= start_rel) & (key_rel <= query_rel), raw, NEG)
        own_scores[own_rows] = raw
        max_ref[half * 8 : (half + 1) * 8] = jnp.max(by_sublane(raw), axis=0)
        own_grads[own_rows] = matmul(values, g_t[:, lanes])


def attention_kernel(
    bounds_ref, start_ref, max_ref, q_cat, g_cat, q_t, g_t, own_scores, own_grads, own_t,
    pair_ref, kv2_ref, kv13_ref, kv4_ref,
    out_ref, dq_ref, t0, t1, t2, t3, t4a, t4b,
    kv_buf, kv_t, scores, grads, kv_acc, o_acc, dq_acc,
):
    kv_acc[...] = jnp.zeros_like(kv_acc)
    sources = (
        (1, kv13_ref, 0), (2, kv2_ref, 0), (3, kv13_ref, TOK_DEV), (4, kv4_ref, 0)
    )
    for distance, source, row in sources:
        place = (WINDOW - distance) * TOK_DEV

        @pl.when(bounds_ref[0] < OWN_TILE - 2 * (distance - 1))
        def _(source=source, row=row, place=place):
            kv_buf[place : place + TOK_DEV, :] = source[row : row + TOK_DEV, :]
            for part in range(HALVES):
                piece = source[row + part * TILE : row + (part + 1) * TILE, :]
                kv_t[place // TILE + part] = piece.T

    def in_steps(low, step, carry):
        middle = low + (OWN_TILE - low) // STEP * STEP
        carry = lax.fori_loop(
            0, (OWN_TILE - low) // STEP, lambda at, held: step(low + at * STEP, STEP, held), carry
        )
        return lax.fori_loop(middle, OWN_TILE, lambda at, held: step(at, 1, held), carry)

    for half in range(HALVES):
        rows = slice(half * TILE, (half + 1) * TILE)
        lanes = slice(half * LANES, (half + 1) * LANES)
        lowest = bounds_ref[2 * half]
        first_full = bounds_ref[2 * half + 1]
        count = 1 + half
        own_part = slice(half * TILE, (half + count) * TILE)
        own_rows = slice(OWN_ROW, OWN_ROW + count * TILE)

        def score_masked(tile, row_max):
            kv_rows = tile_rows(tile, 1)
            raw = matmul(kv_buf[kv_rows, :HEAD_DIM], q_t[:, lanes])
            key_rel = tile * TILE + lax.broadcasted_iota(jnp.int32, raw.shape, 0)
            start_rel = jnp.concatenate([start_ref[:, rows]] * LOCAL, axis=1)
            raw = jnp.where(key_rel >= start_rel, raw, NEG)
            scores[kv_rows] = raw
            return jnp.maximum(row_max, jnp.max(by_sublane(raw), axis=0))

        def score_full(tile, count, row_max):
            kv_rows = tile_rows(tile, count)
            raw = matmul(kv_buf[kv_rows, :HEAD_DIM], q_t[:, lanes])
            scores[kv_rows] = raw
            return jnp.maximum(row_max, jnp.max(by_sublane(raw), axis=0))

        row_max = in_steps(first_full, score_full, max_ref[half * 8 : (half + 1) * 8])
        row_max = lax.fori_loop(lowest, first_full, score_masked, row_max)
        shift = jnp.max(row_max, axis=0, keepdims=True) * SCALE_LOG2

        def add_totals(carry, weights, prob_grad):
            total, dots = carry
            total = total + jnp.sum(by_sublane(weights), axis=0)
            dots = dots + jnp.sum(by_sublane(weights * prob_grad), axis=0)
            return total, dots

        def total_tile(tile, count, carry):
            kv_rows = tile_rows(tile, count)
            prob_grad = matmul(kv_buf[kv_rows, HEAD_DIM:], g_t[:, lanes])
            weights = jnp.exp2(scores[kv_rows] * SCALE_LOG2 - shift)
            scores[kv_rows] = weights
            grads[kv_rows] = prob_grad
            return add_totals(carry, weights, prob_grad)

        nothing = jnp.zeros((8, LANES), jnp.float32)
        weights = jnp.exp2(own_scores[own_part] * SCALE_LOG2 - shift)
        scores[own_rows] = weights
        carry = add_totals((nothing, nothing), weights, own_grads[own_part])
        total, dots = in_steps(lowest, total_tile, carry)
        inverse = 1.0 / jnp.sum(total, axis=0, keepdims=True)
        grad_dot = jnp.sum(dots, axis=0, keepdims=True) * inverse

        def score_grads(weights, prob_grad):
            weights = weights * inverse
            score_grad = (weights * (prob_grad - grad_dot)).astype(jnp.bfloat16)
            return weights.astype(jnp.bfloat16), score_grad

        def transposed_products(turned, prob, score_grad):
            out_add = dq_add = None
            for part, piece in enumerate(turned):
                inner = slice(part * TILE, (part + 1) * TILE)
                out_part = matmul(piece[HEAD_DIM:], prob[inner])
                dq_part = matmul(piece[:HEAD_DIM], score_grad[inner])
                out_add = out_part if part == 0 else out_add + out_part
                dq_add = dq_part if part == 0 else dq_add + dq_part
            return out_add, dq_add

        def backward_tile(tile, count, carry):
            kv_rows = tile_rows(tile, count)
            prob, score_grad = score_grads(scores[kv_rows], grads[kv_rows])
            kv_acc[kv_rows, HEAD_DIM:] += matmul(prob, g_cat[lanes])
            kv_acc[kv_rows, :HEAD_DIM] += matmul(score_grad, q_cat[lanes])
            turned = [kv_t[tile + part] for part in range(count)]
            out_add, dq_add = transposed_products(turned, prob, score_grad)
            o_acc[...] += out_add
            dq_acc[...] += dq_add
            return carry

        prob, score_grad = score_grads(scores[own_rows], own_grads[own_part])
        kv_acc[own_rows, HEAD_DIM:] += matmul(prob, g_cat[lanes])
        kv_acc[own_rows, :HEAD_DIM] += matmul(score_grad, q_cat[lanes])
        turned = [own_t[part] for part in range(count)]
        o_acc[...], dq_acc[...] = transposed_products(turned, prob, score_grad)
        in_steps(lowest, backward_tile, 0)
        for head in range(LOCAL):
            cols = slice(head * HEAD_DIM, (head + 1) * HEAD_DIM)
            place = slice(head * TILE, (head + 1) * TILE)
            out_ref[rows, cols] = o_acc[:, place].T.astype(jnp.bfloat16)
            dq_ref[rows, cols] = (dq_acc[:, place].T * SCALE).astype(jnp.bfloat16)

    def write_term(term, row, rows):
        keys = (kv_acc[row : row + rows, :HEAD_DIM] * SCALE).T.astype(term.dtype)
        values = kv_acc[row : row + rows, HEAD_DIM:].T.astype(term.dtype)
        for half in range(2):
            part = slice(half * HALF, (half + 1) * HALF)
            term[2 * half * HALF : (2 * half + 1) * HALF, :] = keys[part]
            term[(2 * half + 1) * HALF : (2 * half + 2) * HALF, :] = values[part]

    for distance, term in enumerate((t0, t1, t2, t3)):
        write_term(term, (WINDOW - distance) * TOK_DEV, TOK_DEV)
    write_term(t4a, 0, TILE)
    write_term(t4b, TILE, TILE)


def pick_kernel(column_ref, keys_ref, values_ref, pair_ref, sems):
    column = pl.multiple_of(column_ref[0], HEAD_DIM)
    copies = []
    for place, source in enumerate((keys_ref, values_ref)):
        cols = pl.ds(place * HEAD_DIM, HEAD_DIM)
        copies.append(
            pltpu.make_async_copy(
                source.at[:, pl.ds(column, HEAD_DIM)], pair_ref.at[:, cols], sems.at[place]
            )
        )
    for copy in copies:
        copy.start()
    for copy in copies:
        copy.wait()


def pick_block(column, keys, values):
    smem = pl.BlockSpec(memory_space=pltpu.SMEM)
    vmem = pl.BlockSpec(memory_space=pltpu.VMEM)
    anywhere = pl.BlockSpec(memory_space=pltpu.HBM)
    return pl.pallas_call(
        pick_kernel,
        out_shape=jax.ShapeDtypeStruct((TOK_DEV, 2 * HEAD_DIM), jnp.bfloat16),
        in_specs=[smem, anywhere, anywhere],
        out_specs=vmem,
        scratch_shapes=[pltpu.SemaphoreType.DMA((2,))],
        compiler_params=pltpu.CompilerParams(vmem_limit_bytes=60 * 1024 * 1024),
        cost_estimate=pl.CostEstimate(flops=0, bytes_accessed=10**6, transcendentals=0),
        name="pick",
    )(column, keys, values)


def prepare(lengths, block, queries, grads, pair):
    vmem = pl.BlockSpec(memory_space=pltpu.VMEM)
    smem = pl.BlockSpec(memory_space=pltpu.SMEM)
    own = jax.ShapeDtypeStruct((3 * TILE, LANES), jnp.float32)
    rows = jax.ShapeDtypeStruct((HALVES * LANES, HEAD_DIM), jnp.bfloat16)
    cols = jax.ShapeDtypeStruct((HEAD_DIM, HALVES * LANES), jnp.bfloat16)
    return pl.pallas_call(
        prepare_kernel,
        out_shape=[
            jax.ShapeDtypeStruct((2 * HALVES,), jnp.int32),
            jax.ShapeDtypeStruct((1,), jnp.int32),
            jax.ShapeDtypeStruct((1, TOK_DEV), jnp.int32),
            jax.ShapeDtypeStruct((8 * HALVES, LANES), jnp.float32),
            rows, rows, cols, cols, own, own,
            jax.ShapeDtypeStruct((HALVES, 2 * HEAD_DIM, TILE), jnp.bfloat16),
        ],
        in_specs=[smem, smem, vmem, vmem, vmem],
        out_specs=[smem, smem] + [vmem] * 9,
        compiler_params=pltpu.CompilerParams(vmem_limit_bytes=24 * 1024 * 1024),
        cost_estimate=pl.CostEstimate(
            flops=2 * 10**9, bytes_accessed=10**6, transcendentals=0
        ),
        name="prepare",
    )(lengths, block, queries, grads, pair)


def attention_block(bounds, state, kv_blocks):
    vmem = pl.BlockSpec(memory_space=pltpu.VMEM)
    smem = pl.BlockSpec(memory_space=pltpu.SMEM)
    wide = jax.ShapeDtypeStruct((TOK_DEV, LOCAL * HEAD_DIM), jnp.bfloat16)
    own = jax.ShapeDtypeStruct((2 * HEAD_DIM, TOK_DEV), jnp.float32)
    term = jax.ShapeDtypeStruct((2 * HEAD_DIM, TOK_DEV), jnp.bfloat16)
    short = jax.ShapeDtypeStruct((2 * HEAD_DIM, TILE), jnp.bfloat16)
    return pl.pallas_call(
        attention_kernel,
        out_shape=[wide, wide, own, term, term, term, short, short],
        in_specs=[smem] + [vmem] * 13,
        out_specs=[vmem] * 8,
        scratch_shapes=[
            pltpu.VMEM((WINDOW * TOK_DEV, 2 * HEAD_DIM), jnp.bfloat16),
            pltpu.VMEM((OWN_TILE, 2 * HEAD_DIM, TILE), jnp.bfloat16),
            pltpu.VMEM((SPAN, LANES), jnp.float32),
            pltpu.VMEM((WINDOW * TOK_DEV, LANES), jnp.float32),
            pltpu.VMEM((SPAN, 2 * HEAD_DIM), jnp.float32),
            pltpu.VMEM((HEAD_DIM, LANES), jnp.float32),
            pltpu.VMEM((HEAD_DIM, LANES), jnp.float32),
        ],
        compiler_params=pltpu.CompilerParams(vmem_limit_bytes=40 * 1024 * 1024),
        cost_estimate=pl.CostEstimate(
            flops=5 * 10**9, bytes_accessed=4 * 10**6, transcendentals=6 * 10**6
        ),
        name="attention",
    )(bounds, *state, *kv_blocks)


def moved(value, pairs):
    return lax.ppermute(value, "ctx", pairs)


def from_partner(value, axis, apart):
    mask = 2**apart
    pairs = [(source, source ^ mask) for source in range(lax.axis_size(axis))]
    return lax.ppermute(value, axis, pairs)


def pairs_at(distance, count):
    return [(source, source + distance) for source in range(count - distance)]


def needed(source, target):
    return target < 5 or source >= 4


def reversed_pairs(pairs):
    return [(target, source) for source, target in pairs]


def shards(query_states, key_states, value_states, out_grad, lengths):
    count = lax.axis_size("ctx")
    block_index = lax.axis_index("ctx")
    head_index = lax.axis_index("head")
    kv_start = head_index * LOCAL // (HEADS // KV_HEADS) * HEAD_DIM
    own_half = head_index % 2
    own_pair = pick_block(kv_start.astype(jnp.int32).reshape(1), key_states, value_states)
    near = {
        distance: [pair for pair in pairs_at(distance, count) if needed(*pair)]
        for distance in (1, 2)
    }
    near[3] = [(0, 3), (1, 4)]
    near[4] = [(0, 4)]
    wide = {distance: pairs_at(distance, count)[WINDOW:] for distance in (3, 4)}
    second = moved(own_pair, pairs_at(2, count))
    fourth = moved(own_pair, [(0, 4), (1, 5)])
    bounds, far_flag, *state = prepare(
        lengths, block_index.astype(jnp.int32).reshape(1), query_states, out_grad, own_pair
    )
    is_far = far_flag[0] == 1
    second, fourth = lax.optimization_barrier((second, fourth))
    fourth = lax.cond(
        is_far,
        lambda got, pair: got + moved(pair, wide[4]),
        lambda got, pair: got,
        fourth, own_pair,
    )
    is_even = block_index % 2 == 0
    outbound = jnp.concatenate(
        [jnp.where(is_even, own_pair, second), jnp.where(is_even, second, fourth)], axis=0
    )
    swapped = moved(outbound, [(place, place ^ 1) for place in range(count)])
    attended, query_grad, t0, t1, t2, t3, t4a, t4b = attention_block(
        bounds, state, [own_pair, second, swapped, fourth]
    )
    back4 = moved(t4b, reversed_pairs(near[4]))
    back3 = moved(t3, reversed_pairs(near[3]))
    back2 = moved(t2, reversed_pairs(near[2]))
    back1 = moved(t1, reversed_pairs(near[1]))
    gathered = t0 + back3.astype(jnp.float32)
    gathered = gathered + jnp.pad(back4, ((0, 0), (TILE, 0))).astype(jnp.float32)
    gathered = lax.optimization_barrier(gathered)
    gathered = gathered + back2.astype(jnp.float32) + back1.astype(jnp.float32)

    def with_far(total, third_term, low_term, high_term):
        fourth_term = jnp.concatenate([low_term, high_term], axis=1)
        from3 = moved(third_term, reversed_pairs(wide[3]))
        from4 = moved(fourth_term, reversed_pairs(wide[4]))
        return total + from3.astype(jnp.float32) + from4.astype(jnp.float32)

    gathered = lax.cond(
        is_far, with_far, lambda total, *others: total, gathered, t3, t4a, t4b
    )
    outgoing = lax.dynamic_slice_in_dim(gathered, (1 - own_half) * HEAD_DIM, HEAD_DIM, 0)
    received = from_partner(outgoing.astype(jnp.bfloat16), "head", 0).astype(jnp.float32)
    kept = lax.dynamic_slice_in_dim(gathered, own_half * HEAD_DIM, HEAD_DIM, 0)
    both = (kept + received).astype(jnp.bfloat16)
    return attended, query_grad, both[:HALF].T, both[HALF:].T


def solution(mesh):
    return jax.shard_map(
        shards,
        mesh=mesh,
        in_specs=(P("ctx", "head"), P("ctx", None), P("ctx", None), P("ctx", "head"), P()),
        out_specs=(P("ctx", "head"), P("ctx", "head"), P("ctx", "head"), P("ctx", "head")),
        check_vma=False,
    )
```

time: 55.9 us -> 57.7 us (1.032)
  local copies, waits for them, and re-layouts: 2.27 us -> 11.5 us
  waiting for transfers between devices: 19.7 us -> 16.1 us
  starting transfers between devices: 19.6 us -> 16.2 us
  other arithmetic: 1.29 us -> 0.44 us
    unnamed x8 -> x22, local copies, waits for them, and re-layouts: 1.45 us -> 10.8 us
    ppermute x9 -> x7, waiting for transfers between devices: 17.2 us -> 13.5 us  [moved(): return lax.ppermute(value, 'ctx', pairs)]
    ppermute x9 -> x7, starting transfers between devices: 18.2 us -> 14.8 us  [moved(): return lax.ppermute(value, 'ctx', pairs)]
    pallas_call x1 -> x2, Pallas kernels: 1.78 us -> 3.84 us  [the longest x1 2.86 us: prepare(): pl.pallas_call(prepare_kernel, out_shape=[jax.ShapeDtypeStruct((2 * HALVE...]
    pallas_call x1, Pallas kernels: 9.46 us -> 7.71 us  [attention_block(): pl.pallas_call(attention_kernel, out_shape=[wide, wide, own, term, term,...]
    reduce_or x1 -> x0, other arithmetic: 0.66 us -> none  [any_far(): return jnp.any((blocks_back >= 3) & (jnp.arange(NDOCS) != 1))]
  transfers between devices with their start and end apart: 10 -> 8, of which waited for: 4 -> 4; matrix products, arithmetic and copies ran while one was open for 2% -> 0% of each run, Pallas kernels for 0% -> 5%
where the time goes in v3:
time: 57.7 us; the launch traced here: 57.2 us
  starting transfers between devices  16.2 us (28%)
  waiting for transfers between devices  16.1 us (28%)
  Pallas kernels  11.5 us (20%)
  local copies, waits for them, and re-layouts  11.5 us (20%)
  between operations  1.52 us (3%)
    ppermute x7, starting transfers between devices, moved(): return lax.ppermute(value, 'ctx', pairs)  14.8 us
    ppermute x7, waiting for transfers between devices, moved(): return lax.ppermute(value, 'ctx', pairs)  13.5 us
    unnamed x22, local copies, waits for them, and re-layouts  10.8 us
    pallas_call x1, Pallas kernels, attention_block(): pl.pallas_call(attention_kernel, out_shape=[wide, wide, own, term, term,...  7.71 us
    pallas_call x1, Pallas kernels, prepare(): pl.pallas_call(prepare_kernel, out_shape=[jax.ShapeDtypeStruct((2 * HALVE...  2.86 us
    ppermute x1, waiting for transfers between devices, from_partner(): return lax.ppermute(value, axis, pairs)  2.54 us
    ppermute x1, starting transfers between devices, from_partner(): return lax.ppermute(value, axis, pairs)  1.37 us
  transfers between devices with their start and end apart: 8, of which 4 were waited for; matrix products, arithmetic and copies ran while one was open for 0% of the time, Pallas kernels for 5%

profile of v3, /device:TPU:1, one launch (start us, length us, event | category | flops | bytes accessed | tf_op | source)
XLA Modules:
  0.0 57.2 jit_solution(15735820811492328848)
XLA Ops:
  0.6 1.0 %pick.1.pair_ref = bf16[512,256]{1,0:T(8,128)(2,1)S(1)} custom-call(s32[1]{0:T(128)} %bitcast.1.column_ref, bf16[512,256]{1,0:T(8,128)(2,1)} %keys_ref.1, bf16[512,256]{1,0:T(8,128)(2,1)} %values_ref.1), custom_call_target="tpu_custom_call" | custom-call | bytes 1000000 | tf_op jit(solution)/shard_map/pick/pallas_call | solution.py:254
  1.6 0.0 copy-start.10
  1.7 4.0 %collective-permute-start.3 = (bf16[512,256]{1,0:T(8,128)(2,1)S(1)}, bf16[512,256]{1,0:T(8,128)(2,1)S(1)}, u32[]{:S(2)}, u32[]{:S(2)}) collective-permute-start(bf16[512,256]{1,0:T(8,128)(2,1)S(1)} %pick.1.pair_ref), channel_id=1, source_target_pairs={{0,8},{4,12},{8,16},{12,20},{16,24},{20,28},{24,32},{28,36},{32,40... | collective-permute-start | bytes 786440 | tf_op jit(solution)/shard_map/ppermute | solution.py:322
  5.6 4.4 %collective-permute-start.4 = (bf16[512,256]{1,0:T(8,128)(2,1)S(1)}, bf16[512,256]{1,0:T(8,128)(2,1)S(1)}, u32[]{:S(2)}, u32[]{:S(2)}) collective-permute-start(bf16[512,256]{1,0:T(8,128)(2,1)S(1)} %pick.1.pair_ref), channel_id=1, source_target_pairs={{0,16},{4,20},{1,17},{5,21},{2,18},{6,22},{3,19},{7,23}} | collective-permute-start | bytes 786440 | tf_op jit(solution)/shard_map/ppermute | solution.py:322
  10.0 0.0 copy-start
  10.0 1.0 %copy-done = bf16[512,512]{1,0:T(8,128)(2,1)S(1)} copy-done((bf16[512,512]{1,0:T(8,128)(2,1)S(1)}, bf16[512,512]{1,0:T(8,128)(2,1)}, u32[]{:S(2)}) %copy-start) | copy-done | bytes 524312
  11.0 0.0 copy-start.1
  11.0 1.0 %copy-done.1 = bf16[512,512]{1,0:T(8,128)(2,1)S(1)} copy-done((bf16[512,512]{1,0:T(8,128)(2,1)S(1)}, bf16[512,512]{1,0:T(8,128)(2,1)}, u32[]{:S(2)}) %copy-start.1) | copy-done | bytes 524312
  12.1 0.0 copy-start.2
  12.1 0.7 %copy-done.2 = s32[64]{0:T(128)S(1)} copy-done((s32[64]{0:T(128)S(1)}, s32[64]{0:T(128)}, u32[]{:S(2)}) %copy-start.2) | copy-done | bytes 280
  12.7 2.9 %prepare.1 = (s32[4]{0:T(128)S(1)}, s32[1]{0:T(128)}, s32[1,512]{1,0:T(1,128)S(1)}, f32[16,1024]{1,0:T(8,128)S(1)}, bf16[2048,128]{1,0:T(8,128)(2,1)S(1)}, /*ind...) custom-call(s32[64]{0:T(128)S(1)} %copy-done.2, ...), custom_call_target="tpu_custom_call" | custom-call | flops 2000000000 | bytes 1000000 | tf_op jit(solution)/shard_map/prepare/pallas_call | solution.py:272
  15.6 0.0 copy-start.3
  15.6 1.6 %copy-done.3 = f32[768,1024]{1,0:T(8,128)} copy-done((f32[768,1024]{1,0:T(8,128)}, f32[768,1024]{1,0:T(8,128)S(1)}, u32[]{:S(2)}) %copy-start.3) | copy-done | bytes 3145752
  17.2 0.0 copy-start.5
  17.2 1.7 %copy-done.5 = f32[768,1024]{1,0:T(8,128)} copy-done((f32[768,1024]{1,0:T(8,128)}, f32[768,1024]{1,0:T(8,128)S(1)}, u32[]{:S(2)}) %copy-start.5) | copy-done | bytes 3145752
  18.9 0.0 copy-start.7
  19.6 0.0 collective-permute-done.3.kv2_ref
  19.6 0.0 collective-permute-done.4
  19.6 0.0 copy-start.9
  19.6 0.0 copy-done.10
  19.6 0.1 broadcast_select_fusion.1
  19.7 1.3 %collective-permute-start.5 = (bf16[1024,256]{1,0:T(8,128)(2,1)S(1)}, bf16[1024,256]{1,0:T(8,128)(2,1)S(1)}, u32[]{:S(2)}, u32[]{:S(2)}) collective-permute-start(bf16[1024,256]{1,0:T(8,128)(2,1)S(1)} %pad_maximum_fusion.1), channel_id=1, source_target_pairs={{0,4},{4,0},{8,12},{12,8},{16,20},{20,16},{24,28},{28,24},{32,36},... | collective-permute-start | bytes 1572872 | tf_op jit(solution)/shard_map/ppermute | solution.py:322
  21.0 1.5 %collective-permute-done.5.kv13_ref = bf16[1024,256]{1,0:T(8,128)(2,1)S(1)} collective-permute-done((bf16[1024,256]{1,0:T(8,128)(2,1)S(1)}, bf16[1024,256]{1,0:T(8,128)(2,1)S(1)}, u32[]{:S(2)}, u32[]{:S(2)}) %collective-permute-start.5) | collective-permute-done | bytes 524320 | tf_op jit(solution)/shard_map/ppermute | solution.py:322
  22.6 0.0 copy-done.7
  22.6 0.0 copy-done.9
  22.6 0.0 copy-start.4
  22.6 1.9 %copy-done.4 = f32[768,1024]{1,0:T(8,128)S(1)} copy-done((f32[768,1024]{1,0:T(8,128)S(1)}, f32[768,1024]{1,0:T(8,128)}, u32[]{:S(2)}) %copy-start.4) | copy-done | bytes 3145752
  24.5 0.0 copy-start.6
  24.5 1.9 %copy-done.6 = f32[768,1024]{1,0:T(8,128)S(1)} copy-done((f32[768,1024]{1,0:T(8,128)S(1)}, f32[768,1024]{1,0:T(8,128)}, u32[]{:S(2)}) %copy-start.6) | copy-done | bytes 3145752
  26.4 0.0 copy-start.8
  26.4 0.9 %copy-done.8 = bf16[2,256,256]{2,1,0:T(8,128)(2,1)S(1)} copy-done((bf16[2,256,256]{2,1,0:T(8,128)(2,1)S(1)}, bf16[2,256,256]{2,1,0:T(8,128)(2,1)}, u32[]{:S(2)}) %copy-start.8) | copy-done | bytes 262168
  27.3 7.7 %attention.1 = (bf16[512,512]{1,0:T(8,128)(2,1)}, bf16[512,512]{1,0:T(8,128)(2,1)}, f32[256,512]{1,0:T(8,128)S(1)}, bf16[256,512]{1,0:T(8,128)(2,1)S(1)}, bf16[2...) custom-call(s32[4]{0:T(128)S(1)} %get-tuple-element.51.bounds_ref, ...), custom_call_target="tpu_custom_call" | custom-call | flops 5000000000 | bytes 4000000 | tf_op jit(solution)/shard_map/attention/pallas_call | solution.py:299
  35.0 1.3 %collective-permute-start.6 = (bf16[256,512]{1,0:T(8,128)(2,1)}, bf16[256,512]{1,0:T(8,128)(2,1)S(1)}, u32[]{:S(2)}, u32[]{:S(2)}) collective-permute-start(bf16[256,512]{1,0:T(8,128)(2,1)} %get-tuple-element.67), channel_id=1, source_target_pairs={{12,0},{16,4},{13,1},{17,5},{14,2},{18,6},{15,3},{19,7}} | collective-permute-start | bytes 786440 | tf_op jit(solution)/shard_map/ppermute | solution.py:322
  36.3 0.7 %collective-permute-start.7 = (bf16[256,256]{1,0:T(8,128)(2,1)}, bf16[256,256]{1,0:T(8,128)(2,1)S(1)}, u32[]{:S(2)}, u32[]{:S(2)}) collective-permute-start(bf16[256,256]{1,0:T(8,128)(2,1)} %get-tuple-element.68), channel_id=1, source_target_pairs={{16,0},{17,1},{18,2},{19,3}} | collective-permute-start | bytes 393224 | tf_op jit(solution)/shard_map/ppermute | solution.py:322
  37.0 1.3 %collective-permute-start.8 = (bf16[256,512]{1,0:T(8,128)(2,1)S(1)}, bf16[256,512]{1,0:T(8,128)(2,1)S(1)}, u32[]{:S(2)}, u32[]{:S(2)}) collective-permute-start(bf16[256,512]{1,0:T(8,128)(2,1)S(1)} %get-tuple-element.69), channel_id=1, source_target_pairs={{8,0},{12,4},{16,8},{24,16},{28,20},{32,24},{36,28},{40,32},{44,36... | collective-permute-start | bytes 786440 | tf_op jit(solution)/shard_map/ppermute | solution.py:322
  38.3 1.9 %collective-permute-start.9 = (bf16[256,512]{1,0:T(8,128)(2,1)S(1)}, bf16[256,512]{1,0:T(8,128)(2,1)S(1)}, u32[]{:S(2)}, u32[]{:S(2)}) collective-permute-start(bf16[256,512]{1,0:T(8,128)(2,1)S(1)} %get-tuple-element.70), channel_id=1, source_target_pairs={{4,0},{8,4},{12,8},{16,12},{20,16},{24,20},{28,24},{32,28},{36,32}... | collective-permute-start | bytes 786440 | tf_op jit(solution)/shard_map/ppermute | solution.py:322
  40.2 0.0 collective-permute-done.7
  40.3 6.3 %collective-permute-done.6 = bf16[256,512]{1,0:T(8,128)(2,1)S(1)} collective-permute-done((bf16[256,512]{1,0:T(8,128)(2,1)}, bf16[256,512]{1,0:T(8,128)(2,1)S(1)}, u32[]{:S(2)}, u32[]{:S(2)}) %collective-permute-start.6) | collective-permute-done | bytes 262176 | tf_op jit(solution)/shard_map/ppermute | solution.py:322
  46.5 0.1 convert_add_fusion.2
  46.6 5.7 %collective-permute-done.8 = bf16[256,512]{1,0:T(8,128)(2,1)S(1)} collective-permute-done((bf16[256,512]{1,0:T(8,128)(2,1)S(1)}, bf16[256,512]{1,0:T(8,128)(2,1)S(1)}, u32[]{:S(2)}, u32[]{:S(2)}) %collective-permute-start.8) | collective-permute-done | bytes 262176 | tf_op jit(solution)/shard_map/ppermute | solution.py:322
  52.3 0.0 collective-permute-done.9
  52.4 0.2 convert_add_fusion.1
  52.6 1.4 %collective-permute-start.10 = (bf16[128,512]{1,0:T(8,128)(2,1)S(1)}, bf16[128,512]{1,0:T(8,128)(2,1)S(1)}, u32[]{:S(2)}, u32[]{:S(2)}) collective-permute-start(bf16[128,512]{1,0:T(8,128)(2,1)S(1)} %dynamic-slice_convert_fusion), channel_id=1, source_target_pairs={{0,1},{1,0},{2,3},{3,2},{4,5},{5,4},{6,7},{7,6},{8,9},{9,8},{10,11... | collective-permute-start | bytes 393224 | tf_op jit(solution)/shard_map/ppermute | solution.py:328
  54.0 2.5 %collective-permute-done.10 = bf16[128,512]{1,0:T(8,128)(2,1)S(1)} collective-permute-done((bf16[128,512]{1,0:T(8,128)(2,1)S(1)}, bf16[128,512]{1,0:T(8,128)(2,1)S(1)}, u32[]{:S(2)}, u32[]{:S(2)}) %collective-permute-start.10) | collective-permute-done | bytes 131104 | tf_op jit(solution)/shard_map/ppermute | solution.py:328
  56.6 0.7 %slice_bitcast_fusion = (bf16[512,64]{0,1:T(8,128)(2,1)}, bf16[512,64]{0,1:T(8,128)(2,1)}) fusion(bf16[128,512]{1,0:T(8,128)(2,1)S(1)} %add_convert_fusion), kind=kLoop, calls=%fused_computation.9 | loop fusion | bytes 262144 | tf_op jit(solution)/shard_map/transpose | solution.py:400
  (5 shorter events, 0.1 us)
Async XLA Ops:
  1.6 18.0 %copy-start.10 = (bf16[512,256]{1,0:T(8,128)(2,1)}, bf16[512,256]{1,0:T(8,128)(2,1)S(1)}, u32[]{:S(2)}) copy-start(bf16[512,256]{1,0:T(8,128)(2,1)S(1)} %pick.1.pair_ref) | copy-start | bytes 786436
  1.7 17.9 %collective-permute-start.3 = (bf16[512,256]{1,0:T(8,128)(2,1)S(1)}, bf16[512,256]{1,0:T(8,128)(2,1)S(1)}, u32[]{:S(2)}, u32[]{:S(2)}) collective-permute-start(bf16[512,256]{1,0:T(8,128)(2,1)S(1)} %pick.1.pair_ref), channel_id=1, source_target_pairs={{0,8},{4,12},{8,16},{12,20},{16,24},{20,28},{24,32},{28,36},{32,40... | collective-permute-start | bytes 786440 | tf_op jit(solution)/shard_map/ppermute | solution.py:322
  5.6 14.0 %collective-permute-start.4 = (bf16[512,256]{1,0:T(8,128)(2,1)S(1)}, bf16[512,256]{1,0:T(8,128)(2,1)S(1)}, u32[]{:S(2)}, u32[]{:S(2)}) collective-permute-start(bf16[512,256]{1,0:T(8,128)(2,1)S(1)} %pick.1.pair_ref), channel_id=1, source_target_pairs={{0,16},{4,20},{1,17},{5,21},{2,18},{6,22},{3,19},{7,23}} | collective-permute-start | bytes 786440 | tf_op jit(solution)/shard_map/ppermute | solution.py:322
  10.0 1.0 %copy-start = (bf16[512,512]{1,0:T(8,128)(2,1)S(1)}, bf16[512,512]{1,0:T(8,128)(2,1)}, u32[]{:S(2)}) copy-start(bf16[512,512]{1,0:T(8,128)(2,1)} %q_ref.1) | copy-start | bytes 1572868
  11.0 1.0 %copy-start.1 = (bf16[512,512]{1,0:T(8,128)(2,1)S(1)}, bf16[512,512]{1,0:T(8,128)(2,1)}, u32[]{:S(2)}) copy-start(bf16[512,512]{1,0:T(8,128)(2,1)} %grad_ref.1) | copy-start | bytes 1572868
  12.1 0.7 %copy-start.2 = (s32[64]{0:T(128)S(1)}, s32[64]{0:T(128)}, u32[]{:S(2)}) copy-start(s32[64]{0:T(128)} %lengths_ref.1) | copy-start | bytes 772
  15.6 1.6 %copy-start.3 = (f32[768,1024]{1,0:T(8,128)}, f32[768,1024]{1,0:T(8,128)S(1)}, u32[]{:S(2)}) copy-start(f32[768,1024]{1,0:T(8,128)S(1)} %get-tuple-element.58.own_scores) | copy-start | bytes 9437188
  17.2 1.7 %copy-start.5 = (f32[768,1024]{1,0:T(8,128)}, f32[768,1024]{1,0:T(8,128)S(1)}, u32[]{:S(2)}) copy-start(f32[768,1024]{1,0:T(8,128)S(1)} %get-tuple-element.59.own_grads) | copy-start | bytes 9437188
  18.9 3.7 %copy-start.7 = (bf16[2,256,256]{2,1,0:T(8,128)(2,1)}, bf16[2,256,256]{2,1,0:T(8,128)(2,1)S(1)}, u32[]{:S(2)}) copy-start(bf16[2,256,256]{2,1,0:T(8,128)(2,1)S(1)} %get-tuple-element.60.own_t) | copy-start | bytes 786436
  19.6 3.0 %copy-start.9 = (bf16[512,256]{1,0:T(8,128)(2,1)}, bf16[512,256]{1,0:T(8,128)(2,1)S(1)}, u32[]{:S(2)}) copy-start(bf16[512,256]{1,0:T(8,128)(2,1)S(1)} %get-tuple-element.76.kv4_ref) | copy-start | bytes 786436
  19.7 2.8 %collective-permute-start.5 = (bf16[1024,256]{1,0:T(8,128)(2,1)S(1)}, bf16[1024,256]{1,0:T(8,128)(2,1)S(1)}, u32[]{:S(2)}, u32[]{:S(2)}) collective-permute-start(bf16[1024,256]{1,0:T(8,128)(2,1)S(1)} %pad_maximum_fusion.1), channel_id=1, source_target_pairs={{0,4},{4,0},{8,12},{12,8},{16,20},{20,16},{24,28},{28,24},{32,36},... | collective-permute-start | bytes 1572872 | tf_op jit(solution)/shard_map/ppermute | solution.py:322
  22.6 1.9 %copy-start.4 = (f32[768,1024]{1,0:T(8,128)S(1)}, f32[768,1024]{1,0:T(8,128)}, u32[]{:S(2)}) copy-start(f32[768,1024]{1,0:T(8,128)} %copy-done.3) | copy-start | bytes 9437188
  24.5 1.9 %copy-start.6 = (f32[768,1024]{1,0:T(8,128)S(1)}, f32[768,1024]{1,0:T(8,128)}, u32[]{:S(2)}) copy-start(f32[768,1024]{1,0:T(8,128)} %copy-done.5) | copy-start | bytes 9437188
  26.4 0.9 %copy-start.8 = (bf16[2,256,256]{2,1,0:T(8,128)(2,1)S(1)}, bf16[2,256,256]{2,1,0:T(8,128)(2,1)}, u32[]{:S(2)}) copy-start(bf16[2,256,256]{2,1,0:T(8,128)(2,1)} %copy-done.7) | copy-start | bytes 786436
  35.0 11.5 %collective-permute-start.6 = (bf16[256,512]{1,0:T(8,128)(2,1)}, bf16[256,512]{1,0:T(8,128)(2,1)S(1)}, u32[]{:S(2)}, u32[]{:S(2)}) collective-permute-start(bf16[256,512]{1,0:T(8,128)(2,1)} %get-tuple-element.67), channel_id=1, source_target_pairs={{12,0},{16,4},{13,1},{17,5},{14,2},{18,6},{15,3},{19,7}} | collective-permute-start | bytes 786440 | tf_op jit(solution)/shard_map/ppermute | solution.py:322
  36.3 3.9 %collective-permute-start.7 = (bf16[256,256]{1,0:T(8,128)(2,1)}, bf16[256,256]{1,0:T(8,128)(2,1)S(1)}, u32[]{:S(2)}, u32[]{:S(2)}) collective-permute-start(bf16[256,256]{1,0:T(8,128)(2,1)} %get-tuple-element.68), channel_id=1, source_target_pairs={{16,0},{17,1},{18,2},{19,3}} | collective-permute-start | bytes 393224 | tf_op jit(solution)/shard_map/ppermute | solution.py:322
  37.0 15.4 %collective-permute-start.8 = (bf16[256,512]{1,0:T(8,128)(2,1)S(1)}, bf16[256,512]{1,0:T(8,128)(2,1)S(1)}, u32[]{:S(2)}, u32[]{:S(2)}) collective-permute-start(bf16[256,512]{1,0:T(8,128)(2,1)S(1)} %get-tuple-element.69), channel_id=1, source_target_pairs={{8,0},{12,4},{16,8},{24,16},{28,20},{32,24},{36,28},{40,32},{44,36... | collective-permute-start | bytes 786440 | tf_op jit(solution)/shard_map/ppermute | solution.py:322
  38.3 14.1 %collective-permute-start.9 = (bf16[256,512]{1,0:T(8,128)(2,1)S(1)}, bf16[256,512]{1,0:T(8,128)(2,1)S(1)}, u32[]{:S(2)}, u32[]{:S(2)}) collective-permute-start(bf16[256,512]{1,0:T(8,128)(2,1)S(1)} %get-tuple-element.70), channel_id=1, source_target_pairs={{4,0},{8,4},{12,8},{16,12},{20,16},{24,20},{28,24},{32,28},{36,32}... | collective-permute-start | bytes 786440 | tf_op jit(solution)/shard_map/ppermute | solution.py:322
  52.6 3.9 %collective-permute-start.10 = (bf16[128,512]{1,0:T(8,128)(2,1)S(1)}, bf16[128,512]{1,0:T(8,128)(2,1)S(1)}, u32[]{:S(2)}, u32[]{:S(2)}) collective-permute-start(bf16[128,512]{1,0:T(8,128)(2,1)S(1)} %dynamic-slice_convert_fusion), channel_id=1, source_target_pairs={{0,1},{1,0},{2,3},{3,2},{4,5},{5,4},{6,7},{7,6},{8,9},{9,8},{10,11... | collective-permute-start | bytes 393224 | tf_op jit(solution)/shard_map/ppermute | solution.py:328

commit v4 on v3

--- a/solution.py
+++ b/solution.py
@@ -47,29 +47,26 @@
 
 def prepare_kernel(
     lengths_ref, block_ref, q_ref, grad_ref, pair_ref,
-    bounds_ref, far_ref, start_ref, max_ref, q_cat, g_cat, q_t, g_t, own_scores, own_grads, own_t,
+    bounds_ref, start_ref, max_ref, q_cat, g_cat, q_t, g_t, own_scores, own_grads, own_t,
 ):
     first_query = block_ref[0] * TOK_DEV
     origin = first_query - WINDOW * TOK_DEV
     lane_pos = first_query + lax.broadcasted_iota(jnp.int32, (1, TOK_DEV), 1)
 
     def next_doc(doc, carry):
-        start, is_far, lane_start, edges = carry
-        end = start + lengths_ref[doc]
-        reach = lax.div(end - 1, TOK_DEV) - lax.div(start, TOK_DEV)
-        is_far = jnp.where((reach >= 3) & (doc != 1), 1, is_far)
+        end, lane_start, edges = carry
+        end = end + lengths_ref[doc]
         lane_start = jnp.where(lane_pos >= end, end, lane_start)
         edges = tuple(
             jnp.where(first_query + place >= end, end, edge)
             for place, edge in zip((0, TILE - 1, TILE, TOK_DEV - 1), edges)
         )
-        return end, is_far, lane_start, edges
+        return end, lane_start, edges
 
     zero = jnp.int32(0)
-    _, is_far, lane_start, edges = lax.fori_loop(
-        0, NDOCS, next_doc, (zero, zero, jnp.zeros((1, TOK_DEV), jnp.int32), (zero,) * 4), unroll=8
-    )
-    far_ref[0] = is_far
+    _, lane_start, edges = lax.fori_loop(
+        0, NDOCS, next_doc, (zero, jnp.zeros((1, TOK_DEV), jnp.int32), (zero,) * 4), unroll=8
+    )
     start_ref[...] = lane_start - origin
     for half in range(HALVES):
         lowest = lax.div(edges[2 * half] - origin, TILE)
@@ -273,14 +270,13 @@
         prepare_kernel,
         out_shape=[
             jax.ShapeDtypeStruct((2 * HALVES,), jnp.int32),
-            jax.ShapeDtypeStruct((1,), jnp.int32),
             jax.ShapeDtypeStruct((1, TOK_DEV), jnp.int32),
             jax.ShapeDtypeStruct((8 * HALVES, LANES), jnp.float32),
             rows, rows, cols, cols, own, own,
             jax.ShapeDtypeStruct((HALVES, 2 * HEAD_DIM, TILE), jnp.bfloat16),
         ],
         in_specs=[smem, smem, vmem, vmem, vmem],
-        out_specs=[smem, smem] + [vmem] * 9,
+        out_specs=[smem] + [vmem] * 9,
         compiler_params=pltpu.CompilerParams(vmem_limit_bytes=24 * 1024 * 1024),
         cost_estimate=pl.CostEstimate(
             flops=2 * 10**9, bytes_accessed=10**6, transcendentals=0
@@ -340,6 +336,13 @@
     return [(target, source) for source, target in pairs]
 
 
+def any_far(lengths):
+    ends = jnp.cumsum(lengths)
+    starts = ends - lengths
+    blocks_back = (ends - 1) // TOK_DEV - starts // TOK_DEV
+    return jnp.any((blocks_back >= 3) & (jnp.arange(NDOCS) != 1))
+
+
 def shards(query_states, key_states, value_states, out_grad, lengths):
     count = lax.axis_size("ctx")
     block_index = lax.axis_index("ctx")
@@ -356,17 +359,19 @@
     wide = {distance: pairs_at(distance, count)[WINDOW:] for distance in (3, 4)}
     second = moved(own_pair, pairs_at(2, count))
     fourth = moved(own_pair, [(0, 4), (1, 5)])
-    bounds, far_flag, *state = prepare(
+    is_far = any_far(lengths)
+    far_fourth = lax.cond(
+        is_far,
+        lambda pair: moved(pair, wide[4]),
+        lambda pair: jnp.zeros_like(pair),
+        own_pair,
+    )
+    own_pair, far_fourth = lax.optimization_barrier((own_pair, far_fourth))
+    bounds, *state = prepare(
         lengths, block_index.astype(jnp.int32).reshape(1), query_states, out_grad, own_pair
     )
-    is_far = far_flag[0] == 1
-    second, fourth = lax.optimization_barrier((second, fourth))
-    fourth = lax.cond(
-        is_far,
-        lambda got, pair: got + moved(pair, wide[4]),
-        lambda got, pair: got,
-        fourth, own_pair,
-    )
+    second, fourth, bounds = lax.optimization_barrier((second, fourth, bounds))
+    fourth = fourth + far_fourth
     is_even = block_index % 2 == 0
     outbound = jnp.concatenate(
         [jnp.where(is_even, own_pair, second), jnp.where(is_even, second, fourth)], axis=0

time: 57.7 us -> 52.9 us (0.917)
  local copies, waits for them, and re-layouts: 11.5 us -> 4.9 us
  other arithmetic: 0.44 us -> 2.91 us
  Pallas kernels: 11.5 us -> 10.9 us
    unnamed x22 -> x6, local copies, waits for them, and re-layouts: 10.8 us -> 2.74 us
    another operation x0 -> x2, local copies, waits for them, and re-layouts: none -> 1.47 us
    reduce_or x0 -> x1, other arithmetic: none -> 1.31 us  [any_far(): return jnp.any((blocks_back >= 3) & (jnp.arange(NDOCS) != 1))]
    select_n x1, other arithmetic: 0.06 us -> 1.02 us  [shards(): jnp.where(is_even, second, fourth)]
  transfers between devices with their start and end apart: 8 -> 8, of which waited for: 4 -> 4; matrix products, arithmetic and copies ran while one was open for 0% -> 6% of each run, Pallas kernels for 5% -> 5%
where the time goes in v4:
time: 52.9 us; the launch traced here: 52.5 us
  starting transfers between devices  16.2 us (31%)
  waiting for transfers between devices  16.1 us (30%)
  Pallas kernels  10.9 us (21%)
  local copies, waits for them, and re-layouts  4.9 us (9%)
  other arithmetic  2.91 us (6%)
  between operations  1.47 us (3%)
    ppermute x7, starting transfers between devices, moved(): return lax.ppermute(value, 'ctx', pairs)  14.8 us
    ppermute x7, waiting for transfers between devices, moved(): return lax.ppermute(value, 'ctx', pairs)  13.6 us
    pallas_call x1, Pallas kernels, attention_block(): pl.pallas_call(attention_kernel, out_shape=[wide, wide, own, term, term,...  7.34 us
    unnamed x6, local copies, waits for them, and re-layouts  2.74 us
    pallas_call x1, Pallas kernels, prepare(): pl.pallas_call(prepare_kernel, out_shape=[jax.ShapeDtypeStruct((2 * HALVE...  2.58 us
    ppermute x1, waiting for transfers between devices, from_partner(): return lax.ppermute(value, axis, pairs)  2.53 us
    another operation x2, local copies, waits for them, and re-layouts  1.47 us
    ppermute x1, starting transfers between devices, from_partner(): return lax.ppermute(value, axis, pairs)  1.38 us
  transfers between devices with their start and end apart: 8, of which 4 were waited for; matrix products, arithmetic and copies ran while one was open for 6% of the time, Pallas kernels for 5%

profile of v4, /device:TPU:1, one launch (start us, length us, event | category | flops | bytes accessed | tf_op | source)
XLA Modules:
  0.0 52.5 jit_solution(10743985673871153370)
XLA Ops:
  0.6 1.0 %pick.1.pair_ref = bf16[512,256]{1,0:T(8,128)(2,1)S(1)} custom-call(s32[1]{0:T(128)} %bitcast.column_ref, bf16[512,256]{1,0:T(8,128)(2,1)} %keys_ref.1, bf16[512,256]{1,0:T(8,128)(2,1)} %values_ref.1), custom_call_target="tpu_custom_call" | custom-call | bytes 1000000 | tf_op jit(solution)/shard_map/pick/pallas_call | solution.py:251
  1.6 4.0 %collective-permute-start.3 = (bf16[512,256]{1,0:T(8,128)(2,1)S(1)}, bf16[512,256]{1,0:T(8,128)(2,1)S(1)}, u32[]{:S(2)}, u32[]{:S(2)}) collective-permute-start(bf16[512,256]{1,0:T(8,128)(2,1)S(1)} %pick.1.pair_ref), channel_id=1, source_target_pairs={{0,8},{4,12},{8,16},{12,20},{16,24},{20,28},{24,32},{28,36},{32,40... | collective-permute-start | bytes 786440 | tf_op jit(solution)/shard_map/ppermute | solution.py:318
  5.6 4.4 %collective-permute-start.4 = (bf16[512,256]{1,0:T(8,128)(2,1)S(1)}, bf16[512,256]{1,0:T(8,128)(2,1)S(1)}, u32[]{:S(2)}, u32[]{:S(2)}) collective-permute-start(bf16[512,256]{1,0:T(8,128)(2,1)S(1)} %pick.1.pair_ref), channel_id=1, source_target_pairs={{0,16},{4,20},{1,17},{5,21},{2,18},{6,22},{3,19},{7,23}} | collective-permute-start | bytes 786440 | tf_op jit(solution)/shard_map/ppermute | solution.py:318
  10.0 0.7 %copy.10 = s32[64,1]{1,0:T(8,128)S(1)} copy(s32[64,1]{0,1:T(1,128)} %bitcast.7) | data formatting | bytes 512 | tf_op jit(solution)/shard_map/reshape.24
  10.7 0.1 reduce-window.9
  10.8 0.1 reduce
  10.9 1.3 %and_reduce_fusion = pred[]{:T(512)} fusion(s32[64]{0:T(128)S(1)} %reduce, s32[64]{0:T(128)} %lengths_ref.1), kind=kLoop, calls=%fused_computation.11 | loop fusion | flops 2367 | bytes 513 | tf_op jit(solution)/shard_map/reduce_or | solution.py:343
  12.9 0.7 %conditional.2 = (bf16[512,256]{1,0:T(8,128)(2,1)}) conditional(s32[]{:T(128)} %convert_element_type.33, () %tuple.22, bf16[512,256]{1,0:T(8,128)(2,1)S(1)} %pick.1.pair_ref), branch_computations={%region_2.3_spmd, %region_3.4_spmd} | conditional | bytes 1048624 | solution.py:363
  12.9 0.7 %broadcast.19 = bf16[512,256]{1,0:T(8,128)(2,1)} broadcast(bf16[]{:T(256)} %constant.63.clone), dimensions={} | broadcast | bytes 262146 | tf_op jit(solution)/shard_map/broadcast.2
  13.6 0.0 copy-start
  13.6 0.7 %copy-done = s32[64]{0:T(128)S(1)} copy-done((s32[64]{0:T(128)S(1)}, s32[64]{0:T(128)}, u32[]{:S(2)}) %copy-start) | copy-done | bytes 280
  14.3 0.0 copy-start.1
  14.3 1.0 %copy-done.1 = bf16[512,512]{1,0:T(8,128)(2,1)S(1)} copy-done((bf16[512,512]{1,0:T(8,128)(2,1)S(1)}, bf16[512,512]{1,0:T(8,128)(2,1)}, u32[]{:S(2)}) %copy-start.1) | copy-done | bytes 524312
  15.3 0.0 copy-start.2
  15.3 1.0 %copy-done.2 = bf16[512,512]{1,0:T(8,128)(2,1)S(1)} copy-done((bf16[512,512]{1,0:T(8,128)(2,1)S(1)}, bf16[512,512]{1,0:T(8,128)(2,1)}, u32[]{:S(2)}) %copy-start.2) | copy-done | bytes 524312
  16.4 2.6 %prepare.1 = (s32[4]{0:T(128)S(1)}, s32[1,512]{1,0:T(1,128)S(1)}, f32[16,1024]{1,0:T(8,128)S(1)}, bf16[2048,128]{1,0:T(8,128)(2,1)S(1)}, bf16[2048,128]{1,0:T(8,...) custom-call(s32[64]{0:T(128)S(1)} %copy-done, ...), custom_call_target="tpu_custom_call" | custom-call | flops 2000000000 | bytes 1000000 | tf_op jit(solution)/shard_map/prepare/pallas_call | solution.py:269
  19.0 0.0 collective-permute-done.3.kv2_ref
  19.0 0.0 collective-permute-done.4
  19.0 1.0 %broadcast_select_fusion = (bf16[512,256]{1,0:T(8,128)(2,1)S(1)}, bf16[512,256]{1,0:T(8,128)(2,1)S(1)}, bf16[512,256]{1,0:T(8,128)(2,1)S(1)}) fusion(bf16[512,256]{1,0:T(8,128)(2,1)S(1)} %collective-permute-done.3.kv2_ref, pred[]{:T(512)S(6)} %eq.6, bf16[512,256]{1,0:T(8,128)(2,1)S(1)} %collective-permute-done.4, bf16[512,256]{1,0:T(8,128)(2,1)} %get-tuple-element.75, ...), kind=kLoop, calls=%fused_computation.7 | loop fusion | flops 393216 | bytes 1835009 | tf_op jit(solution)/shard_map/jit(_where)/select_n | solution.py:377
  20.0 1.3 %collective-permute-start.5 = (bf16[1024,256]{1,0:T(8,128)(2,1)S(1)}, bf16[1024,256]{1,0:T(8,128)(2,1)S(1)}, u32[]{:S(2)}, u32[]{:S(2)}) collective-permute-start(bf16[1024,256]{1,0:T(8,128)(2,1)S(1)} %pad_maximum_fusion.1), channel_id=1, source_target_pairs={{0,4},{4,0},{8,12},{12,8},{16,20},{20,16},{24,28},{28,24},{32,36},... | collective-permute-start | bytes 1572872 | tf_op jit(solution)/shard_map/ppermute | solution.py:318
  21.4 1.5 %collective-permute-done.5.kv13_ref = bf16[1024,256]{1,0:T(8,128)(2,1)S(1)} collective-permute-done((bf16[1024,256]{1,0:T(8,128)(2,1)S(1)}, bf16[1024,256]{1,0:T(8,128)(2,1)S(1)}, u32[]{:S(2)}, u32[]{:S(2)}) %collective-permute-start.5) | collective-permute-done | bytes 524320 | tf_op jit(solution)/shard_map/ppermute | solution.py:318
  22.9 7.3 %attention.1 = (bf16[512,512]{1,0:T(8,128)(2,1)}, bf16[512,512]{1,0:T(8,128)(2,1)}, f32[256,512]{1,0:T(8,128)S(1)}, bf16[256,512]{1,0:T(8,128)(2,1)S(1)}, bf16[2...) custom-call(s32[4]{0:T(128)S(1)} %get-tuple-element.49.bounds_ref, ...), custom_call_target="tpu_custom_call" | custom-call | flops 5000000000 | bytes 4000000 | tf_op jit(solution)/shard_map/attention/pallas_call | solution.py:295
  30.2 1.3 %collective-permute-start.6 = (bf16[256,512]{1,0:T(8,128)(2,1)S(1)}, bf16[256,512]{1,0:T(8,128)(2,1)S(1)}, u32[]{:S(2)}, u32[]{:S(2)}) collective-permute-start(bf16[256,512]{1,0:T(8,128)(2,1)S(1)} %get-tuple-element.65), channel_id=1, source_target_pairs={{12,0},{16,4},{13,1},{17,5},{14,2},{18,6},{15,3},{19,7}} | collective-permute-start | bytes 786440 | tf_op jit(solution)/shard_map/ppermute | solution.py:318
  31.5 0.7 %collective-permute-start.7 = (bf16[256,256]{1,0:T(8,128)(2,1)S(1)}, bf16[256,256]{1,0:T(8,128)(2,1)S(1)}, u32[]{:S(2)}, u32[]{:S(2)}) collective-permute-start(bf16[256,256]{1,0:T(8,128)(2,1)S(1)} %get-tuple-element.66), channel_id=1, source_target_pairs={{16,0},{17,1},{18,2},{19,3}} | collective-permute-start | bytes 393224 | tf_op jit(solution)/shard_map/ppermute | solution.py:318
  32.2 1.3 %collective-permute-start.8 = (bf16[256,512]{1,0:T(8,128)(2,1)S(1)}, bf16[256,512]{1,0:T(8,128)(2,1)S(1)}, u32[]{:S(2)}, u32[]{:S(2)}) collective-permute-start(bf16[256,512]{1,0:T(8,128)(2,1)S(1)} %get-tuple-element.67), channel_id=1, source_target_pairs={{8,0},{12,4},{16,8},{24,16},{28,20},{32,24},{36,28},{40,32},{44,36... | collective-permute-start | bytes 786440 | tf_op jit(solution)/shard_map/ppermute | solution.py:318
  33.5 1.9 %collective-permute-start.9 = (bf16[256,512]{1,0:T(8,128)(2,1)S(1)}, bf16[256,512]{1,0:T(8,128)(2,1)S(1)}, u32[]{:S(2)}, u32[]{:S(2)}) collective-permute-start(bf16[256,512]{1,0:T(8,128)(2,1)S(1)} %get-tuple-element.68), channel_id=1, source_target_pairs={{4,0},{8,4},{12,8},{16,12},{20,16},{24,20},{28,24},{32,28},{36,32}... | collective-permute-start | bytes 786440 | tf_op jit(solution)/shard_map/ppermute | solution.py:318
  35.5 0.0 collective-permute-done.7
  35.5 6.7 %collective-permute-done.6 = bf16[256,512]{1,0:T(8,128)(2,1)S(1)} collective-permute-done((bf16[256,512]{1,0:T(8,128)(2,1)S(1)}, bf16[256,512]{1,0:T(8,128)(2,1)S(1)}, u32[]{:S(2)}, u32[]{:S(2)}) %collective-permute-start.6) | collective-permute-done | bytes 262176 | tf_op jit(solution)/shard_map/ppermute | solution.py:318
  42.2 0.1 convert_add_fusion.2
  42.3 5.3 %collective-permute-done.8 = bf16[256,512]{1,0:T(8,128)(2,1)S(1)} collective-permute-done((bf16[256,512]{1,0:T(8,128)(2,1)S(1)}, bf16[256,512]{1,0:T(8,128)(2,1)S(1)}, u32[]{:S(2)}, u32[]{:S(2)}) %collective-permute-start.8) | collective-permute-done | bytes 262176 | tf_op jit(solution)/shard_map/ppermute | solution.py:318
  47.6 0.0 collective-permute-done.9
  47.6 0.2 convert_add_fusion.1
  47.9 1.4 %collective-permute-start.10 = (bf16[128,512]{1,0:T(8,128)(2,1)S(1)}, bf16[128,512]{1,0:T(8,128)(2,1)S(1)}, u32[]{:S(2)}, u32[]{:S(2)}) collective-permute-start(bf16[128,512]{1,0:T(8,128)(2,1)S(1)} %dynamic-slice_convert_fusion), channel_id=1, source_target_pairs={{0,1},{1,0},{2,3},{3,2},{4,5},{5,4},{6,7},{7,6},{8,9},{9,8},{10,11... | collective-permute-start | bytes 393224 | tf_op jit(solution)/shard_map/ppermute | solution.py:324
  49.3 2.5 %collective-permute-done.10 = bf16[128,512]{1,0:T(8,128)(2,1)S(1)} collective-permute-done((bf16[128,512]{1,0:T(8,128)(2,1)S(1)}, bf16[128,512]{1,0:T(8,128)(2,1)S(1)}, u32[]{:S(2)}, u32[]{:S(2)}) %collective-permute-start.10) | collective-permute-done | bytes 131104 | tf_op jit(solution)/shard_map/ppermute | solution.py:324
  51.8 0.7 %slice_bitcast_fusion = (bf16[512,64]{0,1:T(8,128)(2,1)}, bf16[512,64]{0,1:T(8,128)(2,1)}) fusion(bf16[128,512]{1,0:T(8,128)(2,1)S(1)} %add_convert_fusion), kind=kLoop, calls=%fused_computation.9 | loop fusion | bytes 262144 | tf_op jit(solution)/shard_map/transpose | solution.py:405
  (4 shorter events, 0.1 us)
Async XLA Ops:
  1.6 17.3 %collective-permute-start.3 = (bf16[512,256]{1,0:T(8,128)(2,1)S(1)}, bf16[512,256]{1,0:T(8,128)(2,1)S(1)}, u32[]{:S(2)}, u32[]{:S(2)}) collective-permute-start(bf16[512,256]{1,0:T(8,128)(2,1)S(1)} %pick.1.pair_ref), channel_id=1, source_target_pairs={{0,8},{4,12},{8,16},{12,20},{16,24},{20,28},{24,32},{28,36},{32,40... | collective-permute-start | bytes 786440 | tf_op jit(solution)/shard_map/ppermute | solution.py:318
  5.6 13.4 %collective-permute-start.4 = (bf16[512,256]{1,0:T(8,128)(2,1)S(1)}, bf16[512,256]{1,0:T(8,128)(2,1)S(1)}, u32[]{:S(2)}, u32[]{:S(2)}) collective-permute-start(bf16[512,256]{1,0:T(8,128)(2,1)S(1)} %pick.1.pair_ref), channel_id=1, source_target_pairs={{0,16},{4,20},{1,17},{5,21},{2,18},{6,22},{3,19},{7,23}} | collective-permute-start | bytes 786440 | tf_op jit(solution)/shard_map/ppermute | solution.py:318
  13.6 0.7 %copy-start = (s32[64]{0:T(128)S(1)}, s32[64]{0:T(128)}, u32[]{:S(2)}) copy-start(s32[64]{0:T(128)} %lengths_ref.1) | copy-start | bytes 772
  14.3 1.0 %copy-start.1 = (bf16[512,512]{1,0:T(8,128)(2,1)S(1)}, bf16[512,512]{1,0:T(8,128)(2,1)}, u32[]{:S(2)}) copy-start(bf16[512,512]{1,0:T(8,128)(2,1)} %q_ref.1) | copy-start | bytes 1572868
  15.3 1.0 %copy-start.2 = (bf16[512,512]{1,0:T(8,128)(2,1)S(1)}, bf16[512,512]{1,0:T(8,128)(2,1)}, u32[]{:S(2)}) copy-start(bf16[512,512]{1,0:T(8,128)(2,1)} %grad_ref.1) | copy-start | bytes 1572868
  20.0 2.9 %collective-permute-start.5 = (bf16[1024,256]{1,0:T(8,128)(2,1)S(1)}, bf16[1024,256]{1,0:T(8,128)(2,1)S(1)}, u32[]{:S(2)}, u32[]{:S(2)}) collective-permute-start(bf16[1024,256]{1,0:T(8,128)(2,1)S(1)} %pad_maximum_fusion.1), channel_id=1, source_target_pairs={{0,4},{4,0},{8,12},{12,8},{16,20},{20,16},{24,28},{28,24},{32,36},... | collective-permute-start | bytes 1572872 | tf_op jit(solution)/shard_map/ppermute | solution.py:318
  30.2 12.0 %collective-permute-start.6 = (bf16[256,512]{1,0:T(8,128)(2,1)S(1)}, bf16[256,512]{1,0:T(8,128)(2,1)S(1)}, u32[]{:S(2)}, u32[]{:S(2)}) collective-permute-start(bf16[256,512]{1,0:T(8,128)(2,1)S(1)} %get-tuple-element.65), channel_id=1, source_target_pairs={{12,0},{16,4},{13,1},{17,5},{14,2},{18,6},{15,3},{19,7}} | collective-permute-start | bytes 786440 | tf_op jit(solution)/shard_map/ppermute | solution.py:318
  31.5 3.9 %collective-permute-start.7 = (bf16[256,256]{1,0:T(8,128)(2,1)S(1)}, bf16[256,256]{1,0:T(8,128)(2,1)S(1)}, u32[]{:S(2)}, u32[]{:S(2)}) collective-permute-start(bf16[256,256]{1,0:T(8,128)(2,1)S(1)} %get-tuple-element.66), channel_id=1, source_target_pairs={{16,0},{17,1},{18,2},{19,3}} | collective-permute-start | bytes 393224 | tf_op jit(solution)/shard_map/ppermute | solution.py:318
  32.2 15.4 %collective-permute-start.8 = (bf16[256,512]{1,0:T(8,128)(2,1)S(1)}, bf16[256,512]{1,0:T(8,128)(2,1)S(1)}, u32[]{:S(2)}, u32[]{:S(2)}) collective-permute-start(bf16[256,512]{1,0:T(8,128)(2,1)S(1)} %get-tuple-element.67), channel_id=1, source_target_pairs={{8,0},{12,4},{16,8},{24,16},{28,20},{32,24},{36,28},{40,32},{44,36... | collective-permute-start | bytes 786440 | tf_op jit(solution)/shard_map/ppermute | solution.py:318
  33.5 14.1 %collective-permute-start.9 = (bf16[256,512]{1,0:T(8,128)(2,1)S(1)}, bf16[256,512]{1,0:T(8,128)(2,1)S(1)}, u32[]{:S(2)}, u32[]{:S(2)}) collective-permute-start(bf16[256,512]{1,0:T(8,128)(2,1)S(1)} %get-tuple-element.68), channel_id=1, source_target_pairs={{4,0},{8,4},{12,8},{16,12},{20,16},{24,20},{28,24},{32,28},{36,32}... | collective-permute-start | bytes 786440 | tf_op jit(solution)/shard_map/ppermute | solution.py:318
  47.9 3.9 %collective-permute-start.10 = (bf16[128,512]{1,0:T(8,128)(2,1)S(1)}, bf16[128,512]{1,0:T(8,128)(2,1)S(1)}, u32[]{:S(2)}, u32[]{:S(2)}) collective-permute-start(bf16[128,512]{1,0:T(8,128)(2,1)S(1)} %dynamic-slice_convert_fusion), channel_id=1, source_target_pairs={{0,1},{1,0},{2,3},{3,2},{4,5},{5,4},{6,7},{7,6},{8,9},{9,8},{10,11... | collective-permute-start | bytes 393224 | tf_op jit(solution)/shard_map/ppermute | solution.py:324

commit v5 on v3

--- a/solution.py
+++ b/solution.py
@@ -24,7 +24,7 @@
 SCALE = HEAD_DIM ** (-0.5)
 SCALE_LOG2 = SCALE * math.log2(math.e)
 NEG = -1e30
-STEP = 2
+STEPS = (5, 2, 1)
 
 
 def contract_last(first_matrix, second_matrix):
@@ -46,36 +46,9 @@
 
 
 def prepare_kernel(
-    lengths_ref, block_ref, q_ref, grad_ref, pair_ref,
-    bounds_ref, far_ref, start_ref, max_ref, q_cat, g_cat, q_t, g_t, own_scores, own_grads, own_t,
+    start_ref, q_ref, grad_ref, pair_ref,
+    max_ref, q_cat, g_cat, q_t, g_t, own_scores, own_grads, own_t,
 ):
-    first_query = block_ref[0] * TOK_DEV
-    origin = first_query - WINDOW * TOK_DEV
-    lane_pos = first_query + lax.broadcasted_iota(jnp.int32, (1, TOK_DEV), 1)
-
-    def next_doc(doc, carry):
-        start, is_far, lane_start, edges = carry
-        end = start + lengths_ref[doc]
-        reach = lax.div(end - 1, TOK_DEV) - lax.div(start, TOK_DEV)
-        is_far = jnp.where((reach >= 3) & (doc != 1), 1, is_far)
-        lane_start = jnp.where(lane_pos >= end, end, lane_start)
-        edges = tuple(
-            jnp.where(first_query + place >= end, end, edge)
-            for place, edge in zip((0, TILE - 1, TILE, TOK_DEV - 1), edges)
-        )
-        return end, is_far, lane_start, edges
-
-    zero = jnp.int32(0)
-    _, is_far, lane_start, edges = lax.fori_loop(
-        0, NDOCS, next_doc, (zero, zero, jnp.zeros((1, TOK_DEV), jnp.int32), (zero,) * 4), unroll=8
-    )
-    far_ref[0] = is_far
-    start_ref[...] = lane_start - origin
-    for half in range(HALVES):
-        lowest = lax.div(edges[2 * half] - origin, TILE)
-        full = lax.div(edges[2 * half + 1] - origin + TILE - 1, TILE)
-        bounds_ref[2 * half] = jnp.minimum(lowest, OWN_TILE)
-        bounds_ref[2 * half + 1] = jnp.minimum(full, OWN_TILE)
     for part in range(HALVES):
         own_t[part] = pair_ref[part * TILE : (part + 1) * TILE, :].T
     for half in range(HALVES):
@@ -88,8 +61,9 @@
             g_cat[place, :] = grad_ref[rows, cols]
             q_t[:, place] = q_ref[rows, cols].T
             g_t[:, place] = grad_ref[rows, cols].T
-        start_rel = jnp.concatenate([lane_start[:, rows] - first_query] * LOCAL, axis=1)
-        query_rel = jnp.concatenate([lane_pos[:, rows] - first_query] * LOCAL, axis=1)
+        start_rel = jnp.concatenate([start_ref[:, rows] - OWN_ROW] * LOCAL, axis=1)
+        lane = lax.broadcasted_iota(jnp.int32, (1, TILE), 1)
+        query_rel = jnp.concatenate([lane + half * TILE] * LOCAL, axis=1)
         count = 1 + half
         own_rows = slice(half * TILE, (half + count) * TILE)
         keys = pair_ref[: count * TILE, :HEAD_DIM]
@@ -123,11 +97,16 @@
                 kv_t[place // TILE + part] = piece.T
 
     def in_steps(low, step, carry):
-        middle = low + (OWN_TILE - low) // STEP * STEP
-        carry = lax.fori_loop(
-            0, (OWN_TILE - low) // STEP, lambda at, held: step(low + at * STEP, STEP, held), carry
-        )
-        return lax.fori_loop(middle, OWN_TILE, lambda at, held: step(at, 1, held), carry)
+        for size in STEPS:
+            times = lax.div(OWN_TILE - low, size)
+            carry = lax.fori_loop(
+                0,
+                times,
+                lambda at, held, low=low, size=size: step(low + at * size, size, held),
+                carry,
+            )
+            low = low + times * size
+        return carry
 
     for half in range(HALVES):
         rows = slice(half * TILE, (half + 1) * TILE)
@@ -231,9 +210,12 @@
     write_term(t4b, TILE, TILE)
 
 
-def pick_kernel(column_ref, keys_ref, values_ref, pair_ref, sems):
-    column = pl.multiple_of(column_ref[0], HEAD_DIM)
-    copies = []
+def pick_kernel(
+    place_ref, lengths_ref, keys_ref, values_ref,
+    pair_ref, start_ref, bounds_ref, far_ref, lengths, sems,
+):
+    column = pl.multiple_of(place_ref[0], HEAD_DIM)
+    copies = [pltpu.make_async_copy(lengths_ref, lengths, sems.at[2])]
     for place, source in enumerate((keys_ref, values_ref)):
         cols = pl.ds(place * HEAD_DIM, HEAD_DIM)
         copies.append(
@@ -243,50 +225,79 @@
         )
     for copy in copies:
         copy.start()
-    for copy in copies:
+    first_query = place_ref[1] * TOK_DEV
+    origin = first_query - WINDOW * TOK_DEV
+    lane_pos = first_query + lax.broadcasted_iota(jnp.int32, (1, TOK_DEV), 1)
+    copies[0].wait()
+
+    def next_doc(doc, carry):
+        start, is_far, lane_start, edges = carry
+        end = start + lengths[doc]
+        reach = lax.div(end - 1, TOK_DEV) - lax.div(start, TOK_DEV)
+        is_far = jnp.where((reach >= 3) & (doc != 1), 1, is_far)
+        lane_start = jnp.where(lane_pos >= end, end, lane_start)
+        edges = tuple(
+            jnp.where(first_query + place >= end, end, edge)
+            for place, edge in zip((0, TILE - 1, TILE, TOK_DEV - 1), edges)
+        )
+        return end, is_far, lane_start, edges
+
+    zero = jnp.int32(0)
+    _, is_far, lane_start, edges = lax.fori_loop(
+        0, NDOCS, next_doc, (zero, zero, jnp.zeros((1, TOK_DEV), jnp.int32), (zero,) * 4), unroll=8
+    )
+    far_ref[0] = is_far
+    start_ref[...] = lane_start - origin
+    for half in range(HALVES):
+        lowest = lax.div(edges[2 * half] - origin, TILE)
+        full = lax.div(edges[2 * half + 1] - origin + TILE - 1, TILE)
+        bounds_ref[2 * half] = jnp.minimum(lowest, OWN_TILE)
+        bounds_ref[2 * half + 1] = jnp.minimum(full, OWN_TILE)
+    for copy in copies[1:]:
         copy.wait()
 
 
-def pick_block(column, keys, values):
+def pick_block(place, lengths, keys, values):
     smem = pl.BlockSpec(memory_space=pltpu.SMEM)
     vmem = pl.BlockSpec(memory_space=pltpu.VMEM)
     anywhere = pl.BlockSpec(memory_space=pltpu.HBM)
     return pl.pallas_call(
         pick_kernel,
-        out_shape=jax.ShapeDtypeStruct((TOK_DEV, 2 * HEAD_DIM), jnp.bfloat16),
-        in_specs=[smem, anywhere, anywhere],
-        out_specs=vmem,
-        scratch_shapes=[pltpu.SemaphoreType.DMA((2,))],
+        out_shape=[
+            jax.ShapeDtypeStruct((TOK_DEV, 2 * HEAD_DIM), jnp.bfloat16),
+            jax.ShapeDtypeStruct((1, TOK_DEV), jnp.int32),
+            jax.ShapeDtypeStruct((2 * HALVES,), jnp.int32),
+            jax.ShapeDtypeStruct((1,), jnp.int32),
+        ],
+        in_specs=[smem, anywhere, anywhere, anywhere],
+        out_specs=[vmem, vmem, smem, smem],
+        scratch_shapes=[pltpu.SMEM((NDOCS,), jnp.int32), pltpu.SemaphoreType.DMA((3,))],
         compiler_params=pltpu.CompilerParams(vmem_limit_bytes=60 * 1024 * 1024),
         cost_estimate=pl.CostEstimate(flops=0, bytes_accessed=10**6, transcendentals=0),
         name="pick",
-    )(column, keys, values)
-
-
-def prepare(lengths, block, queries, grads, pair):
+    )(place, lengths, keys, values)
+
+
+def prepare(starts, queries, grads, pair):
     vmem = pl.BlockSpec(memory_space=pltpu.VMEM)
-    smem = pl.BlockSpec(memory_space=pltpu.SMEM)
     own = jax.ShapeDtypeStruct((3 * TILE, LANES), jnp.float32)
     rows = jax.ShapeDtypeStruct((HALVES * LANES, HEAD_DIM), jnp.bfloat16)
     cols = jax.ShapeDtypeStruct((HEAD_DIM, HALVES * LANES), jnp.bfloat16)
     return pl.pallas_call(
         prepare_kernel,
         out_shape=[
-            jax.ShapeDtypeStruct((2 * HALVES,), jnp.int32),
-            jax.ShapeDtypeStruct((1,), jnp.int32),
-            jax.ShapeDtypeStruct((1, TOK_DEV), jnp.int32),
             jax.ShapeDtypeStruct((8 * HALVES, LANES), jnp.float32),
             rows, rows, cols, cols, own, own,
             jax.ShapeDtypeStruct((HALVES, 2 * HEAD_DIM, TILE), jnp.bfloat16),
         ],
-        in_specs=[smem, smem, vmem, vmem, vmem],
-        out_specs=[smem, smem] + [vmem] * 9,
+        in_specs=[vmem] * 4,
+        out_specs=[vmem] * 8,
         compiler_params=pltpu.CompilerParams(vmem_limit_bytes=24 * 1024 * 1024),
         cost_estimate=pl.CostEstimate(
             flops=2 * 10**9, bytes_accessed=10**6, transcendentals=0
         ),
         name="prepare",
-    )(lengths, block, queries, grads, pair)
+    )(starts, queries, grads, pair)
 
 
 def attention_block(bounds, state, kv_blocks):
@@ -346,7 +357,8 @@
     head_index = lax.axis_index("head")
     kv_start = head_index * LOCAL // (HEADS // KV_HEADS) * HEAD_DIM
     own_half = head_index % 2
-    own_pair = pick_block(kv_start.astype(jnp.int32).reshape(1), key_states, value_states)
+    place = jnp.stack([kv_start.astype(jnp.int32), block_index.astype(jnp.int32)])
+    own_pair, starts, bounds, far_flag = pick_block(place, lengths, key_states, value_states)
     near = {
         distance: [pair for pair in pairs_at(distance, count) if needed(*pair)]
         for distance in (1, 2)
@@ -354,19 +366,15 @@
     near[3] = [(0, 3), (1, 4)]
     near[4] = [(0, 4)]
     wide = {distance: pairs_at(distance, count)[WINDOW:] for distance in (3, 4)}
+    is_far = far_flag[0] == 1
+    far_fourth = lax.cond(is_far, lambda pair: moved(pair, wide[4]), lambda pair: pair, own_pair)
     second = moved(own_pair, pairs_at(2, count))
     fourth = moved(own_pair, [(0, 4), (1, 5)])
-    bounds, far_flag, *state = prepare(
-        lengths, block_index.astype(jnp.int32).reshape(1), query_states, out_grad, own_pair
-    )
-    is_far = far_flag[0] == 1
-    second, fourth = lax.optimization_barrier((second, fourth))
-    fourth = lax.cond(
-        is_far,
-        lambda got, pair: got + moved(pair, wide[4]),
-        lambda got, pair: got,
-        fourth, own_pair,
-    )
+    own_pair, far_fourth = lax.optimization_barrier((own_pair, far_fourth))
+    state = prepare(starts, query_states, out_grad, own_pair)
+    second, fourth, highest = lax.optimization_barrier((second, fourth, state[0]))
+    state = [starts, highest] + list(state[1:])
+    fourth = jnp.where(block_index < 6, fourth, far_fourth)
     is_even = block_index % 2 == 0
     outbound = jnp.concatenate(
         [jnp.where(is_even, own_pair, second), jnp.where(is_even, second, fourth)], axis=0

time: 57.7 us -> 52.2 us (0.905)
  local copies, waits for them, and re-layouts: 11.5 us -> 4.16 us
  waiting for transfers between devices: 16.1 us -> 17.3 us
  other arithmetic: 0.44 us -> 1.03 us
    unnamed x22 -> x10, local copies, waits for them, and re-layouts: 10.8 us -> 2.77 us
    ppermute x7, waiting for transfers between devices: 13.5 us -> 14.8 us  [moved(): return lax.ppermute(value, 'ctx', pairs)]
    cond x0 -> x1, local copies, waits for them, and re-layouts: none -> 0.7 us
    another operation x0 -> x1, other arithmetic: none -> 0.59 us  [shards(): jnp.stack([kv_start.astype(jnp.int32), block_index.astype(jnp.int32)])]
  transfers between devices with their start and end apart: 8 -> 8, of which waited for: 4 -> 6; matrix products, arithmetic and copies ran while one was open for 0% -> 2% of each run, Pallas kernels for 5% -> 2%
where the time goes in v5:
time: 52.2 us; the launch traced here: 51.6 us
  waiting for transfers between devices  17.3 us (33%)
  starting transfers between devices  16.5 us (32%)
  Pallas kernels  11.1 us (21%)
  local copies, waits for them, and re-layouts  4.16 us (8%)
  between operations  1.42 us (3%)
  other arithmetic  1.03 us (2%)
    ppermute x7, starting transfers between devices, moved(): return lax.ppermute(value, 'ctx', pairs)  15.1 us
    ppermute x7, waiting for transfers between devices, moved(): return lax.ppermute(value, 'ctx', pairs)  14.8 us
    pallas_call x1, Pallas kernels, attention_block(): pl.pallas_call(attention_kernel, out_shape=[wide, wide, own, term, term,...  7.39 us
    unnamed x10, local copies, waits for them, and re-layouts  2.77 us
    pallas_call x1, Pallas kernels, pick_block(): pl.pallas_call(pick_kernel, out_shape=[jax.ShapeDtypeStruct((TOK_DEV, 2 *...  2.57 us
    ppermute x1, waiting for transfers between devices, from_partner(): return lax.ppermute(value, axis, pairs)  2.5 us
    ppermute x1, starting transfers between devices, from_partner(): return lax.ppermute(value, axis, pairs)  1.4 us
    pallas_call x1, Pallas kernels, prepare(): pl.pallas_call(prepare_kernel, out_shape=[jax.ShapeDtypeStruct((8 * HALVE...  1.19 us
  transfers between devices with their start and end apart: 8, of which 6 were waited for; matrix products, arithmetic and copies ran while one was open for 2% of the time, Pallas kernels for 2%

profile of v5, /device:TPU:1, one launch (start us, length us, event | category | flops | bytes accessed | tf_op | source)
XLA Modules:
  0.0 51.6 jit_solution(6830580626675737981)
XLA Ops:
  0.6 0.6 %pad_add_fusion.place_ref = s32[2]{0:T(128)} fusion(s32[1]{0:T(128)} %bitcast.1, s32[1]{0:T(128)} %bitcast), kind=kLoop, calls=%fused_computation.12 | loop fusion | flops 2 | bytes 16 | tf_op jit(solution)/shard_map/stack | solution.py:360
  1.2 2.6 %pick.1 = (bf16[512,256]{1,0:T(8,128)(2,1)S(1)}, s32[1,512]{1,0:T(1,128)}, s32[4]{0:T(128)}, s32[1]{0:T(128)}) custom-call(s32[2]{0:T(128)} %pad_add_fusion.place_ref, s32[64]{0:T(128)} %lengths_ref.1, bf16[512,256]{1,0:T(8,128)(2,1)} %keys_ref.1, bf16[512,256]{1,0:T(8,128)(2,1)} %values_ref.1), custom_call_target="tpu_custom_call" | custom-call | bytes 1000000 | tf_op jit(solution)/shard_map/pick/pallas_call | solution.py:264
  3.8 4.0 %collective-permute-start.3 = (bf16[512,256]{1,0:T(8,128)(2,1)S(1)}, bf16[512,256]{1,0:T(8,128)(2,1)S(1)}, u32[]{:S(2)}, u32[]{:S(2)}) collective-permute-start(bf16[512,256]{1,0:T(8,128)(2,1)S(1)} %get-tuple-element.54.pair_ref), channel_id=1, source_target_pairs={{0,8},{4,12},{8,16},{12,20},{16,24},{20,28},{24,32},{28,36},{32,40... | collective-permute-start | bytes 786440 | tf_op jit(solution)/shard_map/ppermute | solution.py:333
  7.8 4.4 %collective-permute-start.4 = (bf16[512,256]{1,0:T(8,128)(2,1)S(1)}, bf16[512,256]{1,0:T(8,128)(2,1)S(1)}, u32[]{:S(2)}, u32[]{:S(2)}) collective-permute-start(bf16[512,256]{1,0:T(8,128)(2,1)S(1)} %get-tuple-element.54.pair_ref), channel_id=1, source_target_pairs={{0,16},{4,20},{1,17},{5,21},{2,18},{6,22},{3,19},{7,23}} | collective-permute-start | bytes 786440 | tf_op jit(solution)/shard_map/ppermute | solution.py:333
  12.8 0.7 %conditional.2 = (bf16[512,256]{1,0:T(8,128)(2,1)}) conditional(s32[]{:T(128)} %bitcast.2, bf16[512,256]{1,0:T(8,128)(2,1)S(1)} %get-tuple-element.54.pair_ref, bf16[512,256]{1,0:T(8,128)(2,1)S(1)} %get-tuple-element.54.pair_ref), branch_computations={%region_0.1_spmd, %region_1.2_spmd} | conditional | bytes 1048624 | solution.py:370
  12.8 0.7 %copy.9 = bf16[512,256]{1,0:T(8,128)(2,1)} copy(bf16[512,256]{1,0:T(8,128)(2,1)S(1)} %param) | data formatting | bytes 524288 | tf_op jit(solution)/shard_map/cond
  13.5 0.0 copy-start
  13.5 1.0 %copy-done = bf16[512,512]{1,0:T(8,128)(2,1)S(1)} copy-done((bf16[512,512]{1,0:T(8,128)(2,1)S(1)}, bf16[512,512]{1,0:T(8,128)(2,1)}, u32[]{:S(2)}) %copy-start) | copy-done | bytes 524312
  14.5 0.0 copy-start.1
  14.5 1.0 %copy-done.1 = bf16[512,512]{1,0:T(8,128)(2,1)S(1)} copy-done((bf16[512,512]{1,0:T(8,128)(2,1)S(1)}, bf16[512,512]{1,0:T(8,128)(2,1)}, u32[]{:S(2)}) %copy-start.1) | copy-done | bytes 524312
  15.6 0.0 copy-start.2
  15.6 0.7 %copy-done.2 = s32[1,512]{1,0:T(1,128)S(1)} copy-done((s32[1,512]{1,0:T(1,128)S(1)}, s32[1,512]{1,0:T(1,128)}, u32[]{:S(2)}) %copy-start.2) | copy-done | bytes 2072
  16.3 0.0 copy-start.3
  16.3 0.0 copy-start.4
  16.3 1.2 %prepare.1 = (f32[16,1024]{1,0:T(8,128)S(1)}, bf16[2048,128]{1,0:T(8,128)(2,1)S(1)}, bf16[2048,128]{1,0:T(8,128)(2,1)S(1)}, bf16[128,2048]{1,0:T(8,128)(2,1)S(1)...) custom-call(s32[1,512]{1,0:T(1,128)S(1)} %copy-done.2, ...), custom_call_target="tpu_custom_call" | custom-call | flops 2000000000 | bytes 1000000 | tf_op jit(solution)/shard_map/prepare/pallas_call | solution.py:286
  17.4 0.0 collective-permute-done.3.kv2_ref
  17.5 0.9 %collective-permute-done.4 = bf16[512,256]{1,0:T(8,128)(2,1)S(1)} collective-permute-done((bf16[512,256]{1,0:T(8,128)(2,1)S(1)}, bf16[512,256]{1,0:T(8,128)(2,1)S(1)}, u32[]{:S(2)}, u32[]{:S(2)}) %collective-permute-start.4) | collective-permute-done | bytes 262176 | tf_op jit(solution)/shard_map/ppermute | solution.py:333
  18.3 0.1 broadcast_select_fusion.1
  18.4 1.6 %collective-permute-start.5 = (bf16[1024,256]{1,0:T(8,128)(2,1)S(1)}, bf16[1024,256]{1,0:T(8,128)(2,1)S(1)}, u32[]{:S(2)}, u32[]{:S(2)}) collective-permute-start(bf16[1024,256]{1,0:T(8,128)(2,1)S(1)} %pad_maximum_fusion.1), channel_id=1, source_target_pairs={{0,4},{4,0},{8,12},{12,8},{16,20},{20,16},{24,28},{28,24},{32,36},... | collective-permute-start | bytes 1572872 | tf_op jit(solution)/shard_map/ppermute | solution.py:333
  20.1 1.5 %collective-permute-done.5.kv13_ref = bf16[1024,256]{1,0:T(8,128)(2,1)S(1)} collective-permute-done((bf16[1024,256]{1,0:T(8,128)(2,1)S(1)}, bf16[1024,256]{1,0:T(8,128)(2,1)S(1)}, u32[]{:S(2)}, u32[]{:S(2)}) %collective-permute-start.5) | collective-permute-done | bytes 524320 | tf_op jit(solution)/shard_map/ppermute | solution.py:333
  21.6 0.0 copy-done.3
  21.6 0.0 copy-done.4
  21.6 7.4 %attention.1 = (bf16[512,512]{1,0:T(8,128)(2,1)}, bf16[512,512]{1,0:T(8,128)(2,1)}, f32[256,512]{1,0:T(8,128)S(1)}, bf16[256,512]{1,0:T(8,128)(2,1)S(1)}, bf16[2...) custom-call(s32[4]{0:T(128)S(1)} %copy-done.4, ...), custom_call_target="tpu_custom_call" | custom-call | flops 5000000000 | bytes 4000000 | tf_op jit(solution)/shard_map/attention/pallas_call | solution.py:310
  29.0 1.3 %collective-permute-start.6 = (bf16[256,512]{1,0:T(8,128)(2,1)S(1)}, bf16[256,512]{1,0:T(8,128)(2,1)S(1)}, u32[]{:S(2)}, u32[]{:S(2)}) collective-permute-start(bf16[256,512]{1,0:T(8,128)(2,1)S(1)} %get-tuple-element.70), channel_id=1, source_target_pairs={{12,0},{16,4},{13,1},{17,5},{14,2},{18,6},{15,3},{19,7}} | collective-permute-start | bytes 786440 | tf_op jit(solution)/shard_map/ppermute | solution.py:333
  30.3 0.7 %collective-permute-start.7 = (bf16[256,256]{1,0:T(8,128)(2,1)S(1)}, bf16[256,256]{1,0:T(8,128)(2,1)S(1)}, u32[]{:S(2)}, u32[]{:S(2)}) collective-permute-start(bf16[256,256]{1,0:T(8,128)(2,1)S(1)} %get-tuple-element.71), channel_id=1, source_target_pairs={{16,0},{17,1},{18,2},{19,3}} | collective-permute-start | bytes 393224 | tf_op jit(solution)/shard_map/ppermute | solution.py:333
  31.0 1.3 %collective-permute-start.8 = (bf16[256,512]{1,0:T(8,128)(2,1)S(1)}, bf16[256,512]{1,0:T(8,128)(2,1)S(1)}, u32[]{:S(2)}, u32[]{:S(2)}) collective-permute-start(bf16[256,512]{1,0:T(8,128)(2,1)S(1)} %get-tuple-element.72), channel_id=1, source_target_pairs={{8,0},{12,4},{16,8},{24,16},{28,20},{32,24},{36,28},{40,32},{44,36... | collective-permute-start | bytes 786440 | tf_op jit(solution)/shard_map/ppermute | solution.py:333
  32.3 1.9 %collective-permute-start.9 = (bf16[256,512]{1,0:T(8,128)(2,1)S(1)}, bf16[256,512]{1,0:T(8,128)(2,1)S(1)}, u32[]{:S(2)}, u32[]{:S(2)}) collective-permute-start(bf16[256,512]{1,0:T(8,128)(2,1)S(1)} %get-tuple-element.73), channel_id=1, source_target_pairs={{4,0},{8,4},{12,8},{16,12},{20,16},{24,20},{28,24},{32,28},{36,32}... | collective-permute-start | bytes 786440 | tf_op jit(solution)/shard_map/ppermute | solution.py:333
  34.2 0.0 collective-permute-done.7
  34.2 8.4 %collective-permute-done.6 = bf16[256,512]{1,0:T(8,128)(2,1)S(1)} collective-permute-done((bf16[256,512]{1,0:T(8,128)(2,1)S(1)}, bf16[256,512]{1,0:T(8,128)(2,1)S(1)}, u32[]{:S(2)}, u32[]{:S(2)}) %collective-permute-start.6) | collective-permute-done | bytes 262176 | tf_op jit(solution)/shard_map/ppermute | solution.py:333
  42.6 0.1 convert_add_fusion.2
  42.7 3.8 %collective-permute-done.8 = bf16[256,512]{1,0:T(8,128)(2,1)S(1)} collective-permute-done((bf16[256,512]{1,0:T(8,128)(2,1)S(1)}, bf16[256,512]{1,0:T(8,128)(2,1)S(1)}, u32[]{:S(2)}, u32[]{:S(2)}) %collective-permute-start.8) | collective-permute-done | bytes 262176 | tf_op jit(solution)/shard_map/ppermute | solution.py:333
  46.5 0.2 collective-permute-done.9
  46.7 0.2 convert_add_fusion.1
  47.0 1.4 %collective-permute-start.10 = (bf16[128,512]{1,0:T(8,128)(2,1)S(1)}, bf16[128,512]{1,0:T(8,128)(2,1)S(1)}, u32[]{:S(2)}, u32[]{:S(2)}) collective-permute-start(bf16[128,512]{1,0:T(8,128)(2,1)S(1)} %dynamic-slice_convert_fusion), channel_id=1, source_target_pairs={{0,1},{1,0},{2,3},{3,2},{4,5},{5,4},{6,7},{7,6},{8,9},{9,8},{10,11... | collective-permute-start | bytes 393224 | tf_op jit(solution)/shard_map/ppermute | solution.py:339
  48.4 2.5 %collective-permute-done.10 = bf16[128,512]{1,0:T(8,128)(2,1)S(1)} collective-permute-done((bf16[128,512]{1,0:T(8,128)(2,1)S(1)}, bf16[128,512]{1,0:T(8,128)(2,1)S(1)}, u32[]{:S(2)}, u32[]{:S(2)}) %collective-permute-start.10) | collective-permute-done | bytes 131104 | tf_op jit(solution)/shard_map/ppermute | solution.py:339
  50.9 0.7 %slice_bitcast_fusion = (bf16[512,64]{0,1:T(8,128)(2,1)}, bf16[512,64]{0,1:T(8,128)(2,1)}) fusion(bf16[128,512]{1,0:T(8,128)(2,1)S(1)} %add_convert_fusion), kind=kLoop, calls=%fused_computation.10 | loop fusion | bytes 262144 | tf_op jit(solution)/shard_map/transpose | solution.py:408
  (4 shorter events, 0.1 us)
Async XLA Ops:
  3.8 13.6 %collective-permute-start.3 = (bf16[512,256]{1,0:T(8,128)(2,1)S(1)}, bf16[512,256]{1,0:T(8,128)(2,1)S(1)}, u32[]{:S(2)}, u32[]{:S(2)}) collective-permute-start(bf16[512,256]{1,0:T(8,128)(2,1)S(1)} %get-tuple-element.54.pair_ref), channel_id=1, source_target_pairs={{0,8},{4,12},{8,16},{12,20},{16,24},{20,28},{24,32},{28,36},{32,40... | collective-permute-start | bytes 786440 | tf_op jit(solution)/shard_map/ppermute | solution.py:333
  7.8 10.6 %collective-permute-start.4 = (bf16[512,256]{1,0:T(8,128)(2,1)S(1)}, bf16[512,256]{1,0:T(8,128)(2,1)S(1)}, u32[]{:S(2)}, u32[]{:S(2)}) collective-permute-start(bf16[512,256]{1,0:T(8,128)(2,1)S(1)} %get-tuple-element.54.pair_ref), channel_id=1, source_target_pairs={{0,16},{4,20},{1,17},{5,21},{2,18},{6,22},{3,19},{7,23}} | collective-permute-start | bytes 786440 | tf_op jit(solution)/shard_map/ppermute | solution.py:333
  13.5 1.0 %copy-start = (bf16[512,512]{1,0:T(8,128)(2,1)S(1)}, bf16[512,512]{1,0:T(8,128)(2,1)}, u32[]{:S(2)}) copy-start(bf16[512,512]{1,0:T(8,128)(2,1)} %q_ref.1) | copy-start | bytes 1572868
  14.5 1.0 %copy-start.1 = (bf16[512,512]{1,0:T(8,128)(2,1)S(1)}, bf16[512,512]{1,0:T(8,128)(2,1)}, u32[]{:S(2)}) copy-start(bf16[512,512]{1,0:T(8,128)(2,1)} %grad_ref.1) | copy-start | bytes 1572868
  15.6 0.7 %copy-start.2 = (s32[1,512]{1,0:T(1,128)S(1)}, s32[1,512]{1,0:T(1,128)}, u32[]{:S(2)}) copy-start(s32[1,512]{1,0:T(1,128)} %get-tuple-element.51.start_ref) | copy-start | bytes 6148
  16.3 5.4 %copy-start.3 = (s32[1,512]{1,0:T(1,128)S(1)}, s32[1,512]{1,0:T(1,128)}, u32[]{:S(2)}) copy-start(s32[1,512]{1,0:T(1,128)} %get-tuple-element.51.start_ref) | copy-start | bytes 6148
  16.3 5.4 %copy-start.4 = (s32[4]{0:T(128)S(1)}, s32[4]{0:T(128)}, u32[]{:S(2)}) copy-start(s32[4]{0:T(128)} %get-tuple-element.50.bounds_ref) | copy-start | bytes 52
  18.4 3.2 %collective-permute-start.5 = (bf16[1024,256]{1,0:T(8,128)(2,1)S(1)}, bf16[1024,256]{1,0:T(8,128)(2,1)S(1)}, u32[]{:S(2)}, u32[]{:S(2)}) collective-permute-start(bf16[1024,256]{1,0:T(8,128)(2,1)S(1)} %pad_maximum_fusion.1), channel_id=1, source_target_pairs={{0,4},{4,0},{8,12},{12,8},{16,20},{20,16},{24,28},{28,24},{32,36},... | collective-permute-start | bytes 1572872 | tf_op jit(solution)/shard_map/ppermute | solution.py:333
  29.0 13.6 %collective-permute-start.6 = (bf16[256,512]{1,0:T(8,128)(2,1)S(1)}, bf16[256,512]{1,0:T(8,128)(2,1)S(1)}, u32[]{:S(2)}, u32[]{:S(2)}) collective-permute-start(bf16[256,512]{1,0:T(8,128)(2,1)S(1)} %get-tuple-element.70), channel_id=1, source_target_pairs={{12,0},{16,4},{13,1},{17,5},{14,2},{18,6},{15,3},{19,7}} | collective-permute-start | bytes 786440 | tf_op jit(solution)/shard_map/ppermute | solution.py:333
  30.3 3.9 %collective-permute-start.7 = (bf16[256,256]{1,0:T(8,128)(2,1)S(1)}, bf16[256,256]{1,0:T(8,128)(2,1)S(1)}, u32[]{:S(2)}, u32[]{:S(2)}) collective-permute-start(bf16[256,256]{1,0:T(8,128)(2,1)S(1)} %get-tuple-element.71), channel_id=1, source_target_pairs={{16,0},{17,1},{18,2},{19,3}} | collective-permute-start | bytes 393224 | tf_op jit(solution)/shard_map/ppermute | solution.py:333
  31.0 15.6 %collective-permute-start.8 = (bf16[256,512]{1,0:T(8,128)(2,1)S(1)}, bf16[256,512]{1,0:T(8,128)(2,1)S(1)}, u32[]{:S(2)}, u32[]{:S(2)}) collective-permute-start(bf16[256,512]{1,0:T(8,128)(2,1)S(1)} %get-tuple-element.72), channel_id=1, source_target_pairs={{8,0},{12,4},{16,8},{24,16},{28,20},{32,24},{36,28},{40,32},{44,36... | collective-permute-start | bytes 786440 | tf_op jit(solution)/shard_map/ppermute | solution.py:333
  32.3 14.4 %collective-permute-start.9 = (bf16[256,512]{1,0:T(8,128)(2,1)S(1)}, bf16[256,512]{1,0:T(8,128)(2,1)S(1)}, u32[]{:S(2)}, u32[]{:S(2)}) collective-permute-start(bf16[256,512]{1,0:T(8,128)(2,1)S(1)} %get-tuple-element.73), channel_id=1, source_target_pairs={{4,0},{8,4},{12,8},{16,12},{20,16},{24,20},{28,24},{32,28},{36,32}... | collective-permute-start | bytes 786440 | tf_op jit(solution)/shard_map/ppermute | solution.py:333
  47.0 3.9 %collective-permute-start.10 = (bf16[128,512]{1,0:T(8,128)(2,1)S(1)}, bf16[128,512]{1,0:T(8,128)(2,1)S(1)}, u32[]{:S(2)}, u32[]{:S(2)}) collective-permute-start(bf16[128,512]{1,0:T(8,128)(2,1)S(1)} %dynamic-slice_convert_fusion), channel_id=1, source_target_pairs={{0,1},{1,0},{2,3},{3,2},{4,5},{5,4},{6,7},{7,6},{8,9},{9,8},{10,11... | collective-permute-start | bytes 393224 | tf_op jit(solution)/shard_map/ppermute | solution.py:339

commit v6 on v5

--- a/solution.py
+++ b/solution.py
@@ -210,12 +210,9 @@
     write_term(t4b, TILE, TILE)
 
 
-def pick_kernel(
-    place_ref, lengths_ref, keys_ref, values_ref,
-    pair_ref, start_ref, bounds_ref, far_ref, lengths, sems,
-):
-    column = pl.multiple_of(place_ref[0], HEAD_DIM)
-    copies = [pltpu.make_async_copy(lengths_ref, lengths, sems.at[2])]
+def pick_kernel(column_ref, keys_ref, values_ref, pair_ref, sems):
+    column = pl.multiple_of(column_ref[0], HEAD_DIM)
+    copies = []
     for place, source in enumerate((keys_ref, values_ref)):
         cols = pl.ds(place * HEAD_DIM, HEAD_DIM)
         copies.append(
@@ -225,14 +222,34 @@
         )
     for copy in copies:
         copy.start()
-    first_query = place_ref[1] * TOK_DEV
+    for copy in copies:
+        copy.wait()
+
+
+def pick_block(column, keys, values):
+    smem = pl.BlockSpec(memory_space=pltpu.SMEM)
+    vmem = pl.BlockSpec(memory_space=pltpu.VMEM)
+    anywhere = pl.BlockSpec(memory_space=pltpu.HBM)
+    return pl.pallas_call(
+        pick_kernel,
+        out_shape=jax.ShapeDtypeStruct((TOK_DEV, 2 * HEAD_DIM), jnp.bfloat16),
+        in_specs=[smem, anywhere, anywhere],
+        out_specs=vmem,
+        scratch_shapes=[pltpu.SemaphoreType.DMA((2,))],
+        compiler_params=pltpu.CompilerParams(vmem_limit_bytes=60 * 1024 * 1024),
+        cost_estimate=pl.CostEstimate(flops=0, bytes_accessed=10**6, transcendentals=0),
+        name="pick",
+    )(column, keys, values)
+
+
+def scan_kernel(lengths_ref, block_ref, start_ref, bounds_ref, far_ref):
+    first_query = block_ref[0] * TOK_DEV
     origin = first_query - WINDOW * TOK_DEV
     lane_pos = first_query + lax.broadcasted_iota(jnp.int32, (1, TOK_DEV), 1)
-    copies[0].wait()
 
     def next_doc(doc, carry):
         start, is_far, lane_start, edges = carry
-        end = start + lengths[doc]
+        end = start + lengths_ref[doc]
         reach = lax.div(end - 1, TOK_DEV) - lax.div(start, TOK_DEV)
         is_far = jnp.where((reach >= 3) & (doc != 1), 1, is_far)
         lane_start = jnp.where(lane_pos >= end, end, lane_start)
@@ -253,29 +270,23 @@
         full = lax.div(edges[2 * half + 1] - origin + TILE - 1, TILE)
         bounds_ref[2 * half] = jnp.minimum(lowest, OWN_TILE)
         bounds_ref[2 * half + 1] = jnp.minimum(full, OWN_TILE)
-    for copy in copies[1:]:
-        copy.wait()
-
-
-def pick_block(place, lengths, keys, values):
+
+
+def scan_documents(lengths, block):
     smem = pl.BlockSpec(memory_space=pltpu.SMEM)
     vmem = pl.BlockSpec(memory_space=pltpu.VMEM)
-    anywhere = pl.BlockSpec(memory_space=pltpu.HBM)
     return pl.pallas_call(
-        pick_kernel,
+        scan_kernel,
         out_shape=[
-            jax.ShapeDtypeStruct((TOK_DEV, 2 * HEAD_DIM), jnp.bfloat16),
             jax.ShapeDtypeStruct((1, TOK_DEV), jnp.int32),
             jax.ShapeDtypeStruct((2 * HALVES,), jnp.int32),
             jax.ShapeDtypeStruct((1,), jnp.int32),
         ],
-        in_specs=[smem, anywhere, anywhere, anywhere],
-        out_specs=[vmem, vmem, smem, smem],
-        scratch_shapes=[pltpu.SMEM((NDOCS,), jnp.int32), pltpu.SemaphoreType.DMA((3,))],
-        compiler_params=pltpu.CompilerParams(vmem_limit_bytes=60 * 1024 * 1024),
-        cost_estimate=pl.CostEstimate(flops=0, bytes_accessed=10**6, transcendentals=0),
-        name="pick",
-    )(place, lengths, keys, values)
+        in_specs=[smem, smem],
+        out_specs=[vmem, smem, smem],
+        cost_estimate=pl.CostEstimate(flops=10**6, bytes_accessed=10**4, transcendentals=0),
+        name="scan",
+    )(lengths, block)
 
 
 def prepare(starts, queries, grads, pair):
@@ -357,8 +368,8 @@
     head_index = lax.axis_index("head")
     kv_start = head_index * LOCAL // (HEADS // KV_HEADS) * HEAD_DIM
     own_half = head_index % 2
-    place = jnp.stack([kv_start.astype(jnp.int32), block_index.astype(jnp.int32)])
-    own_pair, starts, bounds, far_flag = pick_block(place, lengths, key_states, value_states)
+    own_pair = pick_block(kv_start.astype(jnp.int32).reshape(1), key_states, value_states)
+    starts, bounds, far_flag = scan_documents(lengths, block_index.astype(jnp.int32).reshape(1))
     near = {
         distance: [pair for pair in pairs_at(distance, count) if needed(*pair)]
         for distance in (1, 2)

time: 52.2 us -> 50 us (0.958)
  waiting for transfers between devices: 17.3 us -> 15.9 us
  other arithmetic: 1.03 us -> 0.45 us
    ppermute x7, waiting for transfers between devices: 14.8 us -> 13.4 us  [moved(): return lax.ppermute(value, 'ctx', pairs)]
    another operation x1 -> x0, other arithmetic: 0.59 us -> none  [shards(): jnp.stack([kv_start.astype(jnp.int32), block_index.astype(jnp.int32)])]
    pallas_call x1 -> x2, Pallas kernels: 2.57 us -> 2.86 us  [the longest x1 1.87 us: scan_documents(): pl.pallas_call(scan_kernel, out_shape=[jax.ShapeDtypeStruct((1, TOK_DEV),...]
  transfers between devices with their start and end apart: 8 -> 8, of which waited for: 6 -> 5; matrix products, arithmetic and copies ran while one was open for 2% -> 2% of each run, Pallas kernels for 2% -> 6%
where the time goes in v6:
time: 50 us; the launch traced here: 49.7 us
  starting transfers between devices  16.2 us (32%)
  waiting for transfers between devices  15.9 us (32%)
  Pallas kernels  11.4 us (23%)
  local copies, waits for them, and re-layouts  4.16 us (8%)
  between operations  1.47 us (3%)
    ppermute x7, starting transfers between devices, moved(): return lax.ppermute(value, 'ctx', pairs)  14.8 us
    ppermute x7, waiting for transfers between devices, moved(): return lax.ppermute(value, 'ctx', pairs)  13.4 us
    pallas_call x1, Pallas kernels, attention_block(): pl.pallas_call(attention_kernel, out_shape=[wide, wide, own, term, term,...  7.4 us
    unnamed x10, local copies, waits for them, and re-layouts  2.77 us
    ppermute x1, waiting for transfers between devices, from_partner(): return lax.ppermute(value, axis, pairs)  2.5 us
    pallas_call x1, Pallas kernels, scan_documents(): pl.pallas_call(scan_kernel, out_shape=[jax.ShapeDtypeStruct((1, TOK_DEV),...  1.87 us
    ppermute x1, starting transfers between devices, from_partner(): return lax.ppermute(value, axis, pairs)  1.41 us
    pallas_call x1, Pallas kernels, prepare(): pl.pallas_call(prepare_kernel, out_shape=[jax.ShapeDtypeStruct((8 * HALVE...  1.19 us
  transfers between devices with their start and end apart: 8, of which 5 were waited for; matrix products, arithmetic and copies ran while one was open for 2% of the time, Pallas kernels for 6%

profile of v6, /device:TPU:1, one launch (start us, length us, event | category | flops | bytes accessed | tf_op | source)
XLA Modules:
  0.0 49.7 jit_solution(17198283181121493711)
XLA Ops:
  0.6 1.0 %pick.1.pair_ref = bf16[512,256]{1,0:T(8,128)(2,1)S(1)} custom-call(s32[1]{0:T(128)} %bitcast.1.column_ref, bf16[512,256]{1,0:T(8,128)(2,1)} %keys_ref.1, bf16[512,256]{1,0:T(8,128)(2,1)} %values_ref.1), custom_call_target="tpu_custom_call" | custom-call | bytes 1000000 | tf_op jit(solution)/shard_map/pick/pallas_call | solution.py:233
  1.6 4.0 %collective-permute-start.3 = (bf16[512,256]{1,0:T(8,128)(2,1)S(1)}, bf16[512,256]{1,0:T(8,128)(2,1)S(1)}, u32[]{:S(2)}, u32[]{:S(2)}) collective-permute-start(bf16[512,256]{1,0:T(8,128)(2,1)S(1)} %pick.1.pair_ref), channel_id=1, source_target_pairs={{0,8},{4,12},{8,16},{12,20},{16,24},{20,28},{24,32},{28,36},{32,40... | collective-permute-start | bytes 786440 | tf_op jit(solution)/shard_map/ppermute | solution.py:344
  5.6 4.4 %collective-permute-start.4 = (bf16[512,256]{1,0:T(8,128)(2,1)S(1)}, bf16[512,256]{1,0:T(8,128)(2,1)S(1)}, u32[]{:S(2)}, u32[]{:S(2)}) collective-permute-start(bf16[512,256]{1,0:T(8,128)(2,1)S(1)} %pick.1.pair_ref), channel_id=1, source_target_pairs={{0,16},{4,20},{1,17},{5,21},{2,18},{6,22},{3,19},{7,23}} | collective-permute-start | bytes 786440 | tf_op jit(solution)/shard_map/ppermute | solution.py:344
  10.0 1.9 %scan.1 = (s32[1,512]{1,0:T(1,128)}, s32[4]{0:T(128)}, s32[1]{0:T(128)}) custom-call(s32[64]{0:T(128)} %lengths_ref.1, s32[1]{0:T(128)} %bitcast.block_ref), custom_call_target="tpu_custom_call" | custom-call | flops 1000000 | bytes 10000 | tf_op jit(solution)/shard_map/scan/pallas_call | solution.py:278
  12.5 0.7 %conditional.2 = (bf16[512,256]{1,0:T(8,128)(2,1)}) conditional(s32[]{:T(128)} %bitcast.2, bf16[512,256]{1,0:T(8,128)(2,1)S(1)} %pick.1.pair_ref, bf16[512,256]{1,0:T(8,128)(2,1)S(1)} %pick.1.pair_ref), branch_computations={%region_0.1_spmd, %region_1.2_spmd} | conditional | bytes 1048624 | solution.py:381
  12.5 0.7 %copy.9 = bf16[512,256]{1,0:T(8,128)(2,1)} copy(bf16[512,256]{1,0:T(8,128)(2,1)S(1)} %param) | data formatting | bytes 524288 | tf_op jit(solution)/shard_map/cond
  13.2 0.0 copy-start
  13.2 1.0 %copy-done = bf16[512,512]{1,0:T(8,128)(2,1)S(1)} copy-done((bf16[512,512]{1,0:T(8,128)(2,1)S(1)}, bf16[512,512]{1,0:T(8,128)(2,1)}, u32[]{:S(2)}) %copy-start) | copy-done | bytes 524312
  14.3 0.0 copy-start.1
  14.3 1.0 %copy-done.1 = bf16[512,512]{1,0:T(8,128)(2,1)S(1)} copy-done((bf16[512,512]{1,0:T(8,128)(2,1)S(1)}, bf16[512,512]{1,0:T(8,128)(2,1)}, u32[]{:S(2)}) %copy-start.1) | copy-done | bytes 524312
  15.3 0.0 copy-start.2
  15.3 0.7 %copy-done.2 = s32[1,512]{1,0:T(1,128)S(1)} copy-done((s32[1,512]{1,0:T(1,128)S(1)}, s32[1,512]{1,0:T(1,128)}, u32[]{:S(2)}) %copy-start.2) | copy-done | bytes 2072
  16.0 0.0 copy-start.3
  16.0 0.0 copy-start.4
  16.0 1.2 %prepare.1 = (f32[16,1024]{1,0:T(8,128)S(1)}, bf16[2048,128]{1,0:T(8,128)(2,1)S(1)}, bf16[2048,128]{1,0:T(8,128)(2,1)S(1)}, bf16[128,2048]{1,0:T(8,128)(2,1)S(1)...) custom-call(s32[1,512]{1,0:T(1,128)S(1)} %copy-done.2, ...), custom_call_target="tpu_custom_call" | custom-call | flops 2000000000 | bytes 1000000 | tf_op jit(solution)/shard_map/prepare/pallas_call | solution.py:297
  17.2 0.0 collective-permute-done.3.kv2_ref
  17.2 0.0 collective-permute-done.4
  17.2 0.1 broadcast_select_fusion.1
  17.3 1.3 %collective-permute-start.5 = (bf16[1024,256]{1,0:T(8,128)(2,1)S(1)}, bf16[1024,256]{1,0:T(8,128)(2,1)S(1)}, u32[]{:S(2)}, u32[]{:S(2)}) collective-permute-start(bf16[1024,256]{1,0:T(8,128)(2,1)S(1)} %pad_maximum_fusion.1), channel_id=1, source_target_pairs={{0,4},{4,0},{8,12},{12,8},{16,20},{20,16},{24,28},{28,24},{32,36},... | collective-permute-start | bytes 1572872 | tf_op jit(solution)/shard_map/ppermute | solution.py:344
  18.7 1.5 %collective-permute-done.5.kv13_ref = bf16[1024,256]{1,0:T(8,128)(2,1)S(1)} collective-permute-done((bf16[1024,256]{1,0:T(8,128)(2,1)S(1)}, bf16[1024,256]{1,0:T(8,128)(2,1)S(1)}, u32[]{:S(2)}, u32[]{:S(2)}) %collective-permute-start.5) | collective-permute-done | bytes 524320 | tf_op jit(solution)/shard_map/ppermute | solution.py:344
  20.2 0.0 copy-done.3
  20.2 0.0 copy-done.4
  20.2 7.4 %attention.1 = (bf16[512,512]{1,0:T(8,128)(2,1)}, bf16[512,512]{1,0:T(8,128)(2,1)}, f32[256,512]{1,0:T(8,128)S(1)}, bf16[256,512]{1,0:T(8,128)(2,1)S(1)}, bf16[2...) custom-call(s32[4]{0:T(128)S(1)} %copy-done.4, ...), custom_call_target="tpu_custom_call" | custom-call | flops 5000000000 | bytes 4000000 | tf_op jit(solution)/shard_map/attention/pallas_call | solution.py:321
  27.6 1.3 %collective-permute-start.6 = (bf16[256,512]{1,0:T(8,128)(2,1)S(1)}, bf16[256,512]{1,0:T(8,128)(2,1)S(1)}, u32[]{:S(2)}, u32[]{:S(2)}) collective-permute-start(bf16[256,512]{1,0:T(8,128)(2,1)S(1)} %get-tuple-element.68), channel_id=1, source_target_pairs={{12,0},{16,4},{13,1},{17,5},{14,2},{18,6},{15,3},{19,7}} | collective-permute-start | bytes 786440 | tf_op jit(solution)/shard_map/ppermute | solution.py:344
  28.9 0.7 %collective-permute-start.7 = (bf16[256,256]{1,0:T(8,128)(2,1)S(1)}, bf16[256,256]{1,0:T(8,128)(2,1)S(1)}, u32[]{:S(2)}, u32[]{:S(2)}) collective-permute-start(bf16[256,256]{1,0:T(8,128)(2,1)S(1)} %get-tuple-element.69), channel_id=1, source_target_pairs={{16,0},{17,1},{18,2},{19,3}} | collective-permute-start | bytes 393224 | tf_op jit(solution)/shard_map/ppermute | solution.py:344
  29.6 1.3 %collective-permute-start.8 = (bf16[256,512]{1,0:T(8,128)(2,1)S(1)}, bf16[256,512]{1,0:T(8,128)(2,1)S(1)}, u32[]{:S(2)}, u32[]{:S(2)}) collective-permute-start(bf16[256,512]{1,0:T(8,128)(2,1)S(1)} %get-tuple-element.70), channel_id=1, source_target_pairs={{8,0},{12,4},{16,8},{24,16},{28,20},{32,24},{36,28},{40,32},{44,36... | collective-permute-start | bytes 786440 | tf_op jit(solution)/shard_map/ppermute | solution.py:344
  30.9 1.9 %collective-permute-start.9 = (bf16[256,512]{1,0:T(8,128)(2,1)S(1)}, bf16[256,512]{1,0:T(8,128)(2,1)S(1)}, u32[]{:S(2)}, u32[]{:S(2)}) collective-permute-start(bf16[256,512]{1,0:T(8,128)(2,1)S(1)} %get-tuple-element.71), channel_id=1, source_target_pairs={{4,0},{8,4},{12,8},{16,12},{20,16},{24,20},{28,24},{32,28},{36,32}... | collective-permute-start | bytes 786440 | tf_op jit(solution)/shard_map/ppermute | solution.py:344
  32.8 0.0 collective-permute-done.7
  32.8 7.6 %collective-permute-done.6 = bf16[256,512]{1,0:T(8,128)(2,1)S(1)} collective-permute-done((bf16[256,512]{1,0:T(8,128)(2,1)S(1)}, bf16[256,512]{1,0:T(8,128)(2,1)S(1)}, u32[]{:S(2)}, u32[]{:S(2)}) %collective-permute-start.6) | collective-permute-done | bytes 262176 | tf_op jit(solution)/shard_map/ppermute | solution.py:344
  40.4 0.1 convert_add_fusion.2
  40.5 4.1 %collective-permute-done.8 = bf16[256,512]{1,0:T(8,128)(2,1)S(1)} collective-permute-done((bf16[256,512]{1,0:T(8,128)(2,1)S(1)}, bf16[256,512]{1,0:T(8,128)(2,1)S(1)}, u32[]{:S(2)}, u32[]{:S(2)}) %collective-permute-start.8) | collective-permute-done | bytes 262176 | tf_op jit(solution)/shard_map/ppermute | solution.py:344
  44.6 0.2 collective-permute-done.9
  44.8 0.2 convert_add_fusion.1
  45.1 1.4 %collective-permute-start.10 = (bf16[128,512]{1,0:T(8,128)(2,1)S(1)}, bf16[128,512]{1,0:T(8,128)(2,1)S(1)}, u32[]{:S(2)}, u32[]{:S(2)}) collective-permute-start(bf16[128,512]{1,0:T(8,128)(2,1)S(1)} %dynamic-slice_convert_fusion), channel_id=1, source_target_pairs={{0,1},{1,0},{2,3},{3,2},{4,5},{5,4},{6,7},{7,6},{8,9},{9,8},{10,11... | collective-permute-start | bytes 393224 | tf_op jit(solution)/shard_map/ppermute | solution.py:350
  46.5 2.5 %collective-permute-done.10 = bf16[128,512]{1,0:T(8,128)(2,1)S(1)} collective-permute-done((bf16[128,512]{1,0:T(8,128)(2,1)S(1)}, bf16[128,512]{1,0:T(8,128)(2,1)S(1)}, u32[]{:S(2)}, u32[]{:S(2)}) %collective-permute-start.10) | collective-permute-done | bytes 131104 | tf_op jit(solution)/shard_map/ppermute | solution.py:350
  49.0 0.7 %slice_bitcast_fusion = (bf16[512,64]{0,1:T(8,128)(2,1)}, bf16[512,64]{0,1:T(8,128)(2,1)}) fusion(bf16[128,512]{1,0:T(8,128)(2,1)S(1)} %add_convert_fusion), kind=kLoop, calls=%fused_computation.10 | loop fusion | bytes 262144 | tf_op jit(solution)/shard_map/transpose | solution.py:419
  (4 shorter events, 0.1 us)
Async XLA Ops:
  1.6 15.5 %collective-permute-start.3 = (bf16[512,256]{1,0:T(8,128)(2,1)S(1)}, bf16[512,256]{1,0:T(8,128)(2,1)S(1)}, u32[]{:S(2)}, u32[]{:S(2)}) collective-permute-start(bf16[512,256]{1,0:T(8,128)(2,1)S(1)} %pick.1.pair_ref), channel_id=1, source_target_pairs={{0,8},{4,12},{8,16},{12,20},{16,24},{20,28},{24,32},{28,36},{32,40... | collective-permute-start | bytes 786440 | tf_op jit(solution)/shard_map/ppermute | solution.py:344
  5.6 11.6 %collective-permute-start.4 = (bf16[512,256]{1,0:T(8,128)(2,1)S(1)}, bf16[512,256]{1,0:T(8,128)(2,1)S(1)}, u32[]{:S(2)}, u32[]{:S(2)}) collective-permute-start(bf16[512,256]{1,0:T(8,128)(2,1)S(1)} %pick.1.pair_ref), channel_id=1, source_target_pairs={{0,16},{4,20},{1,17},{5,21},{2,18},{6,22},{3,19},{7,23}} | collective-permute-start | bytes 786440 | tf_op jit(solution)/shard_map/ppermute | solution.py:344
  13.2 1.0 %copy-start = (bf16[512,512]{1,0:T(8,128)(2,1)S(1)}, bf16[512,512]{1,0:T(8,128)(2,1)}, u32[]{:S(2)}) copy-start(bf16[512,512]{1,0:T(8,128)(2,1)} %q_ref.1) | copy-start | bytes 1572868
  14.3 1.0 %copy-start.1 = (bf16[512,512]{1,0:T(8,128)(2,1)S(1)}, bf16[512,512]{1,0:T(8,128)(2,1)}, u32[]{:S(2)}) copy-start(bf16[512,512]{1,0:T(8,128)(2,1)} %grad_ref.1) | copy-start | bytes 1572868
  15.3 0.7 %copy-start.2 = (s32[1,512]{1,0:T(1,128)S(1)}, s32[1,512]{1,0:T(1,128)}, u32[]{:S(2)}) copy-start(s32[1,512]{1,0:T(1,128)} %get-tuple-element.50.start_ref) | copy-start | bytes 6148
  16.0 4.2 %copy-start.3 = (s32[1,512]{1,0:T(1,128)S(1)}, s32[1,512]{1,0:T(1,128)}, u32[]{:S(2)}) copy-start(s32[1,512]{1,0:T(1,128)} %get-tuple-element.50.start_ref) | copy-start | bytes 6148
  16.0 4.2 %copy-start.4 = (s32[4]{0:T(128)S(1)}, s32[4]{0:T(128)}, u32[]{:S(2)}) copy-start(s32[4]{0:T(128)} %get-tuple-element.49.bounds_ref) | copy-start | bytes 52
  17.3 2.9 %collective-permute-start.5 = (bf16[1024,256]{1,0:T(8,128)(2,1)S(1)}, bf16[1024,256]{1,0:T(8,128)(2,1)S(1)}, u32[]{:S(2)}, u32[]{:S(2)}) collective-permute-start(bf16[1024,256]{1,0:T(8,128)(2,1)S(1)} %pad_maximum_fusion.1), channel_id=1, source_target_pairs={{0,4},{4,0},{8,12},{12,8},{16,20},{20,16},{24,28},{28,24},{32,36},... | collective-permute-start | bytes 1572872 | tf_op jit(solution)/shard_map/ppermute | solution.py:344
  27.6 12.9 %collective-permute-start.6 = (bf16[256,512]{1,0:T(8,128)(2,1)S(1)}, bf16[256,512]{1,0:T(8,128)(2,1)S(1)}, u32[]{:S(2)}, u32[]{:S(2)}) collective-permute-start(bf16[256,512]{1,0:T(8,128)(2,1)S(1)} %get-tuple-element.68), channel_id=1, source_target_pairs={{12,0},{16,4},{13,1},{17,5},{14,2},{18,6},{15,3},{19,7}} | collective-permute-start | bytes 786440 | tf_op jit(solution)/shard_map/ppermute | solution.py:344
  28.9 3.9 %collective-permute-start.7 = (bf16[256,256]{1,0:T(8,128)(2,1)S(1)}, bf16[256,256]{1,0:T(8,128)(2,1)S(1)}, u32[]{:S(2)}, u32[]{:S(2)}) collective-permute-start(bf16[256,256]{1,0:T(8,128)(2,1)S(1)} %get-tuple-element.69), channel_id=1, source_target_pairs={{16,0},{17,1},{18,2},{19,3}} | collective-permute-start | bytes 393224 | tf_op jit(solution)/shard_map/ppermute | solution.py:344
  29.6 15.0 %collective-permute-start.8 = (bf16[256,512]{1,0:T(8,128)(2,1)S(1)}, bf16[256,512]{1,0:T(8,128)(2,1)S(1)}, u32[]{:S(2)}, u32[]{:S(2)}) collective-permute-start(bf16[256,512]{1,0:T(8,128)(2,1)S(1)} %get-tuple-element.70), channel_id=1, source_target_pairs={{8,0},{12,4},{16,8},{24,16},{28,20},{32,24},{36,28},{40,32},{44,36... | collective-permute-start | bytes 786440 | tf_op jit(solution)/shard_map/ppermute | solution.py:344
  30.9 13.9 %collective-permute-start.9 = (bf16[256,512]{1,0:T(8,128)(2,1)S(1)}, bf16[256,512]{1,0:T(8,128)(2,1)S(1)}, u32[]{:S(2)}, u32[]{:S(2)}) collective-permute-start(bf16[256,512]{1,0:T(8,128)(2,1)S(1)} %get-tuple-element.71), channel_id=1, source_target_pairs={{4,0},{8,4},{12,8},{16,12},{20,16},{24,20},{28,24},{32,28},{36,32}... | collective-permute-start | bytes 786440 | tf_op jit(solution)/shard_map/ppermute | solution.py:344
  45.1 3.9 %collective-permute-start.10 = (bf16[128,512]{1,0:T(8,128)(2,1)S(1)}, bf16[128,512]{1,0:T(8,128)(2,1)S(1)}, u32[]{:S(2)}, u32[]{:S(2)}) collective-permute-start(bf16[128,512]{1,0:T(8,128)(2,1)S(1)} %dynamic-slice_convert_fusion), channel_id=1, source_target_pairs={{0,1},{1,0},{2,3},{3,2},{4,5},{5,4},{6,7},{7,6},{8,9},{9,8},{10,11... | collective-permute-start | bytes 393224 | tf_op jit(solution)/shard_map/ppermute | solution.py:350

commit v7 on v6

--- a/solution.py
+++ b/solution.py
@@ -394,14 +394,14 @@
     attended, query_grad, t0, t1, t2, t3, t4a, t4b = attention_block(
         bounds, state, [own_pair, second, swapped, fourth]
     )
-    back4 = moved(t4b, reversed_pairs(near[4]))
-    back3 = moved(t3, reversed_pairs(near[3]))
     back2 = moved(t2, reversed_pairs(near[2]))
     back1 = moved(t1, reversed_pairs(near[1]))
-    gathered = t0 + back3.astype(jnp.float32)
+    back3 = moved(t3, reversed_pairs(near[3]))
+    back4 = moved(t4b, reversed_pairs(near[4]))
+    gathered = t0 + back2.astype(jnp.float32) + back1.astype(jnp.float32)
+    gathered = lax.optimization_barrier(gathered)
+    gathered = gathered + back3.astype(jnp.float32)
     gathered = gathered + jnp.pad(back4, ((0, 0), (TILE, 0))).astype(jnp.float32)
-    gathered = lax.optimization_barrier(gathered)
-    gathered = gathered + back2.astype(jnp.float32) + back1.astype(jnp.float32)
 
     def with_far(total, third_term, low_term, high_term):
         fourth_term = jnp.concatenate([low_term, high_term], axis=1)

time: 50 us -> 51.2 us (1.024)
  the two profiles are of different devices: /device:TPU:1 before, /device:TPU:8 now
where the time goes in v7:
time: 51.2 us; the launch traced here: 50.8 us
  waiting for transfers between devices  21.9 us (43%)
  starting transfers between devices  13.8 us (27%)
  Pallas kernels  8.94 us (17%)
  local copies, waits for them, and re-layouts  4.16 us (8%)
  between operations  1.47 us (3%)
    ppermute x7, waiting for transfers between devices, moved(): return lax.ppermute(value, 'ctx', pairs)  17.4 us
    ppermute x7, starting transfers between devices, moved(): return lax.ppermute(value, 'ctx', pairs)  13.3 us
    pallas_call x1, Pallas kernels, attention_block(): pl.pallas_call(attention_kernel, out_shape=[wide, wide, own, term, term,...  4.89 us
    ppermute x1, waiting for transfers between devices, from_partner(): return lax.ppermute(value, axis, pairs)  4.51 us
    unnamed x10, local copies, waits for them, and re-layouts  2.77 us
    pallas_call x1, Pallas kernels, scan_documents(): pl.pallas_call(scan_kernel, out_shape=[jax.ShapeDtypeStruct((1, TOK_DEV),...  1.87 us
    pallas_call x1, Pallas kernels, prepare(): pl.pallas_call(prepare_kernel, out_shape=[jax.ShapeDtypeStruct((8 * HALVE...  1.19 us
  transfers between devices with their start and end apart: 8, of which 4 were waited for; matrix products, arithmetic and copies ran while one was open for 2% of the time, Pallas kernels for 6%

profile of v7, /device:TPU:8, one launch (start us, length us, event | category | flops | bytes accessed | tf_op | source)
XLA Modules:
  0.0 50.8 jit_solution(3694214772618134241)
XLA Ops:
  0.6 1.0 %pick.1.pair_ref = bf16[512,256]{1,0:T(8,128)(2,1)S(1)} custom-call(s32[1]{0:T(128)} %bitcast.1.column_ref, bf16[512,256]{1,0:T(8,128)(2,1)} %keys_ref.1, bf16[512,256]{1,0:T(8,128)(2,1)} %values_ref.1), custom_call_target="tpu_custom_call" | custom-call | bytes 1000000 | tf_op jit(solution)/shard_map/pick/pallas_call | solution.py:233
  1.6 3.4 %collective-permute-start.3 = (bf16[512,256]{1,0:T(8,128)(2,1)S(1)}, bf16[512,256]{1,0:T(8,128)(2,1)S(1)}, u32[]{:S(2)}, u32[]{:S(2)}) collective-permute-start(bf16[512,256]{1,0:T(8,128)(2,1)S(1)} %pick.1.pair_ref), channel_id=1, source_target_pairs={{0,8},{4,12},{8,16},{12,20},{16,24},{20,28},{24,32},{28,36},{32,40... | collective-permute-start | bytes 786440 | tf_op jit(solution)/shard_map/ppermute | solution.py:344
  5.1 4.6 %collective-permute-start.4 = (bf16[512,256]{1,0:T(8,128)(2,1)S(1)}, bf16[512,256]{1,0:T(8,128)(2,1)S(1)}, u32[]{:S(2)}, u32[]{:S(2)}) collective-permute-start(bf16[512,256]{1,0:T(8,128)(2,1)S(1)} %pick.1.pair_ref), channel_id=1, source_target_pairs={{0,16},{4,20},{1,17},{5,21},{2,18},{6,22},{3,19},{7,23}} | collective-permute-start | bytes 786440 | tf_op jit(solution)/shard_map/ppermute | solution.py:344
  9.7 1.9 %scan.1 = (s32[1,512]{1,0:T(1,128)}, s32[4]{0:T(128)}, s32[1]{0:T(128)}) custom-call(s32[64]{0:T(128)} %lengths_ref.1, s32[1]{0:T(128)} %bitcast.block_ref), custom_call_target="tpu_custom_call" | custom-call | flops 1000000 | bytes 10000 | tf_op jit(solution)/shard_map/scan/pallas_call | solution.py:278
  12.2 0.7 %conditional.2 = (bf16[512,256]{1,0:T(8,128)(2,1)}) conditional(s32[]{:T(128)} %bitcast.2, bf16[512,256]{1,0:T(8,128)(2,1)S(1)} %pick.1.pair_ref, bf16[512,256]{1,0:T(8,128)(2,1)S(1)} %pick.1.pair_ref), branch_computations={%region_0.1_spmd, %region_1.2_spmd} | conditional | bytes 1048624 | solution.py:381
  12.3 0.7 %copy.9 = bf16[512,256]{1,0:T(8,128)(2,1)} copy(bf16[512,256]{1,0:T(8,128)(2,1)S(1)} %param) | data formatting | bytes 524288 | tf_op jit(solution)/shard_map/cond
  13.0 0.0 copy-start
  13.0 1.0 %copy-done = bf16[512,512]{1,0:T(8,128)(2,1)S(1)} copy-done((bf16[512,512]{1,0:T(8,128)(2,1)S(1)}, bf16[512,512]{1,0:T(8,128)(2,1)}, u32[]{:S(2)}) %copy-start) | copy-done | bytes 524312
  14.0 0.0 copy-start.1
  14.0 1.0 %copy-done.1 = bf16[512,512]{1,0:T(8,128)(2,1)S(1)} copy-done((bf16[512,512]{1,0:T(8,128)(2,1)S(1)}, bf16[512,512]{1,0:T(8,128)(2,1)}, u32[]{:S(2)}) %copy-start.1) | copy-done | bytes 524312
  15.0 0.0 copy-start.2
  15.0 0.7 %copy-done.2 = s32[1,512]{1,0:T(1,128)S(1)} copy-done((s32[1,512]{1,0:T(1,128)S(1)}, s32[1,512]{1,0:T(1,128)}, u32[]{:S(2)}) %copy-start.2) | copy-done | bytes 2072
  15.7 0.0 copy-start.3
  15.7 0.0 copy-start.4
  15.7 1.2 %prepare.1 = (f32[16,1024]{1,0:T(8,128)S(1)}, bf16[2048,128]{1,0:T(8,128)(2,1)S(1)}, bf16[2048,128]{1,0:T(8,128)(2,1)S(1)}, bf16[128,2048]{1,0:T(8,128)(2,1)S(1)...) custom-call(s32[1,512]{1,0:T(1,128)S(1)} %copy-done.2, ...), custom_call_target="tpu_custom_call" | custom-call | flops 2000000000 | bytes 1000000 | tf_op jit(solution)/shard_map/prepare/pallas_call | solution.py:297
  16.9 0.0 collective-permute-done.3.kv2_ref
  16.9 0.0 collective-permute-done.4
  16.9 0.1 broadcast_select_fusion.1
  17.1 0.1 collective-permute-start.5
  17.2 1.9 %collective-permute-done.5.kv13_ref = bf16[1024,256]{1,0:T(8,128)(2,1)S(1)} collective-permute-done((bf16[1024,256]{1,0:T(8,128)(2,1)S(1)}, bf16[1024,256]{1,0:T(8,128)(2,1)S(1)}, u32[]{:S(2)}, u32[]{:S(2)}) %collective-permute-start.5) | collective-permute-done | bytes 524320 | tf_op jit(solution)/shard_map/ppermute | solution.py:344
  19.1 0.0 copy-done.3
  19.1 0.0 copy-done.4
  19.1 4.9 %attention.1 = (bf16[512,512]{1,0:T(8,128)(2,1)}, bf16[512,512]{1,0:T(8,128)(2,1)}, f32[256,512]{1,0:T(8,128)S(1)}, bf16[256,512]{1,0:T(8,128)(2,1)S(1)}, bf16[2...) custom-call(s32[4]{0:T(128)S(1)} %copy-done.4, ...), custom_call_target="tpu_custom_call" | custom-call | flops 5000000000 | bytes 4000000 | tf_op jit(solution)/shard_map/attention/pallas_call | solution.py:321
  24.0 1.3 %collective-permute-start.6 = (bf16[256,512]{1,0:T(8,128)(2,1)S(1)}, bf16[256,512]{1,0:T(8,128)(2,1)S(1)}, u32[]{:S(2)}, u32[]{:S(2)}) collective-permute-start(bf16[256,512]{1,0:T(8,128)(2,1)S(1)} %get-tuple-element.68), channel_id=1, source_target_pairs={{8,0},{12,4},{16,8},{24,16},{28,20},{32,24},{36,28},{40,32},{44,36... | collective-permute-start | bytes 786440 | tf_op jit(solution)/shard_map/ppermute | solution.py:344
  25.2 1.3 %collective-permute-start.7 = (bf16[256,512]{1,0:T(8,128)(2,1)S(1)}, bf16[256,512]{1,0:T(8,128)(2,1)S(1)}, u32[]{:S(2)}, u32[]{:S(2)}) collective-permute-start(bf16[256,512]{1,0:T(8,128)(2,1)S(1)} %get-tuple-element.69), channel_id=1, source_target_pairs={{4,0},{8,4},{12,8},{16,12},{20,16},{24,20},{28,24},{32,28},{36,32}... | collective-permute-start | bytes 786440 | tf_op jit(solution)/shard_map/ppermute | solution.py:344
  26.6 1.3 %collective-permute-start.8 = (bf16[256,512]{1,0:T(8,128)(2,1)S(1)}, bf16[256,512]{1,0:T(8,128)(2,1)S(1)}, u32[]{:S(2)}, u32[]{:S(2)}) collective-permute-start(bf16[256,512]{1,0:T(8,128)(2,1)S(1)} %get-tuple-element.70), channel_id=1, source_target_pairs={{12,0},{16,4},{13,1},{17,5},{14,2},{18,6},{15,3},{19,7}} | collective-permute-start | bytes 786440 | tf_op jit(solution)/shard_map/ppermute | solution.py:344
  27.9 1.3 %collective-permute-start.9 = (bf16[256,256]{1,0:T(8,128)(2,1)S(1)}, bf16[256,256]{1,0:T(8,128)(2,1)S(1)}, u32[]{:S(2)}, u32[]{:S(2)}) collective-permute-start(bf16[256,256]{1,0:T(8,128)(2,1)S(1)} %get-tuple-element.71), channel_id=1, source_target_pairs={{16,0},{17,1},{18,2},{19,3}} | collective-permute-start | bytes 393224 | tf_op jit(solution)/shard_map/ppermute | solution.py:344
  29.2 6.7 %collective-permute-done.6 = bf16[256,512]{1,0:T(8,128)(2,1)S(1)} collective-permute-done((bf16[256,512]{1,0:T(8,128)(2,1)S(1)}, bf16[256,512]{1,0:T(8,128)(2,1)S(1)}, u32[]{:S(2)}, u32[]{:S(2)}) %collective-permute-start.6) | collective-permute-done | bytes 262176 | tf_op jit(solution)/shard_map/ppermute | solution.py:344
  35.9 0.0 collective-permute-done.7
  35.9 0.2 convert_add_fusion.2
  36.1 8.8 %collective-permute-done.9 = bf16[256,256]{1,0:T(8,128)(2,1)S(1)} collective-permute-done((bf16[256,256]{1,0:T(8,128)(2,1)S(1)}, bf16[256,256]{1,0:T(8,128)(2,1)S(1)}, u32[]{:S(2)}, u32[]{:S(2)}) %collective-permute-start.9) | collective-permute-done | bytes 131104 | tf_op jit(solution)/shard_map/ppermute | solution.py:344
  44.9 0.0 collective-permute-done.8
  44.9 0.1 convert_add_fusion.1
  45.0 0.5 %collective-permute-start.10 = (bf16[128,512]{1,0:T(8,128)(2,1)S(1)}, bf16[128,512]{1,0:T(8,128)(2,1)S(1)}, u32[]{:S(2)}, u32[]{:S(2)}) collective-permute-start(bf16[128,512]{1,0:T(8,128)(2,1)S(1)} %dynamic-slice_convert_fusion), channel_id=1, source_target_pairs={{0,1},{1,0},{2,3},{3,2},{4,5},{5,4},{6,7},{7,6},{8,9},{9,8},{10,11... | collective-permute-start | bytes 393224 | tf_op jit(solution)/shard_map/ppermute | solution.py:350
  45.6 4.5 %collective-permute-done.10 = bf16[128,512]{1,0:T(8,128)(2,1)S(1)} collective-permute-done((bf16[128,512]{1,0:T(8,128)(2,1)S(1)}, bf16[128,512]{1,0:T(8,128)(2,1)S(1)}, u32[]{:S(2)}, u32[]{:S(2)}) %collective-permute-start.10) | collective-permute-done | bytes 131104 | tf_op jit(solution)/shard_map/ppermute | solution.py:350
  50.1 0.7 %slice_bitcast_fusion = (bf16[512,64]{0,1:T(8,128)(2,1)}, bf16[512,64]{0,1:T(8,128)(2,1)}) fusion(bf16[128,512]{1,0:T(8,128)(2,1)S(1)} %add_convert_fusion), kind=kLoop, calls=%fused_computation.10 | loop fusion | bytes 262144 | tf_op jit(solution)/shard_map/transpose | solution.py:419
  (4 shorter events, 0.1 us)
Async XLA Ops:
  1.6 15.3 %collective-permute-start.3 = (bf16[512,256]{1,0:T(8,128)(2,1)S(1)}, bf16[512,256]{1,0:T(8,128)(2,1)S(1)}, u32[]{:S(2)}, u32[]{:S(2)}) collective-permute-start(bf16[512,256]{1,0:T(8,128)(2,1)S(1)} %pick.1.pair_ref), channel_id=1, source_target_pairs={{0,8},{4,12},{8,16},{12,20},{16,24},{20,28},{24,32},{28,36},{32,40... | collective-permute-start | bytes 786440 | tf_op jit(solution)/shard_map/ppermute | solution.py:344
  5.1 11.9 %collective-permute-start.4 = (bf16[512,256]{1,0:T(8,128)(2,1)S(1)}, bf16[512,256]{1,0:T(8,128)(2,1)S(1)}, u32[]{:S(2)}, u32[]{:S(2)}) collective-permute-start(bf16[512,256]{1,0:T(8,128)(2,1)S(1)} %pick.1.pair_ref), channel_id=1, source_target_pairs={{0,16},{4,20},{1,17},{5,21},{2,18},{6,22},{3,19},{7,23}} | collective-permute-start | bytes 786440 | tf_op jit(solution)/shard_map/ppermute | solution.py:344
  13.0 1.0 %copy-start = (bf16[512,512]{1,0:T(8,128)(2,1)S(1)}, bf16[512,512]{1,0:T(8,128)(2,1)}, u32[]{:S(2)}) copy-start(bf16[512,512]{1,0:T(8,128)(2,1)} %q_ref.1) | copy-start | bytes 1572868
  14.0 1.0 %copy-start.1 = (bf16[512,512]{1,0:T(8,128)(2,1)S(1)}, bf16[512,512]{1,0:T(8,128)(2,1)}, u32[]{:S(2)}) copy-start(bf16[512,512]{1,0:T(8,128)(2,1)} %grad_ref.1) | copy-start | bytes 1572868
  15.0 0.7 %copy-start.2 = (s32[1,512]{1,0:T(1,128)S(1)}, s32[1,512]{1,0:T(1,128)}, u32[]{:S(2)}) copy-start(s32[1,512]{1,0:T(1,128)} %get-tuple-element.50.start_ref) | copy-start | bytes 6148
  15.7 3.3 %copy-start.3 = (s32[1,512]{1,0:T(1,128)S(1)}, s32[1,512]{1,0:T(1,128)}, u32[]{:S(2)}) copy-start(s32[1,512]{1,0:T(1,128)} %get-tuple-element.50.start_ref) | copy-start | bytes 6148
  15.7 3.3 %copy-start.4 = (s32[4]{0:T(128)S(1)}, s32[4]{0:T(128)}, u32[]{:S(2)}) copy-start(s32[4]{0:T(128)} %get-tuple-element.49.bounds_ref) | copy-start | bytes 52
  17.1 2.0 %collective-permute-start.5 = (bf16[1024,256]{1,0:T(8,128)(2,1)S(1)}, bf16[1024,256]{1,0:T(8,128)(2,1)S(1)}, u32[]{:S(2)}, u32[]{:S(2)}) collective-permute-start(bf16[1024,256]{1,0:T(8,128)(2,1)S(1)} %pad_maximum_fusion.1), channel_id=1, source_target_pairs={{0,4},{4,0},{8,12},{12,8},{16,20},{20,16},{24,28},{28,24},{32,36},... | collective-permute-start | bytes 1572872 | tf_op jit(solution)/shard_map/ppermute | solution.py:344
  24.0 11.9 %collective-permute-start.6 = (bf16[256,512]{1,0:T(8,128)(2,1)S(1)}, bf16[256,512]{1,0:T(8,128)(2,1)S(1)}, u32[]{:S(2)}, u32[]{:S(2)}) collective-permute-start(bf16[256,512]{1,0:T(8,128)(2,1)S(1)} %get-tuple-element.68), channel_id=1, source_target_pairs={{8,0},{12,4},{16,8},{24,16},{28,20},{32,24},{36,28},{40,32},{44,36... | collective-permute-start | bytes 786440 | tf_op jit(solution)/shard_map/ppermute | solution.py:344
  25.2 10.7 %collective-permute-start.7 = (bf16[256,512]{1,0:T(8,128)(2,1)S(1)}, bf16[256,512]{1,0:T(8,128)(2,1)S(1)}, u32[]{:S(2)}, u32[]{:S(2)}) collective-permute-start(bf16[256,512]{1,0:T(8,128)(2,1)S(1)} %get-tuple-element.69), channel_id=1, source_target_pairs={{4,0},{8,4},{12,8},{16,12},{20,16},{24,20},{28,24},{32,28},{36,32}... | collective-permute-start | bytes 786440 | tf_op jit(solution)/shard_map/ppermute | solution.py:344
  26.6 18.3 %collective-permute-start.8 = (bf16[256,512]{1,0:T(8,128)(2,1)S(1)}, bf16[256,512]{1,0:T(8,128)(2,1)S(1)}, u32[]{:S(2)}, u32[]{:S(2)}) collective-permute-start(bf16[256,512]{1,0:T(8,128)(2,1)S(1)} %get-tuple-element.70), channel_id=1, source_target_pairs={{12,0},{16,4},{13,1},{17,5},{14,2},{18,6},{15,3},{19,7}} | collective-permute-start | bytes 786440 | tf_op jit(solution)/shard_map/ppermute | solution.py:344
  27.9 17.0 %collective-permute-start.9 = (bf16[256,256]{1,0:T(8,128)(2,1)S(1)}, bf16[256,256]{1,0:T(8,128)(2,1)S(1)}, u32[]{:S(2)}, u32[]{:S(2)}) collective-permute-start(bf16[256,256]{1,0:T(8,128)(2,1)S(1)} %get-tuple-element.71), channel_id=1, source_target_pairs={{16,0},{17,1},{18,2},{19,3}} | collective-permute-start | bytes 393224 | tf_op jit(solution)/shard_map/ppermute | solution.py:344
  45.0 5.1 %collective-permute-start.10 = (bf16[128,512]{1,0:T(8,128)(2,1)S(1)}, bf16[128,512]{1,0:T(8,128)(2,1)S(1)}, u32[]{:S(2)}, u32[]{:S(2)}) collective-permute-start(bf16[128,512]{1,0:T(8,128)(2,1)S(1)} %dynamic-slice_convert_fusion), channel_id=1, source_target_pairs={{0,1},{1,0},{2,3},{3,2},{4,5},{5,4},{6,7},{7,6},{8,9},{9,8},{10,11... | collective-permute-start | bytes 393224 | tf_op jit(solution)/shard_map/ppermute | solution.py:350

commit v8 on v7

--- a/solution.py
+++ b/solution.py
@@ -394,14 +394,15 @@
     attended, query_grad, t0, t1, t2, t3, t4a, t4b = attention_block(
         bounds, state, [own_pair, second, swapped, fourth]
     )
+    back4 = moved(t4b, reversed_pairs(near[4]))
     back2 = moved(t2, reversed_pairs(near[2]))
     back1 = moved(t1, reversed_pairs(near[1]))
     back3 = moved(t3, reversed_pairs(near[3]))
-    back4 = moved(t4b, reversed_pairs(near[4]))
-    gathered = t0 + back2.astype(jnp.float32) + back1.astype(jnp.float32)
+    gathered = t0 + jnp.pad(back4, ((0, 0), (TILE, 0))).astype(jnp.float32)
+    gathered = lax.optimization_barrier(gathered)
+    gathered = gathered + back2.astype(jnp.float32) + back1.astype(jnp.float32)
     gathered = lax.optimization_barrier(gathered)
     gathered = gathered + back3.astype(jnp.float32)
-    gathered = gathered + jnp.pad(back4, ((0, 0), (TILE, 0))).astype(jnp.float32)
 
     def with_far(total, third_term, low_term, high_term):
         fourth_term = jnp.concatenate([low_term, high_term], axis=1)

time: 51.2 us -> 52 us (1.016)
  the two profiles are of different devices: /device:TPU:8 before, /device:TPU:1 now
where the time goes in v8:
time: 52 us; the launch traced here: 51.6 us
  waiting for transfers between devices  17.9 us (34%)
  starting transfers between devices  16.2 us (31%)
  Pallas kernels  11.4 us (22%)
  local copies, waits for them, and re-layouts  4.16 us (8%)
  between operations  1.48 us (3%)
    ppermute x7, starting transfers between devices, moved(): return lax.ppermute(value, 'ctx', pairs)  14.8 us
    ppermute x7, waiting for transfers between devices, moved(): return lax.ppermute(value, 'ctx', pairs)  14.1 us
    pallas_call x1, Pallas kernels, attention_block(): pl.pallas_call(attention_kernel, out_shape=[wide, wide, own, term, term,...  7.4 us
    ppermute x1, waiting for transfers between devices, from_partner(): return lax.ppermute(value, axis, pairs)  3.79 us
    unnamed x10, local copies, waits for them, and re-layouts  2.77 us
    pallas_call x1, Pallas kernels, scan_documents(): pl.pallas_call(scan_kernel, out_shape=[jax.ShapeDtypeStruct((1, TOK_DEV),...  1.87 us
    ppermute x1, starting transfers between devices, from_partner(): return lax.ppermute(value, axis, pairs)  1.38 us
    pallas_call x1, Pallas kernels, prepare(): pl.pallas_call(prepare_kernel, out_shape=[jax.ShapeDtypeStruct((8 * HALVE...  1.19 us
  transfers between devices with their start and end apart: 8, of which 5 were waited for; matrix products, arithmetic and copies ran while one was open for 2% of the time, Pallas kernels for 6%

profile of v8, /device:TPU:1, one launch (start us, length us, event | category | flops | bytes accessed | tf_op | source)
XLA Modules:
  0.0 51.6 jit_solution(15694504246207916971)
XLA Ops:
  0.6 1.0 %pick.1.pair_ref = bf16[512,256]{1,0:T(8,128)(2,1)S(1)} custom-call(s32[1]{0:T(128)} %bitcast.1.column_ref, bf16[512,256]{1,0:T(8,128)(2,1)} %keys_ref.1, bf16[512,256]{1,0:T(8,128)(2,1)} %values_ref.1), custom_call_target="tpu_custom_call" | custom-call | bytes 1000000 | tf_op jit(solution)/shard_map/pick/pallas_call | solution.py:233
  1.6 4.0 %collective-permute-start.3 = (bf16[512,256]{1,0:T(8,128)(2,1)S(1)}, bf16[512,256]{1,0:T(8,128)(2,1)S(1)}, u32[]{:S(2)}, u32[]{:S(2)}) collective-permute-start(bf16[512,256]{1,0:T(8,128)(2,1)S(1)} %pick.1.pair_ref), channel_id=1, source_target_pairs={{0,8},{4,12},{8,16},{12,20},{16,24},{20,28},{24,32},{28,36},{32,40... | collective-permute-start | bytes 786440 | tf_op jit(solution)/shard_map/ppermute | solution.py:344
  5.6 4.4 %collective-permute-start.4 = (bf16[512,256]{1,0:T(8,128)(2,1)S(1)}, bf16[512,256]{1,0:T(8,128)(2,1)S(1)}, u32[]{:S(2)}, u32[]{:S(2)}) collective-permute-start(bf16[512,256]{1,0:T(8,128)(2,1)S(1)} %pick.1.pair_ref), channel_id=1, source_target_pairs={{0,16},{4,20},{1,17},{5,21},{2,18},{6,22},{3,19},{7,23}} | collective-permute-start | bytes 786440 | tf_op jit(solution)/shard_map/ppermute | solution.py:344
  10.0 1.9 %scan.1 = (s32[1,512]{1,0:T(1,128)}, s32[4]{0:T(128)}, s32[1]{0:T(128)}) custom-call(s32[64]{0:T(128)} %lengths_ref.1, s32[1]{0:T(128)} %bitcast.block_ref), custom_call_target="tpu_custom_call" | custom-call | flops 1000000 | bytes 10000 | tf_op jit(solution)/shard_map/scan/pallas_call | solution.py:278
  12.5 0.7 %conditional.2 = (bf16[512,256]{1,0:T(8,128)(2,1)}) conditional(s32[]{:T(128)} %bitcast.2, bf16[512,256]{1,0:T(8,128)(2,1)S(1)} %pick.1.pair_ref, bf16[512,256]{1,0:T(8,128)(2,1)S(1)} %pick.1.pair_ref), branch_computations={%region_0.1_spmd, %region_1.2_spmd} | conditional | bytes 1048624 | solution.py:381
  12.5 0.7 %copy.9 = bf16[512,256]{1,0:T(8,128)(2,1)} copy(bf16[512,256]{1,0:T(8,128)(2,1)S(1)} %param) | data formatting | bytes 524288 | tf_op jit(solution)/shard_map/cond
  13.2 0.0 copy-start
  13.2 1.0 %copy-done = bf16[512,512]{1,0:T(8,128)(2,1)S(1)} copy-done((bf16[512,512]{1,0:T(8,128)(2,1)S(1)}, bf16[512,512]{1,0:T(8,128)(2,1)}, u32[]{:S(2)}) %copy-start) | copy-done | bytes 524312
  14.3 0.0 copy-start.1
  14.3 1.0 %copy-done.1 = bf16[512,512]{1,0:T(8,128)(2,1)S(1)} copy-done((bf16[512,512]{1,0:T(8,128)(2,1)S(1)}, bf16[512,512]{1,0:T(8,128)(2,1)}, u32[]{:S(2)}) %copy-start.1) | copy-done | bytes 524312
  15.3 0.0 copy-start.2
  15.3 0.7 %copy-done.2 = s32[1,512]{1,0:T(1,128)S(1)} copy-done((s32[1,512]{1,0:T(1,128)S(1)}, s32[1,512]{1,0:T(1,128)}, u32[]{:S(2)}) %copy-start.2) | copy-done | bytes 2072
  16.0 0.0 copy-start.3
  16.0 0.0 copy-start.4
  16.0 1.2 %prepare.1 = (f32[16,1024]{1,0:T(8,128)S(1)}, bf16[2048,128]{1,0:T(8,128)(2,1)S(1)}, bf16[2048,128]{1,0:T(8,128)(2,1)S(1)}, bf16[128,2048]{1,0:T(8,128)(2,1)S(1)...) custom-call(s32[1,512]{1,0:T(1,128)S(1)} %copy-done.2, ...), custom_call_target="tpu_custom_call" | custom-call | flops 2000000000 | bytes 1000000 | tf_op jit(solution)/shard_map/prepare/pallas_call | solution.py:297
  17.2 0.0 collective-permute-done.3.kv2_ref
  17.2 0.0 collective-permute-done.4
  17.2 0.1 broadcast_select_fusion.1
  17.3 1.3 %collective-permute-start.5 = (bf16[1024,256]{1,0:T(8,128)(2,1)S(1)}, bf16[1024,256]{1,0:T(8,128)(2,1)S(1)}, u32[]{:S(2)}, u32[]{:S(2)}) collective-permute-start(bf16[1024,256]{1,0:T(8,128)(2,1)S(1)} %pad_maximum_fusion.1), channel_id=1, source_target_pairs={{0,4},{4,0},{8,12},{12,8},{16,20},{20,16},{24,28},{28,24},{32,36},... | collective-permute-start | bytes 1572872 | tf_op jit(solution)/shard_map/ppermute | solution.py:344
  18.7 1.5 %collective-permute-done.5.kv13_ref = bf16[1024,256]{1,0:T(8,128)(2,1)S(1)} collective-permute-done((bf16[1024,256]{1,0:T(8,128)(2,1)S(1)}, bf16[1024,256]{1,0:T(8,128)(2,1)S(1)}, u32[]{:S(2)}, u32[]{:S(2)}) %collective-permute-start.5) | collective-permute-done | bytes 524320 | tf_op jit(solution)/shard_map/ppermute | solution.py:344
  20.2 0.0 copy-done.3
  20.2 0.0 copy-done.4
  20.2 7.4 %attention.1 = (bf16[512,512]{1,0:T(8,128)(2,1)}, bf16[512,512]{1,0:T(8,128)(2,1)}, f32[256,512]{1,0:T(8,128)S(1)}, bf16[256,512]{1,0:T(8,128)(2,1)S(1)}, bf16[2...) custom-call(s32[4]{0:T(128)S(1)} %copy-done.4, ...), custom_call_target="tpu_custom_call" | custom-call | flops 5000000000 | bytes 4000000 | tf_op jit(solution)/shard_map/attention/pallas_call | solution.py:321
  27.6 0.7 %collective-permute-start.6 = (bf16[256,256]{1,0:T(8,128)(2,1)S(1)}, bf16[256,256]{1,0:T(8,128)(2,1)S(1)}, u32[]{:S(2)}, u32[]{:S(2)}) collective-permute-start(bf16[256,256]{1,0:T(8,128)(2,1)S(1)} %get-tuple-element.68), channel_id=1, source_target_pairs={{16,0},{17,1},{18,2},{19,3}} | collective-permute-start | bytes 393224 | tf_op jit(solution)/shard_map/ppermute | solution.py:344
  28.3 1.3 %collective-permute-start.7 = (bf16[256,512]{1,0:T(8,128)(2,1)S(1)}, bf16[256,512]{1,0:T(8,128)(2,1)S(1)}, u32[]{:S(2)}, u32[]{:S(2)}) collective-permute-start(bf16[256,512]{1,0:T(8,128)(2,1)S(1)} %get-tuple-element.69), channel_id=1, source_target_pairs={{8,0},{12,4},{16,8},{24,16},{28,20},{32,24},{36,28},{40,32},{44,36... | collective-permute-start | bytes 786440 | tf_op jit(solution)/shard_map/ppermute | solution.py:344
  29.6 1.9 %collective-permute-start.8 = (bf16[256,512]{1,0:T(8,128)(2,1)S(1)}, bf16[256,512]{1,0:T(8,128)(2,1)S(1)}, u32[]{:S(2)}, u32[]{:S(2)}) collective-permute-start(bf16[256,512]{1,0:T(8,128)(2,1)S(1)} %get-tuple-element.70), channel_id=1, source_target_pairs={{4,0},{8,4},{12,8},{16,12},{20,16},{24,20},{28,24},{32,28},{36,32}... | collective-permute-start | bytes 786440 | tf_op jit(solution)/shard_map/ppermute | solution.py:344
  31.5 1.3 %collective-permute-start.9 = (bf16[256,512]{1,0:T(8,128)(2,1)S(1)}, bf16[256,512]{1,0:T(8,128)(2,1)S(1)}, u32[]{:S(2)}, u32[]{:S(2)}) collective-permute-start(bf16[256,512]{1,0:T(8,128)(2,1)S(1)} %get-tuple-element.71), channel_id=1, source_target_pairs={{12,0},{16,4},{13,1},{17,5},{14,2},{18,6},{15,3},{19,7}} | collective-permute-start | bytes 786440 | tf_op jit(solution)/shard_map/ppermute | solution.py:344
  32.8 0.0 collective-permute-done.6
  32.8 0.1 convert_add_fusion.3
  32.9 7.0 %collective-permute-done.7 = bf16[256,512]{1,0:T(8,128)(2,1)S(1)} collective-permute-done((bf16[256,512]{1,0:T(8,128)(2,1)S(1)}, bf16[256,512]{1,0:T(8,128)(2,1)S(1)}, u32[]{:S(2)}, u32[]{:S(2)}) %collective-permute-start.7) | collective-permute-done | bytes 262176 | tf_op jit(solution)/shard_map/ppermute | solution.py:344
  39.9 3.5 %collective-permute-done.8 = bf16[256,512]{1,0:T(8,128)(2,1)S(1)} collective-permute-done((bf16[256,512]{1,0:T(8,128)(2,1)S(1)}, bf16[256,512]{1,0:T(8,128)(2,1)S(1)}, u32[]{:S(2)}, u32[]{:S(2)}) %collective-permute-start.8) | collective-permute-done | bytes 262176 | tf_op jit(solution)/shard_map/ppermute | solution.py:344
  43.3 0.2 convert_add_fusion.2
  43.6 2.1 %collective-permute-done.9 = bf16[256,512]{1,0:T(8,128)(2,1)S(1)} collective-permute-done((bf16[256,512]{1,0:T(8,128)(2,1)S(1)}, bf16[256,512]{1,0:T(8,128)(2,1)S(1)}, u32[]{:S(2)}, u32[]{:S(2)}) %collective-permute-start.9) | collective-permute-done | bytes 262176 | tf_op jit(solution)/shard_map/ppermute | solution.py:344
  45.6 0.1 convert_add_fusion.1
  45.8 1.4 %collective-permute-start.10 = (bf16[128,512]{1,0:T(8,128)(2,1)S(1)}, bf16[128,512]{1,0:T(8,128)(2,1)S(1)}, u32[]{:S(2)}, u32[]{:S(2)}) collective-permute-start(bf16[128,512]{1,0:T(8,128)(2,1)S(1)} %dynamic-slice_convert_fusion), channel_id=1, source_target_pairs={{0,1},{1,0},{2,3},{3,2},{4,5},{5,4},{6,7},{7,6},{8,9},{9,8},{10,11... | collective-permute-start | bytes 393224 | tf_op jit(solution)/shard_map/ppermute | solution.py:350
  47.1 3.8 %collective-permute-done.10 = bf16[128,512]{1,0:T(8,128)(2,1)S(1)} collective-permute-done((bf16[128,512]{1,0:T(8,128)(2,1)S(1)}, bf16[128,512]{1,0:T(8,128)(2,1)S(1)}, u32[]{:S(2)}, u32[]{:S(2)}) %collective-permute-start.10) | collective-permute-done | bytes 131104 | tf_op jit(solution)/shard_map/ppermute | solution.py:350
  51.0 0.7 %slice_bitcast_fusion = (bf16[512,64]{0,1:T(8,128)(2,1)}, bf16[512,64]{0,1:T(8,128)(2,1)}) fusion(bf16[128,512]{1,0:T(8,128)(2,1)S(1)} %add_convert_fusion), kind=kLoop, calls=%fused_computation.11 | loop fusion | bytes 262144 | tf_op jit(solution)/shard_map/transpose | solution.py:420
  (4 shorter events, 0.1 us)
Async XLA Ops:
  1.6 15.5 %collective-permute-start.3 = (bf16[512,256]{1,0:T(8,128)(2,1)S(1)}, bf16[512,256]{1,0:T(8,128)(2,1)S(1)}, u32[]{:S(2)}, u32[]{:S(2)}) collective-permute-start(bf16[512,256]{1,0:T(8,128)(2,1)S(1)} %pick.1.pair_ref), channel_id=1, source_target_pairs={{0,8},{4,12},{8,16},{12,20},{16,24},{20,28},{24,32},{28,36},{32,40... | collective-permute-start | bytes 786440 | tf_op jit(solution)/shard_map/ppermute | solution.py:344
  5.6 11.6 %collective-permute-start.4 = (bf16[512,256]{1,0:T(8,128)(2,1)S(1)}, bf16[512,256]{1,0:T(8,128)(2,1)S(1)}, u32[]{:S(2)}, u32[]{:S(2)}) collective-permute-start(bf16[512,256]{1,0:T(8,128)(2,1)S(1)} %pick.1.pair_ref), channel_id=1, source_target_pairs={{0,16},{4,20},{1,17},{5,21},{2,18},{6,22},{3,19},{7,23}} | collective-permute-start | bytes 786440 | tf_op jit(solution)/shard_map/ppermute | solution.py:344
  13.2 1.0 %copy-start = (bf16[512,512]{1,0:T(8,128)(2,1)S(1)}, bf16[512,512]{1,0:T(8,128)(2,1)}, u32[]{:S(2)}) copy-start(bf16[512,512]{1,0:T(8,128)(2,1)} %q_ref.1) | copy-start | bytes 1572868
  14.3 1.0 %copy-start.1 = (bf16[512,512]{1,0:T(8,128)(2,1)S(1)}, bf16[512,512]{1,0:T(8,128)(2,1)}, u32[]{:S(2)}) copy-start(bf16[512,512]{1,0:T(8,128)(2,1)} %grad_ref.1) | copy-start | bytes 1572868
  15.3 0.7 %copy-start.2 = (s32[1,512]{1,0:T(1,128)S(1)}, s32[1,512]{1,0:T(1,128)}, u32[]{:S(2)}) copy-start(s32[1,512]{1,0:T(1,128)} %get-tuple-element.50.start_ref) | copy-start | bytes 6148
  16.0 4.2 %copy-start.3 = (s32[1,512]{1,0:T(1,128)S(1)}, s32[1,512]{1,0:T(1,128)}, u32[]{:S(2)}) copy-start(s32[1,512]{1,0:T(1,128)} %get-tuple-element.50.start_ref) | copy-start | bytes 6148
  16.0 4.2 %copy-start.4 = (s32[4]{0:T(128)S(1)}, s32[4]{0:T(128)}, u32[]{:S(2)}) copy-start(s32[4]{0:T(128)} %get-tuple-element.49.bounds_ref) | copy-start | bytes 52
  17.3 2.9 %collective-permute-start.5 = (bf16[1024,256]{1,0:T(8,128)(2,1)S(1)}, bf16[1024,256]{1,0:T(8,128)(2,1)S(1)}, u32[]{:S(2)}, u32[]{:S(2)}) collective-permute-start(bf16[1024,256]{1,0:T(8,128)(2,1)S(1)} %pad_maximum_fusion.1), channel_id=1, source_target_pairs={{0,4},{4,0},{8,12},{12,8},{16,20},{20,16},{24,28},{28,24},{32,36},... | collective-permute-start | bytes 1572872 | tf_op jit(solution)/shard_map/ppermute | solution.py:344
  27.6 5.2 %collective-permute-start.6 = (bf16[256,256]{1,0:T(8,128)(2,1)S(1)}, bf16[256,256]{1,0:T(8,128)(2,1)S(1)}, u32[]{:S(2)}, u32[]{:S(2)}) collective-permute-start(bf16[256,256]{1,0:T(8,128)(2,1)S(1)} %get-tuple-element.68), channel_id=1, source_target_pairs={{16,0},{17,1},{18,2},{19,3}} | collective-permute-start | bytes 393224 | tf_op jit(solution)/shard_map/ppermute | solution.py:344
  28.3 11.6 %collective-permute-start.7 = (bf16[256,512]{1,0:T(8,128)(2,1)S(1)}, bf16[256,512]{1,0:T(8,128)(2,1)S(1)}, u32[]{:S(2)}, u32[]{:S(2)}) collective-permute-start(bf16[256,512]{1,0:T(8,128)(2,1)S(1)} %get-tuple-element.69), channel_id=1, source_target_pairs={{8,0},{12,4},{16,8},{24,16},{28,20},{32,24},{36,28},{40,32},{44,36... | collective-permute-start | bytes 786440 | tf_op jit(solution)/shard_map/ppermute | solution.py:344
  29.6 13.8 %collective-permute-start.8 = (bf16[256,512]{1,0:T(8,128)(2,1)S(1)}, bf16[256,512]{1,0:T(8,128)(2,1)S(1)}, u32[]{:S(2)}, u32[]{:S(2)}) collective-permute-start(bf16[256,512]{1,0:T(8,128)(2,1)S(1)} %get-tuple-element.70), channel_id=1, source_target_pairs={{4,0},{8,4},{12,8},{16,12},{20,16},{24,20},{28,24},{32,28},{36,32}... | collective-permute-start | bytes 786440 | tf_op jit(solution)/shard_map/ppermute | solution.py:344
  31.5 14.1 %collective-permute-start.9 = (bf16[256,512]{1,0:T(8,128)(2,1)S(1)}, bf16[256,512]{1,0:T(8,128)(2,1)S(1)}, u32[]{:S(2)}, u32[]{:S(2)}) collective-permute-start(bf16[256,512]{1,0:T(8,128)(2,1)S(1)} %get-tuple-element.71), channel_id=1, source_target_pairs={{12,0},{16,4},{13,1},{17,5},{14,2},{18,6},{15,3},{19,7}} | collective-permute-start | bytes 786440 | tf_op jit(solution)/shard_map/ppermute | solution.py:344
  45.8 5.2 %collective-permute-start.10 = (bf16[128,512]{1,0:T(8,128)(2,1)S(1)}, bf16[128,512]{1,0:T(8,128)(2,1)S(1)}, u32[]{:S(2)}, u32[]{:S(2)}) collective-permute-start(bf16[128,512]{1,0:T(8,128)(2,1)S(1)} %dynamic-slice_convert_fusion), channel_id=1, source_target_pairs={{0,1},{1,0},{2,3},{3,2},{4,5},{5,4},{6,7},{7,6},{8,9},{9,8},{10,11... | collective-permute-start | bytes 393224 | tf_op jit(solution)/shard_map/ppermute | solution.py:350
